TPU v7x, 512 devices: a whole 4x4x16 slice. The times are simulated.
512 devices in a mesh: expert: 8 (over z_hi, core), tensor: 64 (over y, z_lo, x).
Axes of the slice: x: 4, y: 4, z: 16 (z_hi: 4, z_lo: 4; z = z_hi * 4 + z_lo), core: 2. Of those that a mesh axis runs over, the one named last changes fastest.
Arguments:
- tokens: bfloat16 [1024, 4096], P('tensor'), may hold values from -6 to 6
- cotangent: bfloat16 [1024, 4096], P('tensor'), may hold values from -6 to 6
- expert_id: int32 [1024], P('tensor'), may hold values from 0 to 7, as said below
- gate_weight: bfloat16 [8, 4096, 8192], P('expert', None, 'tensor'), may hold values from -0.09375 to 0.09375
- up_weight: bfloat16 [8, 4096, 8192], P('expert', None, 'tensor'), may hold values from -0.09375 to 0.09375
- down_weight: bfloat16 [8, 8192, 4096], P('expert', 'tensor'), may hold values from -0.0625 to 0.0625
Outputs:
- layer_out: bfloat16 [1024, 4096], P('tensor')
- grad_in: bfloat16 [1024, 4096], P('tensor')
Inputs may be any that keep to these rules, and one draw needn't show every extreme that they name: `expert_id`: the 16 rows of each owner name every expert at most 4 times; every expert is named 4 times by some owner.
All inputs are finite; a program needn't handle non-finite values.
Results may differ from a plain program's by a relative error of at most 0.005.
Values may be sent and summed in bfloat16 or wider, within the bound.
No kernel may reach another device: no remote copies, remote signals or barrier semaphores. Data moves between devices by JAX's collectives and lax.ppermute only.
A program may use at most 64 MiB of HBM per device.

v0:
```python
import jax
import jax.numpy as jnp
from jax import lax
from jax.sharding import PartitionSpec as P

SEND = 4


def contract_last(left, right):
    return lax.dot_general(
        left, right, (((1,), (1,)), ((), ())), preferred_element_type=jnp.float32
    )


def contract_first(left, right):
    return lax.dot_general(
        left, right, (((0,), (0,)), ((), ())), preferred_element_type=jnp.float32
    )


def shards(tokens, cotangent, expert_id, gate_weight, up_weight, down_weight):
    my_expert = lax.axis_index("expert")
    group_size = lax.axis_size("tensor")
    count = expert_id.shape[0]
    earlier = (
        jnp.arange(count, dtype=jnp.int32)[:, None] > jnp.arange(count, dtype=jnp.int32)[None, :]
    )
    slot = jnp.sum(((expert_id[:, None] == expert_id[None, :]) & earlier).astype(jnp.int32), axis=1)
    positions = jnp.arange(SEND, dtype=jnp.int32)
    selector = ((expert_id[None, :] == my_expert) & (slot[None, :] == positions[:, None])).astype(
        jnp.bfloat16
    )
    own_rows = jnp.dot(selector, tokens, preferred_element_type=jnp.float32).astype(jnp.bfloat16)
    own_grads = jnp.dot(selector, cotangent, preferred_element_type=jnp.float32).astype(
        jnp.bfloat16
    )
    w_gate = gate_weight[0]
    w_up = up_weight[0]
    w_down = down_weight[0]
    expert_rows = lax.all_gather(own_rows, "tensor", axis=0, tiled=True)
    gate_pre = jnp.dot(expert_rows, w_gate, preferred_element_type=jnp.float32)
    upper = jnp.dot(expert_rows, w_up, preferred_element_type=jnp.float32)
    sigmoid_gate = jax.nn.sigmoid(gate_pre)
    hidden = (gate_pre * sigmoid_gate * upper).astype(jnp.bfloat16)
    partial_value = jnp.dot(hidden, w_down, preferred_element_type=jnp.float32).reshape(
        group_size, SEND, -1
    )
    summed = jnp.sum(
        lax.all_to_all(partial_value, "tensor", split_axis=0, concat_axis=0, tiled=True), axis=0
    )
    out_rows = summed.astype(jnp.bfloat16)
    spread = contract_first(selector, out_rows)
    layer_out = lax.psum(spread.astype(jnp.bfloat16), "expert")
    d_hidden = contract_last(lax.all_gather(own_grads, "tensor", axis=0, tiled=True), w_down)
    d_gate = (d_hidden * upper * sigmoid_gate * (1.0 + gate_pre * (1.0 - sigmoid_gate))).astype(
        jnp.bfloat16
    )
    d_up = (d_hidden * gate_pre * sigmoid_gate).astype(jnp.bfloat16)
    grad_partial = contract_last(d_gate, w_gate) + contract_last(d_up, w_up)
    grad_sum = jnp.sum(
        lax.all_to_all(
            grad_partial.reshape(group_size, SEND, -1),
            "tensor",
            split_axis=0,
            concat_axis=0,
            tiled=True,
        ),
        axis=0,
    )
    din_rows = grad_sum.astype(jnp.bfloat16)
    grad_spread = contract_first(selector, din_rows)
    grad_in = lax.psum(grad_spread.astype(jnp.bfloat16), "expert")
    return (layer_out, grad_in)


def solution(mesh):
    placed = (
        P("tensor", None),
        P("tensor", None),
        P("tensor"),
        P("expert", None, "tensor"),
        P("expert", None, "tensor"),
        P("expert", "tensor", None),
    )
    return jax.shard_map(
        shards,
        mesh=mesh,
        in_specs=placed,
        out_specs=(P("tensor", None), P("tensor", None)),
        check_vma=False,
    )
```

profile of v0, /device:TPU:1, one launch (start us, length us, event | category | flops | bytes accessed | tf_op | source)
XLA Modules:
  0.0 1013.6 jit_solution(14283385552122773989)
XLA Ops:
  7.2 0.0 copy-start
  7.2 0.0 all-gather.5.cloned.1.call-start
  7.2 0.9 convert_reduce_fusion
  8.2 0.7 broadcast_compare_fusion
  8.8 1.7 fusion
  10.5 0.0 all-gather.5.cloned.1.call-update
  10.5 0.0 all-gather.7.cloned.1.call-start
  10.6 1.7 fusion.1
  12.2 0.0 all-gather.7.cloned.1.call-update
  12.3 314.1 %all-gather.5.cloned.1.call-done = bf16[64,4,4096]{2,1,0:T(4,128)(2,1)} async-done(((bf16[1,4,4096]{2,1,0:T(4,128)(2,1)}), bf16[64,4,4096]{2,1,0:T(4,128)(2,1)}) %all-gather.5.cloned.1.call-update) | async-done | bytes 2097168 | tf_op jit(solution)/shard_map/all_gather | solution.py:40
  326.4 2.5 reshape.16
  328.9 1.9 fusion.11
  330.9 0.0 copy-done
  330.9 0.7 multiply_convert_fusion.2
  331.6 350.2 %all-gather.7.cloned.1.call-done = bf16[64,4,4096]{2,1,0:T(4,128)(2,1)} async-done(((bf16[1,4,4096]{2,1,0:T(4,128)(2,1)}), bf16[64,4,4096]{2,1,0:T(4,128)(2,1)}) %all-gather.7.cloned.1.call-update) | async-done | bytes 2097168 | tf_op jit(solution)/shard_map/all_gather | solution.py:54
  681.8 2.5 reshape.18
  684.3 0.0 copy-start.1
  684.3 2.0 fusion.4
  686.3 0.0 copy-done.1
  686.3 0.7 fusion.9
  687.1 2.7 convolution_add_fusion
  689.8 5.2 reshape.14
  695.0 0.0 copy-start.2
  695.0 9.3 all-to-all-start.1
  704.3 0.0 copy-done.2
  704.3 0.7 fusion.2
  705.0 4.7 copy.10
  709.7 45.6 %all-to-all-done.1 = f32[64,4,4096]{2,1,0:T(4,128)} async-done(((f32[64,4,4096]{2,1,0:T(4,128)}), f32[64,4,4096]{2,1,0:T(4,128)}, u32[]{:S(2)}, u32[]{:S(2)}) %all-to-all-start.1) | async-done | bytes 4194336 | tf_op jit(solution)/shard_map/all_to_all | solution.py:61
  755.3 6.1 all-to-all-start
  761.3 0.0 all-reduce.3.cloned.1.call-start
  761.4 2.8 reduce_sum.29
  764.2 0.9 convolution_convert_fusion
  765.1 84.0 %all-to-all-done = f32[64,4,4096]{2,1,0:T(4,128)} async-done(((f32[64,4,4096]{2,1,0:T(4,128)}), f32[64,4,4096]{2,1,0:T(4,128)}, u32[]{:S(2)}, u32[]{:S(2)}) %all-to-all-start) | async-done | bytes 4194336 | tf_op jit(solution)/shard_map/all_to_all | solution.py:49
  849.1 2.8 reduce_sum.28
  851.9 0.9 convolution_convert_fusion.1
  852.8 0.0 all-reduce.3.cloned.1.call-update
  852.8 151.1 %all-reduce.3.cloned.1.call-done = (bf16[16,4096]{1,0:T(8,128)(2,1)}, bf16[16,4096]{1,0:T(8,128)(2,1)}) async-done(((bf16[16,4096]{1,0:T(8,128)(2,1)}, bf16[16,4096]{1,0:T(8,128)(2,1)}), (bf16[16,4096]{1,0:T(8,128)(2,1)}, bf16[16,4096]{1,0:T(8,128)(2,1)})) %all-reduce.3.cloned.1.call-update) | async-done | bytes 262160 | tf_op jit(solution)/shard_map/psum | solution.py:53
  1003.9 1.6 copy.17
  1005.5 1.6 copy.18
  (1 shorter events, 0.0 us)
Async XLA Ops:
  7.2 323.7 %copy-start = (bf16[1,4096,128]{2,1,0:T(8,128)(2,1)S(1)}, bf16[1,4096,128]{2,1,0:T(8,128)(2,1)}, u32[]{:S(2)}) copy-start(bf16[1,4096,128]{2,1,0:T(8,128)(2,1)} %param.10) | copy-start | bytes 3145732
  7.2 319.2 %all-gather.5.cloned.1.call-start = ((), (), s32[]{:S(2)}) async-start(), calls=%async_computation.2 | async-start | bytes 2129920 | tf_op jit(solution)/shard_map/all_gather | solution.py:40
  10.5 671.2 %all-gather.7.cloned.1.call-start = ((), (), s32[]{:S(2)}) async-start(), calls=%async_computation.3 | async-start | bytes 2129920 | tf_op jit(solution)/shard_map/all_gather | solution.py:54
  684.3 2.0 copy-start.1
  695.0 9.3 copy-start.2
  695.0 60.3 %all-to-all-start.1 = ((f32[64,4,4096]{2,1,0:T(4,128)}), f32[64,4,4096]{2,1,0:T(4,128)}, u32[]{:S(2)}, u32[]{:S(2)}) async-start(f32[64,4,4096]{2,1,0:T(4,128)} %reshape.14), calls=%async_computation.1 | async-start | bytes 8388608 | tf_op jit(solution)/shard_map/all_to_all | solution.py:61
  755.3 93.8 %all-to-all-start = ((f32[64,4,4096]{2,1,0:T(4,128)}), f32[64,4,4096]{2,1,0:T(4,128)}, u32[]{:S(2)}, u32[]{:S(2)}) async-start(f32[64,4,4096]{2,1,0:T(4,128)} %copy.10), calls=%async_computation | async-start | bytes 8388608 | tf_op jit(solution)/shard_map/all_to_all | solution.py:49
  761.3 242.6 %all-reduce.3.cloned.1.call-start = ((), (), s32[]{:S(2)}) async-start(), calls=%async_computation.4 | async-start | bytes 524288 | tf_op jit(solution)/shard_map/psum | solution.py:53
Sparse Core Ops, SparseCore 0:
  10.7 315.6 all-gather.4
  329.0 352.6 all-gather.6
  852.9 150.9 all-reduce.2
where the time goes:
time: 1010 us
  waiting for transfers between devices  945 us (94%)
  local copies, waits for them, and re-layouts  18.1 us (2%)
  starting transfers between devices  15.5 us (2%)
  between operations  13.9 us (1%)
  matrix products  13.8 us (1%)
    all_gather x1, waiting for transfers between devices, shards(): lax.all_gather(own_grads, 'tensor', axis=0, tiled=True)  350 us
    all_gather x1, waiting for transfers between devices, shards(): expert_rows = lax.all_gather(own_rows, 'tensor', axis=0, tiled=True)  314 us
    psum x1, waiting for transfers between devices, shards(): layer_out = lax.psum(spread.astype(jnp.bfloat16), 'expert')  151 us
    all_to_all x1, waiting for transfers between devices, shards(): lax.all_to_all(partial_value, 'tensor', split_axis=0, concat_axis=0, tile...  84 us
    all_to_all x1, waiting for transfers between devices, shards(): lax.all_to_all(grad_partial.reshape(group_size, SEND, -1), 'tensor', spli...  45.6 us
  transfers between devices with their start and end apart: 5, of which 5 were waited for; matrix products, arithmetic and copies ran while one was open for 2% of the time, Pallas kernels for 0%

commit v1 on v0

v1 whole, which is shorter than its diff:
```python
import functools

import jax
import jax.numpy as jnp
from jax import lax
from jax.experimental import pallas as pl
from jax.experimental.pallas import tpu as pltpu
from jax.sharding import Mesh, PartitionSpec as P

SEND = 4
AXES = ("zh", "c", "y", "zl", "x")
SIZES = (4, 2, 4, 4, 4)


def device(zh, c, y, zl, x):
    return (((zh * 2 + c) * 4 + y) * 4 + zl) * 4 + x


def mixed_groups(first):
    groups = []
    for zh in range(4):
        for c in range(2):
            for zl in range(4):
                for still in range(4):
                    if (c == 0) == (first == "x"):
                        groups.append([device(zh, c, still, zl, k) for k in range(4)])
                    else:
                        groups.append([device(zh, c, k, zl, still) for k in range(4)])
    return groups


def spread(block, axis, groups=None):
    copies = jnp.broadcast_to(block[None], (4,) + block.shape)
    return lax.all_to_all(copies, axis, 0, 0, axis_index_groups=groups, tiled=True)


def fold(blocks, axis, groups=None):
    got = lax.all_to_all(blocks, axis, 0, 0, axis_index_groups=groups, tiled=True)
    return jnp.sum(got.astype(jnp.float32), axis=0).astype(jnp.bfloat16)


def expert_kernel(steps, rows_ref, wg_ref, wu_ref, wd_ref, out_ref, gu, dh, hid, dgu):
    step = pl.program_id(0)
    half = gu.shape[1] // 2
    rows = gu.shape[0]

    @pl.when(step == 0)
    def _():
        gu[...] = jnp.zeros_like(gu)
        dh[...] = jnp.zeros_like(dh)

    @pl.when(step < steps)
    def _():
        tok = rows_ref[:, 0].reshape(rows, -1)
        cot = rows_ref[:, 1].reshape(rows, -1)
        both = jnp.concatenate([wg_ref[...], wu_ref[...]], axis=1)
        gu[...] += jnp.dot(tok, both, preferred_element_type=jnp.float32)
        dh[...] += lax.dot_general(
            cot, wd_ref[...], (((1,), (1,)), ((), ())), preferred_element_type=jnp.float32
        )

    @pl.when(step == steps - 1)
    def _():
        gate, upper, dhid = gu[:, :half], gu[:, half:], dh[...]
        s = jax.nn.sigmoid(gate)
        hid[...] = (gate * s * upper).astype(jnp.bfloat16)
        dgu[:, :half] = (dhid * upper * s * (1.0 + gate * (1.0 - s))).astype(jnp.bfloat16)
        dgu[:, half:] = (dhid * gate * s).astype(jnp.bfloat16)

    @pl.when(step >= steps)
    def _():
        both = jnp.concatenate([wg_ref[...], wu_ref[...]], axis=1)
        out = jnp.dot(hid[...], wd_ref[...], preferred_element_type=jnp.float32)
        out_ref[:, 0] = out.astype(jnp.bfloat16).reshape(out_ref.shape[0], 16, -1)
        din = lax.dot_general(
            dgu[...], both, (((1,), (1,)), ((), ())), preferred_element_type=jnp.float32
        )
        out_ref[:, 1] = din.astype(jnp.bfloat16).reshape(out_ref.shape[0], 16, -1)


def expert_call(rows, wg, wu, wd):
    steps = 4
    blocks, _, deep, width = rows.shape
    chunk = width // steps
    count = blocks * deep
    hidden = wg.shape[1]
    return pl.pallas_call(
        functools.partial(expert_kernel, steps),
        grid=(2 * steps,),
        in_specs=[
            pl.BlockSpec((blocks, 2, deep, chunk), lambda i: (0, 0, 0, jnp.minimum(i, steps - 1))),
            pl.BlockSpec((chunk, hidden), lambda i: (lax.rem(i, steps), 0)),
            pl.BlockSpec((chunk, hidden), lambda i: (lax.rem(i, steps), 0)),
            pl.BlockSpec((hidden, chunk), lambda i: (0, lax.rem(i, steps))),
        ],
        out_specs=pl.BlockSpec(
            (blocks, 2, deep, chunk), lambda i: (0, 0, 0, jnp.maximum(i - steps, 0))
        ),
        out_shape=jax.ShapeDtypeStruct(rows.shape, jnp.bfloat16),
        scratch_shapes=[
            pltpu.VMEM((count, 2 * hidden), jnp.float32),
            pltpu.VMEM((count, hidden), jnp.float32),
            pltpu.VMEM((count, hidden), jnp.bfloat16),
            pltpu.VMEM((count, 2 * hidden), jnp.bfloat16),
        ],
        compiler_params=pltpu.CompilerParams(vmem_limit_bytes=32 * 1024 * 1024),
        cost_estimate=pl.CostEstimate(
            flops=12 * count * width * hidden, bytes_accessed=14 << 20, transcendentals=count * hidden
        ),
    )(rows, wg, wu, wd)


def shards(tokens, cotangent, expert_id, gate_weight, up_weight, down_weight):
    core = lax.axis_index("c")
    my_expert = lax.axis_index("zh") * 2 + core
    count, width = tokens.shape
    earlier = (
        jnp.arange(count, dtype=jnp.int32)[:, None] > jnp.arange(count, dtype=jnp.int32)[None, :]
    )
    slot = jnp.sum(((expert_id[:, None] == expert_id[None, :]) & earlier).astype(jnp.int32), axis=1)
    positions = jnp.arange(SEND, dtype=jnp.int32)
    selector = ((expert_id[None, :] == my_expert) & (slot[None, :] == positions[:, None])).astype(
        jnp.bfloat16
    )
    own_rows = jnp.dot(selector, tokens, preferred_element_type=jnp.float32)
    own_grads = jnp.dot(selector, cotangent, preferred_element_type=jnp.float32)
    own = jnp.stack([own_rows, own_grads]).astype(jnp.bfloat16)

    first, second = mixed_groups("x"), mixed_groups("y")
    part = spread(own, "zl")
    part = jnp.swapaxes(part, 0, 1).reshape(2, 16, width)
    part = spread(part, AXES, first)
    part = spread(part, AXES, second)
    done = expert_call(
        part.reshape(16, 2, 16, width), gate_weight[0], up_weight[0], down_weight[0]
    )
    part = fold(done.reshape(4, 4, 2, 16, width), AXES, second)
    part = fold(part, AXES, first)
    part = jnp.swapaxes(part.reshape(2, 4, SEND, width), 0, 1)
    mine = fold(part, "zl")

    mine = spread(mine, "zh")
    other = lax.ppermute(mine, "c", [(0, 1), (1, 0)])

    def cells(c):
        expert = (jnp.arange(4, dtype=jnp.int32) * 2 + c)[:, None, None]
        return ((expert_id[None, None, :] == expert) & (slot[None, None, :] == positions[:, None])).astype(
            jnp.bfloat16
        ).reshape(16, count)

    def back(index):
        both = jnp.concatenate([mine[:, index].reshape(16, width), other[:, index].reshape(16, width)])
        table = jnp.concatenate([cells(core), cells(1 - core)])
        return lax.dot_general(
            table, both, (((0,), (0,)), ((), ())), preferred_element_type=jnp.float32
        ).astype(jnp.bfloat16)

    return (back(0), back(1))


def solution(mesh):
    fine = Mesh(mesh.devices.reshape(SIZES), AXES)
    tensor, expert = ("y", "zl", "x"), ("zh", "c")
    placed = (
        P(tensor, None),
        P(tensor, None),
        P(tensor),
        P(expert, None, tensor),
        P(expert, None, tensor),
        P(expert, tensor, None),
    )
    return jax.shard_map(
        shards,
        mesh=fine,
        in_specs=placed,
        out_specs=(P(tensor, None), P(tensor, None)),
        check_vma=False,
    )
```

time: 1010 us -> 165 us (0.16)
  waiting for transfers between devices: 945 us -> 14.1 us
  blocking collectives: 0 us -> 110 us
  local copies, waits for them, and re-layouts: 18.1 us -> 2.69 us
  between operations: 13.9 us -> 0.8 us
  matrix products: 13.8 us -> 2.97 us
    all_gather x2 -> x0, waiting for transfers between devices: 664 us -> none  [the longest x1 350 us: shards(): lax.all_gather(own_grads, 'tensor', axis=0, tiled=True)]
    psum x1 -> x0, waiting for transfers between devices: 151 us -> none  [shards(): layer_out = lax.psum(spread.astype(jnp.bfloat16), 'expert')]
    all_to_all x2 -> x1, waiting for transfers between devices: 130 us -> 13.1 us  [spread(): lax.all_to_all(copies, axis, 0, 0, axis_index_groups=groups, tiled=True)]
    all_to_all x0 -> x6, blocking collectives: none -> 110 us  [the longest x3 57.8 us: spread(): lax.all_to_all(copies, axis, 0, 0, axis_index_groups=groups, tiled=True)]
    ppermute x0 -> x1, starting transfers between devices: none -> 11.5 us  [shards(): other = lax.ppermute(mine, 'c', [(0, 1), (1, 0)])]
    dot_general x10 -> x4, matrix products: 13.8 us -> 2.97 us  [the longest x2 1.78 us: back(): lax.dot_general(table, both, (((0,), (0,)), ((), ())), preferred_element_...]
  transfers between devices with their start and end apart: 5 -> 2, of which waited for: 5 -> 2; matrix products, arithmetic and copies ran while one was open for 2% -> 0% of each run, Pallas kernels for 0% -> 0%
where the time goes in v1:
time: 165 us; the launch traced here: 164 us
  blocking collectives  110 us (67%)
  starting transfers between devices  23.6 us (14%)
  waiting for transfers between devices  14.1 us (9%)
  other arithmetic  5.14 us (3%)
  Pallas kernels  4.65 us (3%)
  matrix products  2.97 us (2%)
  local copies, waits for them, and re-layouts  2.69 us (2%)
    all_to_all x3, blocking collectives, spread(): lax.all_to_all(copies, axis, 0, 0, axis_index_groups=groups, tiled=True)  57.8 us
    all_to_all x3, blocking collectives, fold(): lax.all_to_all(blocks, axis, 0, 0, axis_index_groups=groups, tiled=True)  52.6 us
    all_to_all x1, waiting for transfers between devices, spread(): lax.all_to_all(copies, axis, 0, 0, axis_index_groups=groups, tiled=True)  13.1 us
    all_to_all x1, starting transfers between devices, spread(): lax.all_to_all(copies, axis, 0, 0, axis_index_groups=groups, tiled=True)  12.1 us
    ppermute x1, starting transfers between devices, shards(): other = lax.ppermute(mine, 'c', [(0, 1), (1, 0)])  11.5 us
    pallas_call x1, Pallas kernels, expert_call(): pl.pallas_call(functools.partial(expert_kernel, steps), grid=(2 * steps,)...  4.65 us
    reduce_sum x3, other arithmetic, fold(): return jnp.sum(got.astype(jnp.float32), axis=0).astype(jnp.bfloat16)  3.42 us
  transfers between devices with their start and end apart: 2, of which 2 were waited for; matrix products, arithmetic and copies ran while one was open for 0% of the time, Pallas kernels for 0%

profile of v1, /device:TPU:1, one launch (start us, length us, event | category | flops | bytes accessed | tf_op | source)
XLA Modules:
  0.0 164.4 jit_solution(4547429558035928391)
XLA Ops:
  0.6 0.0 copy-start
  0.7 0.9 convert_reduce_fusion
  1.6 0.7 broadcast_compare_fusion.2
  2.2 0.0 copy-done
  2.2 0.1 fusion.1
  2.4 1.1 fusion
  3.5 0.1 broadcast_in_dim.10
  3.6 12.2 %all_to_all.35 = bf16[4,2,4,4096]{3,2,1,0:T(4,128)(2,1)S(1)} all-to-all(bf16[4,2,4,4096]{3,2,1,0:T(4,128)(2,1)S(1)} %broadcast_in_dim.10), channel_id=1, replica_groups=mesh['zh'=4,'c'=2,'y'=4,'zl'=4,'x'=4] {'zl'}, dimensions={0} | all-to-all | bytes 524288 | tf_op jit(solution)/shard_map/all_to_all | solution.py:34
  15.8 0.3 copy.11
  16.1 0.2 copy.12
  16.2 0.1 broadcast_in_dim.12
  16.3 14.9 %all_to_all.36 = bf16[4,2,16,4096]{3,2,1,0:T(8,128)(2,1)S(1)} all-to-all(bf16[4,2,16,4096]{3,2,1,0:T(8,128)(2,1)S(1)} %broadcast_in_dim.12), channel_id=1, replica_groups={{0,1,2,3},{16,17,18,19},{32,33,34,35},{48,49,50,51},{4,5,6,7},{20,21,22..., dimensions={0} | all-to-all | bytes 2097152 | tf_op jit(solution)/shard_map/all_to_all | solution.py:34
  31.3 0.5 broadcast_in_dim.13
  31.8 0.0 copy-start.1
  31.8 0.0 copy-start.2
  31.8 0.0 copy-start.3
  31.8 30.7 %all_to_all.37 = bf16[4,4,2,16,4096]{4,3,2,1,0:T(8,128)(2,1)S(1)} all-to-all(bf16[4,4,2,16,4096]{4,3,2,1,0:T(8,128)(2,1)S(1)} %broadcast_in_dim.13), channel_id=1, replica_groups={{0,16,32,48},{1,17,33,49},{2,18,34,50},{3,19,35,51},{4,20,36,52},{5,21,..., dimensions={0} | all-to-all | bytes 8388608 | tf_op jit(solution)/shard_map/all_to_all | solution.py:34
  62.5 0.0 copy-done.1
  62.5 0.0 copy-done.2
  62.5 0.0 copy-done.3
  62.5 4.7 %shard_map.77 = bf16[16,2,16,4096]{3,2,1,0:T(8,128)(2,1)S(1)} custom-call(bf16[16,2,16,4096]{3,2,1,0:T(8,128)(2,1)S(1)} %bitcast.18, bf16[4096,128]{1,0:T(8,128)(2,1)S(1)} %bitcast.20, bf16[4096,128]{1,0:T(8,128)(2,1)S(1)} %bitcast.21, bf16[128,4096]{1,0:T(8,128)(2,1)S(1)} %bitcast.22), custom_call_target="tpu_custom_call" | custom-call | flops 1610612736 | bytes 14680064 | tf_op jit(solution)/shard_map/pallas_call | solution.py:87
  67.1 30.0 %all_to_all.38 = bf16[4,4,2,16,4096]{4,3,2,1,0:T(8,128)(2,1)} all-to-all(bf16[4,4,2,16,4096]{4,3,2,1,0:T(8,128)(2,1)S(1)} %bitcast.19), channel_id=1, replica_groups={{0,16,32,48},{1,17,33,49},{2,18,34,50},{3,19,35,51},{4,20,36,52},{5,21,..., dimensions={0} | all-to-all | bytes 8388608 | tf_op jit(solution)/shard_map/all_to_all | solution.py:38
  97.1 3.1 %reduce_sum.46 = bf16[4,2,16,4096]{3,2,1,0:T(8,128)(2,1)S(1)} reduce(bf16[4,4,2,16,4096]{4,3,2,1,0:T(8,128)(2,1)} %all_to_all.38, bf16[]{:T(256)} %constant.23.clone.1), dimensions={0}, to_apply=%region_1.0 | reduce | flops 1572864 | bytes 5242882 | tf_op jit(solution)/shard_map/reduce_sum | solution.py:39
  100.2 0.0 copy-start.4
  100.2 12.2 %all_to_all.39 = bf16[4,2,16,4096]{3,2,1,0:T(8,128)(2,1)S(1)} all-to-all(bf16[4,2,16,4096]{3,2,1,0:T(8,128)(2,1)S(1)} %reduce_sum.46), channel_id=1, replica_groups={{0,1,2,3},{16,17,18,19},{32,33,34,35},{48,49,50,51},{4,5,6,7},{20,21,22..., dimensions={0} | all-to-all | bytes 2097152 | tf_op jit(solution)/shard_map/all_to_all | solution.py:38
  112.4 0.2 reduce_sum.47
  112.6 0.3 copy.13
  112.9 0.2 copy.14
  113.1 10.4 %all_to_all.40 = bf16[4,2,4,4096]{3,2,1,0:T(4,128)(2,1)S(1)} all-to-all(bf16[4,2,4,4096]{3,2,1,0:T(4,128)(2,1)S(1)} %copy.14), channel_id=1, replica_groups=mesh['zh'=4,'c'=2,'y'=4,'zl'=4,'x'=4] {'zl'}, dimensions={0} | all-to-all | bytes 524288 | tf_op jit(solution)/shard_map/all_to_all | solution.py:38
  123.5 0.1 reduce_sum.48
  123.7 0.8 broadcast_in_dim.14
  124.4 12.1 %all-to-all-start.6 = ((bf16[4,2,4,4096]{3,2,1,0:T(4,128)(2,1)}), bf16[4,2,4,4096]{3,2,1,0:T(4,128)(2,1)S(1)}, u32[]{:S(2)}, u32[]{:S(2)}) async-start(bf16[4,2,4,4096]{3,2,1,0:T(4,128)(2,1)} %broadcast_in_dim.14), calls=%async_computation.6 | async-start | bytes 524288 | tf_op jit(solution)/shard_map/all_to_all | solution.py:34
  136.5 0.0 copy-done.4
  136.6 0.1 broadcast_compare_fusion.1
  136.6 13.1 %all-to-all-done.6 = bf16[4,2,4,4096]{3,2,1,0:T(4,128)(2,1)S(1)} async-done(((bf16[4,2,4,4096]{3,2,1,0:T(4,128)(2,1)}), bf16[4,2,4,4096]{3,2,1,0:T(4,128)(2,1)S(1)}, u32[]{:S(2)}, u32[]{:S(2)}) %all-to-all-start.6) | async-done | bytes 262176 | tf_op jit(solution)/shard_map/all_to_all | solution.py:34
  149.7 11.5 %collective-permute-start = (bf16[4,2,4,4096]{3,2,1,0:T(4,128)(2,1)S(1)}, bf16[4,2,4,4096]{3,2,1,0:T(4,128)(2,1)S(1)}, u32[]{:S(2)}, u32[]{:S(2)}) collective-permute-start(bf16[4,2,4,4096]{3,2,1,0:T(4,128)(2,1)S(1)} %all-to-all-done.6), channel_id=1, source_target_pairs={{0,64},{64,0},{1,65},{65,1},{2,66},{66,2},{3,67},{67,3},{4,68},{68... | collective-permute-start | bytes 786440 | tf_op jit(solution)/shard_map/ppermute | solution.py:143
  161.3 0.1 fusion.19
  161.4 1.0 collective-permute-done
  162.4 0.1 fusion.20
  162.6 0.9 convolution_convert_fusion.1
  163.5 0.9 convolution_convert_fusion
  (8 shorter events, 0.2 us)
Async XLA Ops:
  0.6 1.6 copy-start
  31.8 30.7 %copy-start.1 = (bf16[1,4096,128]{2,1,0:T(8,128)(2,1)S(1)}, bf16[1,4096,128]{2,1,0:T(8,128)(2,1)}, u32[]{:S(2)}) copy-start(bf16[1,4096,128]{2,1,0:T(8,128)(2,1)} %param.9) | copy-start | bytes 3145732
  31.8 30.7 %copy-start.2 = (bf16[1,4096,128]{2,1,0:T(8,128)(2,1)S(1)}, bf16[1,4096,128]{2,1,0:T(8,128)(2,1)}, u32[]{:S(2)}) copy-start(bf16[1,4096,128]{2,1,0:T(8,128)(2,1)} %param.10) | copy-start | bytes 3145732
  31.8 30.7 %copy-start.3 = (bf16[1,128,4096]{2,1,0:T(8,128)(2,1)S(1)}, bf16[1,128,4096]{2,1,0:T(8,128)(2,1)}, u32[]{:S(2)}) copy-start(bf16[1,128,4096]{2,1,0:T(8,128)(2,1)} %param.11) | copy-start | bytes 3145732
  100.2 36.3 %copy-start.4 = (s32[16]{0:T(128)S(1)}, s32[16]{0:T(128)}, u32[]{:S(2)}) copy-start(s32[16]{0:T(128)} %param.8) | copy-start | bytes 196
  124.4 25.3 %all-to-all-start.6 = ((bf16[4,2,4,4096]{3,2,1,0:T(4,128)(2,1)}), bf16[4,2,4,4096]{3,2,1,0:T(4,128)(2,1)S(1)}, u32[]{:S(2)}, u32[]{:S(2)}) async-start(bf16[4,2,4,4096]{3,2,1,0:T(4,128)(2,1)} %broadcast_in_dim.14), calls=%async_computation.6 | async-start | bytes 524288 | tf_op jit(solution)/shard_map/all_to_all | solution.py:34
  149.7 12.7 %collective-permute-start = (bf16[4,2,4,4096]{3,2,1,0:T(4,128)(2,1)S(1)}, bf16[4,2,4,4096]{3,2,1,0:T(4,128)(2,1)S(1)}, u32[]{:S(2)}, u32[]{:S(2)}) collective-permute-start(bf16[4,2,4,4096]{3,2,1,0:T(4,128)(2,1)S(1)} %all-to-all-done.6), channel_id=1, source_target_pairs={{0,64},{64,0},{1,65},{65,1},{2,66},{66,2},{3,67},{67,3},{4,68},{68... | collective-permute-start | bytes 786440 | tf_op jit(solution)/shard_map/ppermute | solution.py:143

commit v2 on v1

v2 whole, which is shorter than its diff:
```python
import functools

import jax
import jax.numpy as jnp
from jax import lax
from jax.experimental import pallas as pl
from jax.experimental.pallas import tpu as pltpu
from jax.sharding import Mesh, PartitionSpec as P

SEND = 4
AXES = ("zh", "c", "y", "zl", "x")
SIZES = (4, 2, 4, 4, 4)


def device(zh, c, y, zl, x):
    return (((zh * 2 + c) * 4 + y) * 4 + zl) * 4 + x


def mixed_groups(first):
    groups = []
    for zh in range(4):
        for c in range(2):
            for zl in range(4):
                for still in range(4):
                    if (c == 0) == (first == "x"):
                        groups.append([device(zh, c, still, zl, k) for k in range(4)])
                    else:
                        groups.append([device(zh, c, k, zl, still) for k in range(4)])
    return groups


def spread(block, axis, groups=None):
    copies = jnp.broadcast_to(block[None], (4,) + block.shape)
    return lax.all_to_all(copies, axis, 0, 0, axis_index_groups=groups, tiled=True)


def fold(blocks, axis, groups=None):
    got = lax.all_to_all(blocks, axis, 0, 0, axis_index_groups=groups, tiled=True)
    return jnp.sum(got.astype(jnp.float32), axis=0).astype(jnp.bfloat16)


def along(step):
    pairs = []
    for zh in range(4):
        for zl in range(4):
            for y in range(4):
                for x in range(4):
                    pairs.append((device(zh, 0, y, zl, x), device(zh, 0, (y + step) % 4, zl, x)))
                    pairs.append((device(zh, 1, y, zl, x), device(zh, 1, y, zl, (x + step) % 4)))
    return pairs


def right(block):
    return lax.ppermute(block, AXES, along(1))


def left(block):
    return lax.ppermute(block, AXES, along(3))


def block_kernel(number, *refs):
    ins, (wg_ref, wu_ref, wd_ref), outs = refs[:number], refs[number : number + 3], refs[number + 3 :]
    width, hidden = wg_ref.shape
    chunk = 1024
    deep = ins[0].shape[0] * 16
    gu = dh = None
    for k in range(0, width, chunk):
        tok = jnp.concatenate([r[:, 0, :, k : k + chunk].reshape(deep, chunk) for r in ins])
        cot = jnp.concatenate([r[:, 1, :, k : k + chunk].reshape(deep, chunk) for r in ins])
        both = jnp.concatenate([wg_ref[k : k + chunk, :], wu_ref[k : k + chunk, :]], axis=1)
        one = jnp.dot(tok, both, preferred_element_type=jnp.float32)
        two = lax.dot_general(
            cot,
            wd_ref[:, k : k + chunk],
            (((1,), (1,)), ((), ())),
            preferred_element_type=jnp.float32,
        )
        gu, dh = (one, two) if gu is None else (gu + one, dh + two)
    gate, upper = gu[:, :hidden], gu[:, hidden:]
    s = jax.nn.sigmoid(gate)
    hid = (gate * s * upper).astype(jnp.bfloat16)
    dgate = (dh * upper * s * (1.0 + gate * (1.0 - s))).astype(jnp.bfloat16)
    dup = (dh * gate * s).astype(jnp.bfloat16)
    dgu = jnp.concatenate([dgate, dup], axis=1)
    for k in range(0, width, chunk):
        both = jnp.concatenate([wg_ref[k : k + chunk, :], wu_ref[k : k + chunk, :]], axis=1)
        out = jnp.dot(hid, wd_ref[:, k : k + chunk], preferred_element_type=jnp.float32)
        din = lax.dot_general(
            dgu, both, (((1,), (1,)), ((), ())), preferred_element_type=jnp.float32
        )
        for i, ref in enumerate(outs):
            rows = slice(i * deep, (i + 1) * deep)
            ref[:, 0, :, k : k + chunk] = out[rows].astype(jnp.bfloat16).reshape(-1, 16, chunk)
            ref[:, 1, :, k : k + chunk] = din[rows].astype(jnp.bfloat16).reshape(-1, 16, chunk)


def experts(blocks, weights):
    number = len(blocks)
    width, hidden = weights[0].shape
    count = number * blocks[0].shape[0] * 16
    inside = pl.BlockSpec(memory_space=pltpu.VMEM)
    return pl.pallas_call(
        functools.partial(block_kernel, number),
        in_specs=[inside] * (number + 3),
        out_specs=[inside] * number,
        out_shape=[jax.ShapeDtypeStruct(b.shape, jnp.bfloat16) for b in blocks],
        compiler_params=pltpu.CompilerParams(vmem_limit_bytes=24 << 20),
        cost_estimate=pl.CostEstimate(
            flops=12 * count * width * hidden,
            bytes_accessed=(3 << 20) + 4 * count * width * 2,
            transcendentals=count * hidden,
        ),
    )(*blocks, *weights)


def add_kernel(groups, *refs):
    ins, outs = refs[: sum(groups)], refs[sum(groups) :]
    at = 0
    for number, out in zip(groups, outs):
        total = ins[at][...].astype(jnp.float32)
        for ref in ins[at + 1 : at + number]:
            total += ref[...].astype(jnp.float32)
        out[...] = total.astype(jnp.bfloat16)
        at += number


def added(*groups):
    flat = [block for group in groups for block in group]
    size = sum(block.size for block in flat)
    inside = pl.BlockSpec(memory_space=pltpu.VMEM)
    return pl.pallas_call(
        functools.partial(add_kernel, [len(group) for group in groups]),
        in_specs=[inside] * len(flat),
        out_specs=[inside] * len(groups),
        out_shape=[jax.ShapeDtypeStruct(group[0].shape, jnp.bfloat16) for group in groups],
        compiler_params=pltpu.CompilerParams(vmem_limit_bytes=24 << 20),
        cost_estimate=pl.CostEstimate(flops=size, bytes_accessed=3 * size, transcendentals=0),
    )(*flat)


def large_stage(block, weights):
    one, two = block[:2], block[2:]
    from_left_one, from_right_two = right(one), left(two)
    from_left_two, from_right_one = right(two), left(one)
    far_one, far_two = right(from_left_one), left(from_right_two)
    own = experts([block], weights)[0]
    to_left_one, to_left_two, to_right_one, to_right_two = experts(
        [from_left_one, from_left_two, from_right_one, from_right_two], weights
    )
    to_far_one, to_far_two = experts([far_one, far_two], weights)
    got_one, got_two = right(to_far_one), left(to_far_two)
    two_from_left, one_from_right = right(to_right_two), left(to_left_one)
    sum_one, sum_two = added([to_right_one, got_one], [to_left_two, got_two])
    one_from_left, two_from_right = right(sum_one), left(sum_two)
    one, two = added([own[:2], one_from_left, one_from_right], [own[2:], two_from_left, two_from_right])
    return jnp.concatenate([one, two])


def shards(tokens, cotangent, expert_id, gate_weight, up_weight, down_weight):
    core = lax.axis_index("c")
    my_expert = lax.axis_index("zh") * 2 + core
    count, width = tokens.shape
    earlier = (
        jnp.arange(count, dtype=jnp.int32)[:, None] > jnp.arange(count, dtype=jnp.int32)[None, :]
    )
    slot = jnp.sum(((expert_id[:, None] == expert_id[None, :]) & earlier).astype(jnp.int32), axis=1)
    positions = jnp.arange(SEND, dtype=jnp.int32)
    selector = ((expert_id[None, :] == my_expert) & (slot[None, :] == positions[:, None])).astype(
        jnp.bfloat16
    )
    own_rows = jnp.dot(selector, tokens, preferred_element_type=jnp.float32)
    own_grads = jnp.dot(selector, cotangent, preferred_element_type=jnp.float32)
    own = jnp.stack([own_rows, own_grads]).astype(jnp.bfloat16)

    first = mixed_groups("x")
    part = spread(own, "zl")
    part = jnp.swapaxes(part, 0, 1).reshape(2, 16, width)
    part = spread(part, AXES, first)
    part = large_stage(part, (gate_weight[0], up_weight[0], down_weight[0]))
    part = fold(part, AXES, first)
    part = jnp.swapaxes(part.reshape(2, 4, SEND, width), 0, 1)
    mine = fold(part, "zl")

    mine = spread(mine, "zh")
    other = lax.ppermute(mine, "c", [(0, 1), (1, 0)])

    def cells(c):
        expert = (jnp.arange(4, dtype=jnp.int32) * 2 + c)[:, None, None]
        return ((expert_id[None, None, :] == expert) & (slot[None, None, :] == positions[:, None])).astype(
            jnp.bfloat16
        ).reshape(16, count)

    def back(index):
        both = jnp.concatenate([mine[:, index].reshape(16, width), other[:, index].reshape(16, width)])
        table = jnp.concatenate([cells(core), cells(1 - core)])
        return lax.dot_general(
            table, both, (((0,), (0,)), ((), ())), preferred_element_type=jnp.float32
        ).astype(jnp.bfloat16)

    return (back(0), back(1))


def solution(mesh):
    fine = Mesh(mesh.devices.reshape(SIZES), AXES)
    tensor, expert = ("y", "zl", "x"), ("zh", "c")
    placed = (
        P(tensor, None),
        P(tensor, None),
        P(tensor),
        P(expert, None, tensor),
        P(expert, None, tensor),
        P(expert, tensor, None),
    )
    return jax.shard_map(
        shards,
        mesh=fine,
        in_specs=placed,
        out_specs=(P(tensor, None), P(tensor, None)),
        check_vma=False,
    )
```

time: 165 us -> 156 us (0.945)
  blocking collectives: 110 us -> 49.6 us
  starting transfers between devices: 23.6 us -> 65.6 us
  waiting for transfers between devices: 14.1 us -> 26 us
  other arithmetic: 5.14 us -> 2.17 us
    ppermute x0 -> x12, starting transfers between devices: none -> 38.2 us  [the longest x6 24.4 us: left(): return lax.ppermute(block, AXES, along(3))]
    all_to_all x3 -> x2, blocking collectives: 57.8 us -> 27.3 us  [spread(): lax.all_to_all(copies, axis, 0, 0, axis_index_groups=groups, tiled=True)]
    all_to_all x3 -> x2, blocking collectives: 52.6 us -> 22.3 us  [fold(): lax.all_to_all(blocks, axis, 0, 0, axis_index_groups=groups, tiled=True)]
    ppermute x0 -> x12, waiting for transfers between devices: none -> 12.8 us  [the longest x6 6.76 us: right(): return lax.ppermute(block, AXES, along(1))]
    ppermute x1, starting transfers between devices: 11.5 us -> 15.4 us  [shards(): other = lax.ppermute(mine, 'c', [(0, 1), (1, 0)])]
    reduce_sum x3 -> x2, other arithmetic: 3.42 us -> 0.35 us  [fold(): return jnp.sum(got.astype(jnp.float32), axis=0).astype(jnp.bfloat16)]
    pallas_call x1 -> x5, Pallas kernels: 4.65 us -> 5.92 us  [the longest x3 5.3 us: experts(): pl.pallas_call(functools.partial(block_kernel, number), in_specs=[inside]...]
  transfers between devices with their start and end apart: 2 -> 14, of which waited for: 2 -> 6; matrix products, arithmetic and copies ran while one was open for 0% -> 0% of each run, Pallas kernels for 0% -> 4%
where the time goes in v2:
time: 156 us; the launch traced here: 155 us
  starting transfers between devices  65.6 us (42%)
  blocking collectives  49.6 us (32%)
  waiting for transfers between devices  26 us (17%)
  Pallas kernels  5.92 us (4%)
  local copies, waits for them, and re-layouts  3.03 us (2%)
  other arithmetic  2.17 us (1%)
  matrix products  2.07 us (1%)
    all_to_all x2, blocking collectives, spread(): lax.all_to_all(copies, axis, 0, 0, axis_index_groups=groups, tiled=True)  27.3 us
    ppermute x6, starting transfers between devices, left(): return lax.ppermute(block, AXES, along(3))  24.4 us
    all_to_all x2, blocking collectives, fold(): lax.all_to_all(blocks, axis, 0, 0, axis_index_groups=groups, tiled=True)  22.3 us
    ppermute x1, starting transfers between devices, shards(): other = lax.ppermute(mine, 'c', [(0, 1), (1, 0)])  15.4 us
    ppermute x6, starting transfers between devices, right(): return lax.ppermute(block, AXES, along(1))  13.8 us
    all_to_all x1, waiting for transfers between devices, spread(): lax.all_to_all(copies, axis, 0, 0, axis_index_groups=groups, tiled=True)  12.3 us
    all_to_all x1, starting transfers between devices, spread(): lax.all_to_all(copies, axis, 0, 0, axis_index_groups=groups, tiled=True)  12.1 us
    ppermute x6, waiting for transfers between devices, right(): return lax.ppermute(block, AXES, along(1))  6.76 us
  transfers between devices with their start and end apart: 14, of which 6 were waited for; matrix products, arithmetic and copies ran while one was open for 0% of the time, Pallas kernels for 4%

profile of v2, /device:TPU:1, one launch (start us, length us, event | category | flops | bytes accessed | tf_op | source)
XLA Modules:
  0.0 155.4 jit_solution(9898586720444802877)
XLA Ops:
  0.7 0.9 convert_reduce_fusion
  1.6 0.7 broadcast_compare_fusion.2
  2.2 0.1 fusion
  2.4 0.1 fusion.1
  2.7 12.2 %all_to_all.25 = bf16[4,2,4,4096]{3,2,1,0:T(4,128)(2,1)S(1)} all-to-all(bf16[4,2,4,4096]{3,2,1,0:T(4,128)(2,1)S(1)} %broadcast_in_dim.8), channel_id=1, replica_groups=mesh['zh'=4,'c'=2,'y'=4,'zl'=4,'x'=4] {'zl'}, dimensions={0} | all-to-all | bytes 524288 | tf_op jit(solution)/shard_map/all_to_all | solution.py:34
  14.9 0.3 copy.15
  15.2 0.2 copy.16
  15.3 0.1 broadcast_in_dim.10
  15.4 15.1 %all_to_all.26.refs_0_ = bf16[4,2,16,4096]{3,2,1,0:T(8,128)(2,1)S(1)} all-to-all(bf16[4,2,16,4096]{3,2,1,0:T(8,128)(2,1)S(1)} %broadcast_in_dim.10), channel_id=1, replica_groups={{0,1,2,3},{16,17,18,19},{32,33,34,35},{48,49,50,51},{4,5,6,7},{20,21,22..., dimensions={0} | all-to-all | bytes 2097152 | tf_op jit(solution)/shard_map/all_to_all | solution.py:34
  30.6 3.0 %collective-permute-start = (bf16[2,2,16,4096]{3,2,1,0:T(8,128)(2,1)S(1)}, bf16[2,2,16,4096]{3,2,1,0:T(8,128)(2,1)S(1)}, u32[]{:S(2)}, u32[]{:S(2)}) collective-permute-start(bf16[2,2,16,4096]{3,2,1,0:T(8,128)(2,1)S(1)} %get-tuple-element.25), channel_id=1, source_target_pairs={{0,16},{64,65},{1,17},{65,66},{2,18},{66,67},{3,19},{67,64},{16,32... | collective-permute-start | bytes 1572872 | tf_op jit(solution)/shard_map/ppermute | solution.py:54
  33.6 3.7 %collective-permute-start.3 = (bf16[2,2,16,4096]{3,2,1,0:T(8,128)(2,1)S(1)}, bf16[2,2,16,4096]{3,2,1,0:T(8,128)(2,1)S(1)}, u32[]{:S(2)}, u32[]{:S(2)}) collective-permute-start(bf16[2,2,16,4096]{3,2,1,0:T(8,128)(2,1)S(1)} %get-tuple-element.24), channel_id=1, source_target_pairs={{0,48},{64,67},{1,49},{65,64},{2,50},{66,65},{3,51},{67,66},{16,0}... | collective-permute-start | bytes 1572872 | tf_op jit(solution)/shard_map/ppermute | solution.py:58
  37.2 4.9 %collective-permute-done.refs_0_ = bf16[2,2,16,4096]{3,2,1,0:T(8,128)(2,1)S(1)} collective-permute-done((bf16[2,2,16,4096]{3,2,1,0:T(8,128)(2,1)S(1)}, bf16[2,2,16,4096]{3,2,1,0:T(8,128)(2,1)S(1)}, u32[]{:S(2)}, u32[]{:S(2)}) %collective-permute-start) | collective-permute-done | bytes 524320 | tf_op jit(solution)/shard_map/ppermute | solution.py:54
  42.2 1.9 %collective-permute-start.4 = (bf16[2,2,16,4096]{3,2,1,0:T(8,128)(2,1)S(1)}, bf16[2,2,16,4096]{3,2,1,0:T(8,128)(2,1)S(1)}, u32[]{:S(2)}, u32[]{:S(2)}) collective-permute-start(bf16[2,2,16,4096]{3,2,1,0:T(8,128)(2,1)S(1)} %collective-permute-done.refs_0_), channel_id=1, source_target_pairs={{0,16},{64,65},{1,17},{65,66},{2,18},{66,67},{3,19},{67,64},{16,32... | collective-permute-start | bytes 1572872 | tf_op jit(solution)/shard_map/ppermute | solution.py:54
  44.1 4.6 %collective-permute-start.5 = (bf16[2,2,16,4096]{3,2,1,0:T(8,128)(2,1)S(1)}, bf16[2,2,16,4096]{3,2,1,0:T(8,128)(2,1)S(1)}, u32[]{:S(2)}, u32[]{:S(2)}) collective-permute-start(bf16[2,2,16,4096]{3,2,1,0:T(8,128)(2,1)S(1)} %collective-permute-done.3.refs_3_), channel_id=1, source_target_pairs={{0,48},{64,67},{1,49},{65,64},{2,50},{66,65},{3,51},{67,66},{16,0}... | collective-permute-start | bytes 1572872 | tf_op jit(solution)/shard_map/ppermute | solution.py:58
  48.7 1.9 %collective-permute-start.1 = (bf16[2,2,16,4096]{3,2,1,0:T(8,128)(2,1)S(1)}, bf16[2,2,16,4096]{3,2,1,0:T(8,128)(2,1)S(1)}, u32[]{:S(2)}, u32[]{:S(2)}) collective-permute-start(bf16[2,2,16,4096]{3,2,1,0:T(8,128)(2,1)S(1)} %get-tuple-element.24), channel_id=1, source_target_pairs={{0,16},{64,65},{1,17},{65,66},{2,18},{66,67},{3,19},{67,64},{16,32... | collective-permute-start | bytes 1572872 | tf_op jit(solution)/shard_map/ppermute | solution.py:54
  50.6 4.6 %collective-permute-start.2 = (bf16[2,2,16,4096]{3,2,1,0:T(8,128)(2,1)S(1)}, bf16[2,2,16,4096]{3,2,1,0:T(8,128)(2,1)S(1)}, u32[]{:S(2)}, u32[]{:S(2)}) collective-permute-start(bf16[2,2,16,4096]{3,2,1,0:T(8,128)(2,1)S(1)} %get-tuple-element.25), channel_id=1, source_target_pairs={{0,48},{64,67},{1,49},{65,64},{2,50},{66,65},{3,51},{67,66},{16,0}... | collective-permute-start | bytes 1572872 | tf_op jit(solution)/shard_map/ppermute | solution.py:58
  55.2 1.8 %shard_map.79 = (bf16[2,2,16,4096]{3,2,1,0:T(8,128)(2,1)S(1)}, bf16[2,2,16,4096]{3,2,1,0:T(8,128)(2,1)S(1)}) custom-call(bf16[2,2,16,4096]{3,2,1,0:T(8,128)(2,1)S(1)} %collective-permute-done.4.refs_0_, bf16[2,2,16,4096]{3,2,1,0:T(8,128)(2,1)S(1)} %collective-permute-done.5.refs_1_, bf16[4096,128]{1,0:T(8,128)(2,1)S(1)} %bitcast.16, ...), custom_call_target="tpu_custom_call" | custom-call | flops 402653184 | bytes 5242880 | tf_op jit(solution)/shard_map/pallas_call | solution.py:102
  57.0 1.9 %collective-permute-start.6 = (bf16[2,2,16,4096]{3,2,1,0:T(8,128)(2,1)S(1)}, bf16[2,2,16,4096]{3,2,1,0:T(8,128)(2,1)S(1)}, u32[]{:S(2)}, u32[]{:S(2)}) collective-permute-start(bf16[2,2,16,4096]{3,2,1,0:T(8,128)(2,1)S(1)} %get-tuple-element.13), channel_id=1, source_target_pairs={{0,16},{64,65},{1,17},{65,66},{2,18},{66,67},{3,19},{67,64},{16,32... | collective-permute-start | bytes 1572872 | tf_op jit(solution)/shard_map/ppermute | solution.py:54
  58.9 4.9 %collective-permute-start.7 = (bf16[2,2,16,4096]{3,2,1,0:T(8,128)(2,1)S(1)}, bf16[2,2,16,4096]{3,2,1,0:T(8,128)(2,1)S(1)}, u32[]{:S(2)}, u32[]{:S(2)}) collective-permute-start(bf16[2,2,16,4096]{3,2,1,0:T(8,128)(2,1)S(1)} %get-tuple-element.15), channel_id=1, source_target_pairs={{0,48},{64,67},{1,49},{65,64},{2,50},{66,65},{3,51},{67,66},{16,0}... | collective-permute-start | bytes 1572872 | tf_op jit(solution)/shard_map/ppermute | solution.py:58
  63.8 1.8 %shard_map.77 = bf16[4,2,16,4096]{3,2,1,0:T(8,128)(2,1)S(1)} custom-call(bf16[4,2,16,4096]{3,2,1,0:T(8,128)(2,1)S(1)} %all_to_all.26.refs_0_, bf16[4096,128]{1,0:T(8,128)(2,1)S(1)} %bitcast.17, bf16[4096,128]{1,0:T(8,128)(2,1)S(1)} %bitcast.20, bf16[128,4096]{1,0:T(8,128)(2,1)S(1)} %bitcast.23), custom_call_target="tpu_custom_call" | custom-call | flops 402653184 | bytes 5242880 | tf_op jit(solution)/shard_map/pallas_call | solution.py:102
  65.6 1.8 %shard_map.78 = (bf16[2,2,16,4096]{3,2,1,0:T(8,128)(2,1)S(1)}, bf16[2,2,16,4096]{3,2,1,0:T(8,128)(2,1)S(1)}, bf16[2,2,16,4096]{3,2,1,0:T(8,128)(2,1)S(1)}, bf16[2,2,16,4096]{3,2,1,0:T(8,128)(2,1)S(1)}) custom-call(bf16[2,2,16,4096]{3,2,1,0:T(8,128)(2,1)S(1)} %collective-permute-done.refs_0_, bf16[2,2,16,4096]{3,2,1,0:T(8,128)(2,1)S(1)} %collective-permute-done.1.refs_1_, ...), custom_call_target="tpu_custom_call" | custom-call | flops 805306368 | bytes 7340032 | tf_op jit(solution)/shard_map/pallas_call | solution.py:102
  67.4 1.9 %collective-permute-start.10 = (bf16[2,2,16,4096]{3,2,1,0:T(8,128)(2,1)S(1)}, bf16[2,2,16,4096]{3,2,1,0:T(8,128)(2,1)S(1)}, u32[]{:S(2)}, u32[]{:S(2)}) collective-permute-start(bf16[2,2,16,4096]{3,2,1,0:T(8,128)(2,1)S(1)} %get-tuple-element.18), channel_id=1, source_target_pairs={{0,16},{64,65},{1,17},{65,66},{2,18},{66,67},{3,19},{67,64},{16,32... | collective-permute-start | bytes 1572872 | tf_op jit(solution)/shard_map/ppermute | solution.py:54
  69.3 4.6 %collective-permute-start.9 = (bf16[2,2,16,4096]{3,2,1,0:T(8,128)(2,1)S(1)}, bf16[2,2,16,4096]{3,2,1,0:T(8,128)(2,1)S(1)}, u32[]{:S(2)}, u32[]{:S(2)}) collective-permute-start(bf16[2,2,16,4096]{3,2,1,0:T(8,128)(2,1)S(1)} %get-tuple-element.17), channel_id=1, source_target_pairs={{0,48},{64,67},{1,49},{65,64},{2,50},{66,65},{3,51},{67,66},{16,0}... | collective-permute-start | bytes 1572872 | tf_op jit(solution)/shard_map/ppermute | solution.py:58
  73.9 0.2 shard_map.80
  74.2 2.1 %collective-permute-start.11 = (bf16[2,2,16,4096]{3,2,1,0:T(8,128)(2,1)S(1)}, bf16[2,2,16,4096]{3,2,1,0:T(8,128)(2,1)S(1)}, u32[]{:S(2)}, u32[]{:S(2)}) collective-permute-start(bf16[2,2,16,4096]{3,2,1,0:T(8,128)(2,1)S(1)} %get-tuple-element.19), channel_id=1, source_target_pairs={{0,48},{64,67},{1,49},{65,64},{2,50},{66,65},{3,51},{67,66},{16,0}... | collective-permute-start | bytes 1572872 | tf_op jit(solution)/shard_map/ppermute | solution.py:58
  76.3 3.1 %collective-permute-start.8 = (bf16[2,2,16,4096]{3,2,1,0:T(8,128)(2,1)S(1)}, bf16[2,2,16,4096]{3,2,1,0:T(8,128)(2,1)S(1)}, u32[]{:S(2)}, u32[]{:S(2)}) collective-permute-start(bf16[2,2,16,4096]{3,2,1,0:T(8,128)(2,1)S(1)} %get-tuple-element.16), channel_id=1, source_target_pairs={{0,16},{64,65},{1,17},{65,66},{2,18},{66,67},{3,19},{67,64},{16,32... | collective-permute-start | bytes 1572872 | tf_op jit(solution)/shard_map/ppermute | solution.py:54
  79.5 0.1 fusion.19
  79.6 0.4 collective-permute-done.9.refs_2_
  80.0 5.6 %collective-permute-done.11.refs_5_ = bf16[2,2,16,4096]{3,2,1,0:T(8,128)(2,1)S(1)} collective-permute-done((bf16[2,2,16,4096]{3,2,1,0:T(8,128)(2,1)S(1)}, bf16[2,2,16,4096]{3,2,1,0:T(8,128)(2,1)S(1)}, u32[]{:S(2)}, u32[]{:S(2)}) %collective-permute-start.11) | collective-permute-done | bytes 524320 | tf_op jit(solution)/shard_map/ppermute | solution.py:58
  85.6 1.8 %collective-permute-done.8.refs_1_ = bf16[2,2,16,4096]{3,2,1,0:T(8,128)(2,1)S(1)} collective-permute-done((bf16[2,2,16,4096]{3,2,1,0:T(8,128)(2,1)S(1)}, bf16[2,2,16,4096]{3,2,1,0:T(8,128)(2,1)S(1)}, u32[]{:S(2)}, u32[]{:S(2)}) %collective-permute-start.8) | collective-permute-done | bytes 524320 | tf_op jit(solution)/shard_map/ppermute | solution.py:54
  87.5 0.4 shard_map.81
  87.8 0.1 pad_maximum_fusion
  87.9 12.9 %all_to_all.27 = bf16[4,2,16,4096]{3,2,1,0:T(8,128)(2,1)S(1)} all-to-all(bf16[4,2,16,4096]{3,2,1,0:T(8,128)(2,1)S(1)} %pad_maximum_fusion), channel_id=1, replica_groups={{0,1,2,3},{16,17,18,19},{32,33,34,35},{48,49,50,51},{4,5,6,7},{20,21,22..., dimensions={0} | all-to-all | bytes 2097152 | tf_op jit(solution)/shard_map/all_to_all | solution.py:38
  100.8 0.2 reduce_sum.34
  101.1 0.3 copy.17
  101.3 0.2 copy.18
  101.6 9.4 %all_to_all.28 = bf16[4,2,4,4096]{3,2,1,0:T(4,128)(2,1)S(1)} all-to-all(bf16[4,2,4,4096]{3,2,1,0:T(4,128)(2,1)S(1)} %copy.18), channel_id=1, replica_groups=mesh['zh'=4,'c'=2,'y'=4,'zl'=4,'x'=4] {'zl'}, dimensions={0} | all-to-all | bytes 524288 | tf_op jit(solution)/shard_map/all_to_all | solution.py:38
  111.0 0.1 reduce_sum.35
  111.1 0.8 broadcast_in_dim.11
  111.9 12.1 %all-to-all-start.4 = ((bf16[4,2,4,4096]{3,2,1,0:T(4,128)(2,1)}), bf16[4,2,4,4096]{3,2,1,0:T(4,128)(2,1)S(1)}, u32[]{:S(2)}, u32[]{:S(2)}) async-start(bf16[4,2,4,4096]{3,2,1,0:T(4,128)(2,1)} %broadcast_in_dim.11), calls=%async_computation.4 | async-start | bytes 524288 | tf_op jit(solution)/shard_map/all_to_all | solution.py:34
  124.0 0.6 copy-done.5
  124.7 12.3 %all-to-all-done.4 = bf16[4,2,4,4096]{3,2,1,0:T(4,128)(2,1)S(1)} async-done(((bf16[4,2,4,4096]{3,2,1,0:T(4,128)(2,1)}), bf16[4,2,4,4096]{3,2,1,0:T(4,128)(2,1)S(1)}, u32[]{:S(2)}, u32[]{:S(2)}) %all-to-all-start.4) | async-done | bytes 262176 | tf_op jit(solution)/shard_map/all_to_all | solution.py:34
  137.0 15.4 %collective-permute-start.12 = (bf16[4,2,4,4096]{3,2,1,0:T(4,128)(2,1)S(1)}, bf16[4,2,4,4096]{3,2,1,0:T(4,128)(2,1)S(1)}, u32[]{:S(2)}, u32[]{:S(2)}) collective-permute-start(bf16[4,2,4,4096]{3,2,1,0:T(4,128)(2,1)S(1)} %all-to-all-done.4), channel_id=1, source_target_pairs={{0,64},{64,0},{1,65},{65,1},{2,66},{66,2},{3,67},{67,3},{4,68},{68... | collective-permute-start | bytes 786440 | tf_op jit(solution)/shard_map/ppermute | solution.py:185
  152.4 0.1 fusion.21
  152.5 1.0 collective-permute-done.12
  153.5 0.1 fusion.22
  153.7 0.9 convolution_convert_fusion
  154.6 0.9 convolution_convert_fusion.1
  (30 shorter events, 0.5 us)
Async XLA Ops:
  0.6 1.6 %copy-start = (bf16[16,4096]{1,0:T(8,128)(2,1)S(1)}, bf16[16,4096]{1,0:T(8,128)(2,1)}, u32[]{:S(2)}) copy-start(bf16[16,4096]{1,0:T(8,128)(2,1)} %param.6) | copy-start | bytes 393220
  0.6 1.7 %copy-start.4 = (bf16[16,4096]{1,0:T(8,128)(2,1)S(1)}, bf16[16,4096]{1,0:T(8,128)(2,1)}, u32[]{:S(2)}) copy-start(bf16[16,4096]{1,0:T(8,128)(2,1)} %param.7) | copy-start | bytes 393220
  15.4 39.8 %copy-start.3 = (bf16[1,128,4096]{2,1,0:T(8,128)(2,1)S(1)}, bf16[1,128,4096]{2,1,0:T(8,128)(2,1)}, u32[]{:S(2)}) copy-start(bf16[1,128,4096]{2,1,0:T(8,128)(2,1)} %param.11) | copy-start | bytes 3145732
  30.5 24.7 %copy-start.1 = (bf16[1,4096,128]{2,1,0:T(8,128)(2,1)S(1)}, bf16[1,4096,128]{2,1,0:T(8,128)(2,1)}, u32[]{:S(2)}) copy-start(bf16[1,4096,128]{2,1,0:T(8,128)(2,1)} %param.9) | copy-start | bytes 3145732
  30.5 24.7 %copy-start.2 = (bf16[1,4096,128]{2,1,0:T(8,128)(2,1)S(1)}, bf16[1,4096,128]{2,1,0:T(8,128)(2,1)}, u32[]{:S(2)}) copy-start(bf16[1,4096,128]{2,1,0:T(8,128)(2,1)} %param.10) | copy-start | bytes 3145732
  30.6 11.6 %collective-permute-start = (bf16[2,2,16,4096]{3,2,1,0:T(8,128)(2,1)S(1)}, bf16[2,2,16,4096]{3,2,1,0:T(8,128)(2,1)S(1)}, u32[]{:S(2)}, u32[]{:S(2)}) collective-permute-start(bf16[2,2,16,4096]{3,2,1,0:T(8,128)(2,1)S(1)} %get-tuple-element.25), channel_id=1, source_target_pairs={{0,16},{64,65},{1,17},{65,66},{2,18},{66,67},{3,19},{67,64},{16,32... | collective-permute-start | bytes 1572872 | tf_op jit(solution)/shard_map/ppermute | solution.py:54
  33.6 10.5 %collective-permute-start.3 = (bf16[2,2,16,4096]{3,2,1,0:T(8,128)(2,1)S(1)}, bf16[2,2,16,4096]{3,2,1,0:T(8,128)(2,1)S(1)}, u32[]{:S(2)}, u32[]{:S(2)}) collective-permute-start(bf16[2,2,16,4096]{3,2,1,0:T(8,128)(2,1)S(1)} %get-tuple-element.24), channel_id=1, source_target_pairs={{0,48},{64,67},{1,49},{65,64},{2,50},{66,65},{3,51},{67,66},{16,0}... | collective-permute-start | bytes 1572872 | tf_op jit(solution)/shard_map/ppermute | solution.py:58
  42.2 13.0 %collective-permute-start.4 = (bf16[2,2,16,4096]{3,2,1,0:T(8,128)(2,1)S(1)}, bf16[2,2,16,4096]{3,2,1,0:T(8,128)(2,1)S(1)}, u32[]{:S(2)}, u32[]{:S(2)}) collective-permute-start(bf16[2,2,16,4096]{3,2,1,0:T(8,128)(2,1)S(1)} %collective-permute-done.refs_0_), channel_id=1, source_target_pairs={{0,16},{64,65},{1,17},{65,66},{2,18},{66,67},{3,19},{67,64},{16,32... | collective-permute-start | bytes 1572872 | tf_op jit(solution)/shard_map/ppermute | solution.py:54
  44.1 11.1 %collective-permute-start.5 = (bf16[2,2,16,4096]{3,2,1,0:T(8,128)(2,1)S(1)}, bf16[2,2,16,4096]{3,2,1,0:T(8,128)(2,1)S(1)}, u32[]{:S(2)}, u32[]{:S(2)}) collective-permute-start(bf16[2,2,16,4096]{3,2,1,0:T(8,128)(2,1)S(1)} %collective-permute-done.3.refs_3_), channel_id=1, source_target_pairs={{0,48},{64,67},{1,49},{65,64},{2,50},{66,65},{3,51},{67,66},{16,0}... | collective-permute-start | bytes 1572872 | tf_op jit(solution)/shard_map/ppermute | solution.py:58
  48.7 16.9 %collective-permute-start.1 = (bf16[2,2,16,4096]{3,2,1,0:T(8,128)(2,1)S(1)}, bf16[2,2,16,4096]{3,2,1,0:T(8,128)(2,1)S(1)}, u32[]{:S(2)}, u32[]{:S(2)}) collective-permute-start(bf16[2,2,16,4096]{3,2,1,0:T(8,128)(2,1)S(1)} %get-tuple-element.24), channel_id=1, source_target_pairs={{0,16},{64,65},{1,17},{65,66},{2,18},{66,67},{3,19},{67,64},{16,32... | collective-permute-start | bytes 1572872 | tf_op jit(solution)/shard_map/ppermute | solution.py:54
  50.6 15.0 %collective-permute-start.2 = (bf16[2,2,16,4096]{3,2,1,0:T(8,128)(2,1)S(1)}, bf16[2,2,16,4096]{3,2,1,0:T(8,128)(2,1)S(1)}, u32[]{:S(2)}, u32[]{:S(2)}) collective-permute-start(bf16[2,2,16,4096]{3,2,1,0:T(8,128)(2,1)S(1)} %get-tuple-element.25), channel_id=1, source_target_pairs={{0,48},{64,67},{1,49},{65,64},{2,50},{66,65},{3,51},{67,66},{16,0}... | collective-permute-start | bytes 1572872 | tf_op jit(solution)/shard_map/ppermute | solution.py:58
  57.0 16.9 %collective-permute-start.6 = (bf16[2,2,16,4096]{3,2,1,0:T(8,128)(2,1)S(1)}, bf16[2,2,16,4096]{3,2,1,0:T(8,128)(2,1)S(1)}, u32[]{:S(2)}, u32[]{:S(2)}) collective-permute-start(bf16[2,2,16,4096]{3,2,1,0:T(8,128)(2,1)S(1)} %get-tuple-element.13), channel_id=1, source_target_pairs={{0,16},{64,65},{1,17},{65,66},{2,18},{66,67},{3,19},{67,64},{16,32... | collective-permute-start | bytes 1572872 | tf_op jit(solution)/shard_map/ppermute | solution.py:54
  58.9 15.0 %collective-permute-start.7 = (bf16[2,2,16,4096]{3,2,1,0:T(8,128)(2,1)S(1)}, bf16[2,2,16,4096]{3,2,1,0:T(8,128)(2,1)S(1)}, u32[]{:S(2)}, u32[]{:S(2)}) collective-permute-start(bf16[2,2,16,4096]{3,2,1,0:T(8,128)(2,1)S(1)} %get-tuple-element.15), channel_id=1, source_target_pairs={{0,48},{64,67},{1,49},{65,64},{2,50},{66,65},{3,51},{67,66},{16,0}... | collective-permute-start | bytes 1572872 | tf_op jit(solution)/shard_map/ppermute | solution.py:58
  67.4 12.2 %collective-permute-start.10 = (bf16[2,2,16,4096]{3,2,1,0:T(8,128)(2,1)S(1)}, bf16[2,2,16,4096]{3,2,1,0:T(8,128)(2,1)S(1)}, u32[]{:S(2)}, u32[]{:S(2)}) collective-permute-start(bf16[2,2,16,4096]{3,2,1,0:T(8,128)(2,1)S(1)} %get-tuple-element.18), channel_id=1, source_target_pairs={{0,16},{64,65},{1,17},{65,66},{2,18},{66,67},{3,19},{67,64},{16,32... | collective-permute-start | bytes 1572872 | tf_op jit(solution)/shard_map/ppermute | solution.py:54
  69.3 10.7 %collective-permute-start.9 = (bf16[2,2,16,4096]{3,2,1,0:T(8,128)(2,1)S(1)}, bf16[2,2,16,4096]{3,2,1,0:T(8,128)(2,1)S(1)}, u32[]{:S(2)}, u32[]{:S(2)}) collective-permute-start(bf16[2,2,16,4096]{3,2,1,0:T(8,128)(2,1)S(1)} %get-tuple-element.17), channel_id=1, source_target_pairs={{0,48},{64,67},{1,49},{65,64},{2,50},{66,65},{3,51},{67,66},{16,0}... | collective-permute-start | bytes 1572872 | tf_op jit(solution)/shard_map/ppermute | solution.py:58
  74.2 11.5 %collective-permute-start.11 = (bf16[2,2,16,4096]{3,2,1,0:T(8,128)(2,1)S(1)}, bf16[2,2,16,4096]{3,2,1,0:T(8,128)(2,1)S(1)}, u32[]{:S(2)}, u32[]{:S(2)}) collective-permute-start(bf16[2,2,16,4096]{3,2,1,0:T(8,128)(2,1)S(1)} %get-tuple-element.19), channel_id=1, source_target_pairs={{0,48},{64,67},{1,49},{65,64},{2,50},{66,65},{3,51},{67,66},{16,0}... | collective-permute-start | bytes 1572872 | tf_op jit(solution)/shard_map/ppermute | solution.py:58
  76.3 11.1 %collective-permute-start.8 = (bf16[2,2,16,4096]{3,2,1,0:T(8,128)(2,1)S(1)}, bf16[2,2,16,4096]{3,2,1,0:T(8,128)(2,1)S(1)}, u32[]{:S(2)}, u32[]{:S(2)}) collective-permute-start(bf16[2,2,16,4096]{3,2,1,0:T(8,128)(2,1)S(1)} %get-tuple-element.16), channel_id=1, source_target_pairs={{0,16},{64,65},{1,17},{65,66},{2,18},{66,67},{3,19},{67,64},{16,32... | collective-permute-start | bytes 1572872 | tf_op jit(solution)/shard_map/ppermute | solution.py:54
  111.9 25.1 %all-to-all-start.4 = ((bf16[4,2,4,4096]{3,2,1,0:T(4,128)(2,1)}), bf16[4,2,4,4096]{3,2,1,0:T(4,128)(2,1)S(1)}, u32[]{:S(2)}, u32[]{:S(2)}) async-start(bf16[4,2,4,4096]{3,2,1,0:T(4,128)(2,1)} %broadcast_in_dim.11), calls=%async_computation.4 | async-start | bytes 524288 | tf_op jit(solution)/shard_map/all_to_all | solution.py:34
  124.0 0.7 copy-start.5
  137.0 16.5 %collective-permute-start.12 = (bf16[4,2,4,4096]{3,2,1,0:T(4,128)(2,1)S(1)}, bf16[4,2,4,4096]{3,2,1,0:T(4,128)(2,1)S(1)}, u32[]{:S(2)}, u32[]{:S(2)}) collective-permute-start(bf16[4,2,4,4096]{3,2,1,0:T(4,128)(2,1)S(1)} %all-to-all-done.4), channel_id=1, source_target_pairs={{0,64},{64,0},{1,65},{65,1},{2,66},{66,2},{3,67},{67,3},{4,68},{68... | collective-permute-start | bytes 786440 | tf_op jit(solution)/shard_map/ppermute | solution.py:185

commit v3 on v2

v3 whole, which is shorter than its diff:
```python
import functools

import jax
import jax.numpy as jnp
from jax import lax
from jax.experimental import pallas as pl
from jax.experimental.pallas import tpu as pltpu
from jax.sharding import Mesh, PartitionSpec as P

SEND = 4
AXES = ("zh", "c", "y", "zl", "x")
SIZES = (4, 2, 4, 4, 4)
INSIDE = pl.BlockSpec(memory_space=pltpu.VMEM)


def device(zh, c, y, zl, x):
    return (((zh * 2 + c) * 4 + y) * 4 + zl) * 4 + x


def mixed_groups(first):
    groups = []
    for zh in range(4):
        for c in range(2):
            for zl in range(4):
                for still in range(4):
                    if (c == 0) == (first == "x"):
                        groups.append([device(zh, c, still, zl, k) for k in range(4)])
                    else:
                        groups.append([device(zh, c, k, zl, still) for k in range(4)])
    return groups


def along(step):
    pairs = []
    for zh in range(4):
        for zl in range(4):
            for y in range(4):
                for x in range(4):
                    pairs.append((device(zh, 0, y, zl, x), device(zh, 0, (y + step) % 4, zl, x)))
                    pairs.append((device(zh, 1, y, zl, x), device(zh, 1, y, zl, (x + step) % 4)))
    return pairs


def right(block):
    return lax.ppermute(block, AXES, along(1))


def left(block):
    return lax.ppermute(block, AXES, along(3))


def block_kernel(number, *refs):
    ins, (wg_ref, wu_ref, wd_ref), outs = refs[:number], refs[number : number + 3], refs[number + 3 :]
    width, hidden = wg_ref.shape
    chunk = 1024
    deep = ins[0].shape[0] * 16
    gu = dh = None
    for k in range(0, width, chunk):
        tok = jnp.concatenate([r[:, 0, :, k : k + chunk].reshape(deep, chunk) for r in ins])
        cot = jnp.concatenate([r[:, 1, :, k : k + chunk].reshape(deep, chunk) for r in ins])
        both = jnp.concatenate([wg_ref[k : k + chunk, :], wu_ref[k : k + chunk, :]], axis=1)
        one = jnp.dot(tok, both, preferred_element_type=jnp.float32)
        two = lax.dot_general(
            cot,
            wd_ref[:, k : k + chunk],
            (((1,), (1,)), ((), ())),
            preferred_element_type=jnp.float32,
        )
        gu, dh = (one, two) if gu is None else (gu + one, dh + two)
    gate, upper = gu[:, :hidden], gu[:, hidden:]
    s = jax.nn.sigmoid(gate)
    hid = (gate * s * upper).astype(jnp.bfloat16)
    dgate = (dh * upper * s * (1.0 + gate * (1.0 - s))).astype(jnp.bfloat16)
    dup = (dh * gate * s).astype(jnp.bfloat16)
    dgu = jnp.concatenate([dgate, dup], axis=1)
    for k in range(0, width, chunk):
        both = jnp.concatenate([wg_ref[k : k + chunk, :], wu_ref[k : k + chunk, :]], axis=1)
        out = jnp.dot(hid, wd_ref[:, k : k + chunk], preferred_element_type=jnp.float32)
        din = lax.dot_general(
            dgu, both, (((1,), (1,)), ((), ())), preferred_element_type=jnp.float32
        )
        part = outs[0].shape[0] * 16
        for i, ref in enumerate(outs):
            rows = slice(i * part, (i + 1) * part)
            ref[:, 0, :, k : k + chunk] = out[rows].astype(jnp.bfloat16).reshape(-1, 16, chunk)
            ref[:, 1, :, k : k + chunk] = din[rows].astype(jnp.bfloat16).reshape(-1, 16, chunk)


def experts(blocks, weights):
    number = len(blocks)
    width, hidden = weights[0].shape
    count = number * blocks[0].shape[0] * 16
    return pl.pallas_call(
        functools.partial(block_kernel, number),
        in_specs=[INSIDE] * (number + 3),
        out_specs=[INSIDE] * (count // 32),
        out_shape=[jax.ShapeDtypeStruct((2,) + blocks[0].shape[1:], jnp.bfloat16)] * (count // 32),
        compiler_params=pltpu.CompilerParams(vmem_limit_bytes=24 << 20),
        cost_estimate=pl.CostEstimate(
            flops=12 * count * width * hidden,
            bytes_accessed=(3 << 20) + 4 * count * width * 2,
            transcendentals=count * hidden,
        ),
    )(*blocks, *weights)


def add_kernel(groups, *refs):
    ins, outs = refs[: sum(groups)], refs[sum(groups) :]
    at = 0
    for number, out in zip(groups, outs):
        total = ins[at][...].astype(jnp.float32)
        for ref in ins[at + 1 : at + number]:
            total += ref[...].astype(jnp.float32)
        out[...] = total.astype(out.dtype)
        at += number


def added(*groups):
    flat = [block for *group, _ in groups for block in group]
    size = sum(block.size for block in flat)
    return pl.pallas_call(
        functools.partial(add_kernel, [len(group) - 1 for group in groups]),
        in_specs=[INSIDE] * len(flat),
        out_specs=[INSIDE] * len(groups),
        out_shape=[jax.ShapeDtypeStruct(group[0].shape, group[-1]) for group in groups],
        compiler_params=pltpu.CompilerParams(vmem_limit_bytes=24 << 20),
        cost_estimate=pl.CostEstimate(flops=size, bytes_accessed=3 * size, transcendentals=0),
    )(*flat)


def join_kernel(*refs):
    ins, out = refs[:-1], refs[-1]
    half = ins[0].shape[0]
    for k in range(2):
        total = ins[2 * k][...].astype(jnp.float32) + ins[2 * k + 1][...].astype(jnp.float32)
        out[k * half : (k + 1) * half] = total.astype(out.dtype)


def light_kernel(got_ref, out_ref):
    for i in range(2):
        total = got_ref[0, i].astype(jnp.float32)
        for k in range(1, 4):
            total += got_ref[k, i].astype(jnp.float32)
        for z in range(4):
            out_ref[z, i] = total[4 * z : 4 * z + 4].astype(jnp.bfloat16)


def last_kernel(got_ref, out_ref):
    for i in range(2):
        total = got_ref[0, i].astype(jnp.float32)
        for k in range(1, 4):
            total += got_ref[k, i].astype(jnp.float32)
        out_ref[i] = total.astype(jnp.bfloat16)


def widen_kernel(got_ref, out_ref):
    for i in range(2):
        rows = jnp.concatenate([got_ref[z, i].astype(jnp.float32) for z in range(4)])
        rows = rows.astype(jnp.bfloat16)
        for k in range(4):
            out_ref[k, i] = rows


def columns_of(row):
    count = row.shape[1]
    at = lax.broadcasted_iota(jnp.int32, (count, count), 0)
    to = lax.broadcasted_iota(jnp.int32, (count, count), 1)
    return jnp.sum(jnp.where(at == to, row, 0), axis=1, keepdims=True)


def pick_kernel(id_ref, tokens_ref, grads_ref, out_ref):
    expert = lax.axis_index("zh") * 2 + lax.axis_index("c")
    row = id_ref[...]
    count = row.shape[1]
    at = lax.broadcasted_iota(jnp.int32, (count, count), 0)
    to = lax.broadcasted_iota(jnp.int32, (count, count), 1)
    same = (columns_of(row) == row) & (at < to)
    slot = jnp.sum(same.astype(jnp.int32), axis=0, keepdims=True)
    place = jnp.where(row == expert, slot, -1)
    wanted = lax.broadcasted_iota(jnp.int32, (8, count), 0)
    table = (wanted == place).astype(jnp.float32).astype(jnp.bfloat16)
    for i, ref in enumerate((tokens_ref, grads_ref)):
        rows = jnp.dot(table, ref[...], preferred_element_type=jnp.float32)
        for k in range(4):
            out_ref[k, i] = rows[:SEND].astype(jnp.bfloat16)


def back_kernel(id_ref, got_ref, *outs):
    row = id_ref[...]
    count = row.shape[1]
    column = columns_of(row)
    at = lax.broadcasted_iota(jnp.int32, (count, count), 0)
    to = lax.broadcasted_iota(jnp.int32, (count, count), 1)
    same = (column == row) & (to < at)
    slot = jnp.sum(same.astype(jnp.int32), axis=1, keepdims=True)
    cells = got_ref.shape[0] * SEND
    place = column * SEND + slot
    table = lax.broadcasted_iota(jnp.int32, (count, cells), 1) == place
    table = table.astype(jnp.float32).astype(jnp.bfloat16)
    for i, out in enumerate(outs):
        rows = jnp.concatenate([got_ref[e, i].astype(jnp.float32) for e in range(got_ref.shape[0])])
        out[...] = jnp.dot(
            table, rows.astype(jnp.bfloat16), preferred_element_type=jnp.float32
        ).astype(jnp.bfloat16)


def small(kernel, shapes, *arrays):
    size = sum(array.size for array in arrays)
    return pl.pallas_call(
        kernel,
        in_specs=[INSIDE] * len(arrays),
        out_specs=jax.tree.map(lambda _: INSIDE, shapes),
        out_shape=jax.tree.map(lambda shape: jax.ShapeDtypeStruct(shape.shape, jnp.bfloat16), shapes),
        compiler_params=pltpu.CompilerParams(vmem_limit_bytes=24 << 20),
        cost_estimate=pl.CostEstimate(flops=size, bytes_accessed=3 * size, transcendentals=0),
    )(*arrays)


def like(*shape):
    return jax.ShapeDtypeStruct(shape, jnp.bfloat16)


def large_stage(block, weights):
    from_left, from_right = right(block), left(block)
    far_one, far_two = right(from_left[:2]), left(from_right[2:])
    own_one, own_two = experts([block], weights)
    left_one, left_two, right_one, right_two = experts([from_left, from_right], weights)
    far_one, far_two, left_one, left_two, right_one, right_two = lax.optimization_barrier(
        (far_one, far_two, left_one, left_two, right_one, right_two)
    )
    to_far_one, to_far_two = experts([far_one, far_two], weights)
    two_from_left, one_from_right = right(right_two), left(left_one)
    got_one, got_two = right(to_far_one), left(to_far_two)
    sum_one, sum_two, one, two = added(
        [right_one, got_one, jnp.bfloat16],
        [left_two, got_two, jnp.bfloat16],
        [own_one, one_from_right, jnp.float32],
        [own_two, two_from_left, jnp.float32],
    )
    one_from_left, two_from_right = right(sum_one), left(sum_two)
    return small(join_kernel, like(*block.shape), one, one_from_left, two, two_from_right)


def shards(tokens, cotangent, expert_id, gate_weight, up_weight, down_weight):
    count, width = tokens.shape
    ids = expert_id.reshape(1, count)
    first = mixed_groups("x")

    def exchange(blocks, axis, groups=None):
        return lax.all_to_all(blocks, axis, 0, 0, axis_index_groups=groups, tiled=True)

    part = exchange(small(pick_kernel, like(4, 2, SEND, width), ids, tokens, cotangent), "zl")
    part = exchange(small(widen_kernel, like(4, 2, 16, width), part), AXES, first)
    part = large_stage(part, (gate_weight[0], up_weight[0], down_weight[0]))
    part = exchange(part, AXES, first)
    part = exchange(small(light_kernel, like(4, 2, SEND, width), part), "zl")
    mine = small(last_kernel, like(2, SEND, width), part)
    every = lax.all_gather(mine, ("zh", "c"), axis=0)
    return tuple(small(back_kernel, [like(count, width)] * 2, ids, every))


def solution(mesh):
    fine = Mesh(mesh.devices.reshape(SIZES), AXES)
    tensor, expert = ("y", "zl", "x"), ("zh", "c")
    placed = (
        P(tensor, None),
        P(tensor, None),
        P(tensor),
        P(expert, None, tensor),
        P(expert, None, tensor),
        P(expert, tensor, None),
    )
    return jax.shard_map(
        shards,
        mesh=fine,
        in_specs=placed,
        out_specs=(P(tensor, None), P(tensor, None)),
        check_vma=False,
    )
```

time: 156 us -> 163 us (1.045)
  blocking collectives: 49.6 us -> 91.3 us
  starting transfers between devices: 65.6 us -> 32.5 us
  other arithmetic: 2.17 us -> 0 us
  matrix products: 2.07 us -> 0 us
    all_gather x0 -> x1, blocking collectives: none -> 41 us  [shards(): every = lax.all_gather(mine, ('zh', 'c'), axis=0)]
    ppermute x1 -> x0, starting transfers between devices: 15.4 us -> none  [shards(): other = lax.ppermute(mine, 'c', [(0, 1), (1, 0)])]
    all_to_all x1 -> x0, waiting for transfers between devices: 12.3 us -> none  [spread(): lax.all_to_all(copies, axis, 0, 0, axis_index_groups=groups, tiled=True)]
    all_to_all x1 -> x0, starting transfers between devices: 12.1 us -> none  [spread(): lax.all_to_all(copies, axis, 0, 0, axis_index_groups=groups, tiled=True)]
    ppermute x6 -> x5, waiting for transfers between devices: 6.05 us -> 14.2 us  [left(): return lax.ppermute(block, AXES, along(3))]
    ppermute x6 -> x5, waiting for transfers between devices: 6.76 us -> 13.3 us  [right(): return lax.ppermute(block, AXES, along(1))]
    ppermute x6 -> x5, starting transfers between devices: 24.4 us -> 21.3 us  [left(): return lax.ppermute(block, AXES, along(3))]
    ppermute x6 -> x5, starting transfers between devices: 13.8 us -> 11.2 us  [right(): return lax.ppermute(block, AXES, along(1))]
  transfers between devices with their start and end apart: 14 -> 10, of which waited for: 6 -> 7; matrix products, arithmetic and copies ran while one was open for 0% -> 0% of each run, Pallas kernels for 4% -> 3%
where the time goes in v3:
time: 163 us; the launch traced here: 162 us
  blocking collectives  91.3 us (56%)
  starting transfers between devices  32.5 us (20%)
  waiting for transfers between devices  27.6 us (17%)
  Pallas kernels  7.53 us (5%)
  local copies, waits for them, and re-layouts  2.54 us (2%)
    all_to_all x4, blocking collectives, exchange(): lax.all_to_all(blocks, axis, 0, 0, axis_index_groups=groups, tiled=True)  50.2 us
    all_gather x1, blocking collectives, shards(): every = lax.all_gather(mine, ('zh', 'c'), axis=0)  41 us
    ppermute x5, starting transfers between devices, left(): return lax.ppermute(block, AXES, along(3))  21.3 us
    ppermute x5, waiting for transfers between devices, left(): return lax.ppermute(block, AXES, along(3))  14.2 us
    ppermute x5, waiting for transfers between devices, right(): return lax.ppermute(block, AXES, along(1))  13.3 us
    ppermute x5, starting transfers between devices, right(): return lax.ppermute(block, AXES, along(1))  11.2 us
    pallas_call x3, Pallas kernels, experts(): pl.pallas_call(functools.partial(block_kernel, number), in_specs=[INSIDE]...  5.31 us
  transfers between devices with their start and end apart: 10, of which 7 were waited for; matrix products, arithmetic and copies ran while one was open for 0% of the time, Pallas kernels for 3%

profile of v3, /device:TPU:1, one launch (start us, length us, event | category | flops | bytes accessed | tf_op | source)
XLA Modules:
  0.0 162.3 jit_solution(9900098057396002953)
XLA Ops:
  0.6 0.0 copy-start.5
  0.6 0.6 copy-done.5
  1.3 0.0 copy-start.3
  1.3 0.9 copy-done.3
  2.2 0.0 copy-start.4
  2.2 0.9 copy-done.4
  3.1 0.3 shard_map.77
  3.4 12.2 %all_to_all.20.got_ref = bf16[4,2,4,4096]{3,2,1,0:T(4,128)(2,1)S(1)} all-to-all(bf16[4,2,4,4096]{3,2,1,0:T(4,128)(2,1)S(1)} %shard_map.77), channel_id=1, replica_groups=mesh['zh'=4,'c'=2,'y'=4,'zl'=4,'x'=4] {'zl'}, dimensions={0} | all-to-all | bytes 524288 | tf_op jit(solution)/shard_map/all_to_all | solution.py:250
  15.6 0.1 shard_map.78
  15.7 0.0 copy-start.2
  15.7 15.1 %all_to_all.21.refs_0_ = bf16[4,2,16,4096]{3,2,1,0:T(8,128)(2,1)S(1)} all-to-all(bf16[4,2,16,4096]{3,2,1,0:T(8,128)(2,1)S(1)} %shard_map.78), channel_id=1, replica_groups={{0,1,2,3},{16,17,18,19},{32,33,34,35},{48,49,50,51},{4,5,6,7},{20,21,22..., dimensions={0} | all-to-all | bytes 2097152 | tf_op jit(solution)/shard_map/all_to_all | solution.py:250
  30.8 0.0 copy-start
  30.8 0.0 copy-start.1
  30.8 4.3 %collective-permute-start.2 = (bf16[4,2,16,4096]{3,2,1,0:T(8,128)(2,1)S(1)}, bf16[4,2,16,4096]{3,2,1,0:T(8,128)(2,1)S(1)}, u32[]{:S(2)}, u32[]{:S(2)}) collective-permute-start(bf16[4,2,16,4096]{3,2,1,0:T(8,128)(2,1)S(1)} %all_to_all.21.refs_0_), channel_id=1, source_target_pairs={{0,48},{64,67},{1,49},{65,64},{2,50},{66,65},{3,51},{67,66},{16,0}... | collective-permute-start | bytes 3145736 | tf_op jit(solution)/shard_map/ppermute | solution.py:49
  35.1 1.9 %collective-permute-start = (bf16[4,2,16,4096]{3,2,1,0:T(8,128)(2,1)S(1)}, bf16[4,2,16,4096]{3,2,1,0:T(8,128)(2,1)S(1)}, u32[]{:S(2)}, u32[]{:S(2)}) collective-permute-start(bf16[4,2,16,4096]{3,2,1,0:T(8,128)(2,1)S(1)} %all_to_all.21.refs_0_), channel_id=1, source_target_pairs={{0,16},{64,65},{1,17},{65,66},{2,18},{66,67},{3,19},{67,64},{16,32... | collective-permute-start | bytes 3145736 | tf_op jit(solution)/shard_map/ppermute | solution.py:45
  37.0 9.8 %collective-permute-done.2.refs_1_ = bf16[4,2,16,4096]{3,2,1,0:T(8,128)(2,1)S(1)} collective-permute-done((bf16[4,2,16,4096]{3,2,1,0:T(8,128)(2,1)S(1)}, bf16[4,2,16,4096]{3,2,1,0:T(8,128)(2,1)S(1)}, u32[]{:S(2)}, u32[]{:S(2)}) %collective-permute-start.2) | collective-permute-done | bytes 1048608 | tf_op jit(solution)/shard_map/ppermute | solution.py:49
  46.9 5.3 %collective-permute-start.3 = (bf16[2,2,16,4096]{3,2,1,0:T(8,128)(2,1)S(1)}, bf16[2,2,16,4096]{3,2,1,0:T(8,128)(2,1)S(1)}, u32[]{:S(2)}, u32[]{:S(2)}) collective-permute-start(bf16[2,2,16,4096]{3,2,1,0:T(8,128)(2,1)S(1)} %slice.9), channel_id=1, source_target_pairs={{0,48},{64,67},{1,49},{65,64},{2,50},{66,65},{3,51},{67,66},{16,0}... | collective-permute-start | bytes 1572872 | tf_op jit(solution)/shard_map/ppermute | solution.py:49
  52.2 0.0 collective-permute-done.refs_0_
  52.2 1.9 %collective-permute-start.1 = (bf16[2,2,16,4096]{3,2,1,0:T(8,128)(2,1)S(1)}, bf16[2,2,16,4096]{3,2,1,0:T(8,128)(2,1)S(1)}, u32[]{:S(2)}, u32[]{:S(2)}) collective-permute-start(bf16[2,2,16,4096]{3,2,1,0:T(8,128)(2,1)S(1)} %slice.8), channel_id=1, source_target_pairs={{0,16},{64,65},{1,17},{65,66},{2,18},{66,67},{3,19},{67,64},{16,32... | collective-permute-start | bytes 1572872 | tf_op jit(solution)/shard_map/ppermute | solution.py:45
  54.2 0.0 copy-done.2
  54.2 0.0 copy-done
  54.2 0.0 copy-done.1
  54.2 1.8 %shard_map.79 = (bf16[2,2,16,4096]{3,2,1,0:T(8,128)(2,1)S(1)}, bf16[2,2,16,4096]{3,2,1,0:T(8,128)(2,1)S(1)}, bf16[2,2,16,4096]{3,2,1,0:T(8,128)(2,1)S(1)}, bf16[2,2,16,4096]{3,2,1,0:T(8,128)(2,1)S(1)}) custom-call(bf16[4,2,16,4096]{3,2,1,0:T(8,128)(2,1)S(1)} %collective-permute-done.refs_0_, bf16[4,2,16,4096]{3,2,1,0:T(8,128)(2,1)S(1)} %collective-permute-done.2.refs_1_, ...), custom_call_target="tpu_custom_call" | custom-call | flops 805306368 | bytes 7340032 | tf_op jit(solution)/shard_map/pallas_call | solution.py:93
  56.0 2.3 %collective-permute-done.3.refs_1_ = bf16[2,2,16,4096]{3,2,1,0:T(8,128)(2,1)S(1)} collective-permute-done((bf16[2,2,16,4096]{3,2,1,0:T(8,128)(2,1)S(1)}, bf16[2,2,16,4096]{3,2,1,0:T(8,128)(2,1)S(1)}, u32[]{:S(2)}, u32[]{:S(2)}) %collective-permute-start.3) | collective-permute-done | bytes 524320 | tf_op jit(solution)/shard_map/ppermute | solution.py:49
  58.3 5.1 %collective-permute-done.1.refs_0_ = bf16[2,2,16,4096]{3,2,1,0:T(8,128)(2,1)S(1)} collective-permute-done((bf16[2,2,16,4096]{3,2,1,0:T(8,128)(2,1)S(1)}, bf16[2,2,16,4096]{3,2,1,0:T(8,128)(2,1)S(1)}, u32[]{:S(2)}, u32[]{:S(2)}) %collective-permute-start.1) | collective-permute-done | bytes 524320 | tf_op jit(solution)/shard_map/ppermute | solution.py:45
  63.4 1.9 %collective-permute-start.6 = (bf16[2,2,16,4096]{3,2,1,0:T(8,128)(2,1)S(1)}, bf16[2,2,16,4096]{3,2,1,0:T(8,128)(2,1)S(1)}, u32[]{:S(2)}, u32[]{:S(2)}) collective-permute-start(bf16[2,2,16,4096]{3,2,1,0:T(8,128)(2,1)S(1)} %get-tuple-element.31), channel_id=1, source_target_pairs={{0,48},{64,67},{1,49},{65,64},{2,50},{66,65},{3,51},{67,66},{16,0}... | collective-permute-start | bytes 1572872 | tf_op jit(solution)/shard_map/ppermute | solution.py:49
  65.3 3.4 %collective-permute-start.7 = (bf16[2,2,16,4096]{3,2,1,0:T(8,128)(2,1)S(1)}, bf16[2,2,16,4096]{3,2,1,0:T(8,128)(2,1)S(1)}, u32[]{:S(2)}, u32[]{:S(2)}) collective-permute-start(bf16[2,2,16,4096]{3,2,1,0:T(8,128)(2,1)S(1)} %get-tuple-element.33), channel_id=1, source_target_pairs={{0,16},{64,65},{1,17},{65,66},{2,18},{66,67},{3,19},{67,64},{16,32... | collective-permute-start | bytes 1572872 | tf_op jit(solution)/shard_map/ppermute | solution.py:45
  68.7 1.8 %shard_map.80 = (bf16[2,2,16,4096]{3,2,1,0:T(8,128)(2,1)S(1)}, bf16[2,2,16,4096]{3,2,1,0:T(8,128)(2,1)S(1)}) custom-call(bf16[2,2,16,4096]{3,2,1,0:T(8,128)(2,1)S(1)} %collective-permute-done.1.refs_0_, bf16[2,2,16,4096]{3,2,1,0:T(8,128)(2,1)S(1)} %collective-permute-done.3.refs_1_, bf16[4096,128]{1,0:T(8,128)(2,1)S(1)} %bitcast.6, ...), custom_call_target="tpu_custom_call" | custom-call | flops 402653184 | bytes 5242880 | tf_op jit(solution)/shard_map/pallas_call | solution.py:93
  70.4 1.9 %collective-permute-start.4 = (bf16[2,2,16,4096]{3,2,1,0:T(8,128)(2,1)S(1)}, bf16[2,2,16,4096]{3,2,1,0:T(8,128)(2,1)S(1)}, u32[]{:S(2)}, u32[]{:S(2)}) collective-permute-start(bf16[2,2,16,4096]{3,2,1,0:T(8,128)(2,1)S(1)} %get-tuple-element.27), channel_id=1, source_target_pairs={{0,16},{64,65},{1,17},{65,66},{2,18},{66,67},{3,19},{67,64},{16,32... | collective-permute-start | bytes 1572872 | tf_op jit(solution)/shard_map/ppermute | solution.py:45
  72.4 4.6 %collective-permute-start.5 = (bf16[2,2,16,4096]{3,2,1,0:T(8,128)(2,1)S(1)}, bf16[2,2,16,4096]{3,2,1,0:T(8,128)(2,1)S(1)}, u32[]{:S(2)}, u32[]{:S(2)}) collective-permute-start(bf16[2,2,16,4096]{3,2,1,0:T(8,128)(2,1)S(1)} %get-tuple-element.29), channel_id=1, source_target_pairs={{0,48},{64,67},{1,49},{65,64},{2,50},{66,65},{3,51},{67,66},{16,0}... | collective-permute-start | bytes 1572872 | tf_op jit(solution)/shard_map/ppermute | solution.py:49
  76.9 1.8 %shard_map.81 = (bf16[2,2,16,4096]{3,2,1,0:T(8,128)(2,1)S(1)}, bf16[2,2,16,4096]{3,2,1,0:T(8,128)(2,1)S(1)}) custom-call(bf16[4,2,16,4096]{3,2,1,0:T(8,128)(2,1)S(1)} %all_to_all.21.refs_0_, bf16[4096,128]{1,0:T(8,128)(2,1)S(1)} %bitcast.7, bf16[4096,128]{1,0:T(8,128)(2,1)S(1)} %bitcast.10, bf16[128,4096]{1,0:T(8,128)(2,1)S(1)} %bitcast.13), custom_call_target="tpu_custom_call" | custom-call | flops 402653184 | bytes 5242880 | tf_op jit(solution)/shard_map/pallas_call | solution.py:93
  78.7 0.0 collective-permute-done.6.refs_5_
  78.7 0.0 collective-permute-done.7.refs_7_
  78.7 3.6 %collective-permute-done.4.refs_1_ = bf16[2,2,16,4096]{3,2,1,0:T(8,128)(2,1)S(1)} collective-permute-done((bf16[2,2,16,4096]{3,2,1,0:T(8,128)(2,1)S(1)}, bf16[2,2,16,4096]{3,2,1,0:T(8,128)(2,1)S(1)}, u32[]{:S(2)}, u32[]{:S(2)}) %collective-permute-start.4) | collective-permute-done | bytes 524320 | tf_op jit(solution)/shard_map/ppermute | solution.py:45
  82.3 0.7 collective-permute-done.5.refs_3_
  83.0 0.4 shard_map.82
  83.5 2.1 %collective-permute-start.8 = (bf16[2,2,16,4096]{3,2,1,0:T(8,128)(2,1)S(1)}, bf16[2,2,16,4096]{3,2,1,0:T(8,128)(2,1)S(1)}, u32[]{:S(2)}, u32[]{:S(2)}) collective-permute-start(bf16[2,2,16,4096]{3,2,1,0:T(8,128)(2,1)S(1)} %get-tuple-element.35), channel_id=1, source_target_pairs={{0,16},{64,65},{1,17},{65,66},{2,18},{66,67},{3,19},{67,64},{16,32... | collective-permute-start | bytes 1572872 | tf_op jit(solution)/shard_map/ppermute | solution.py:45
  85.6 5.2 %collective-permute-start.9 = (bf16[2,2,16,4096]{3,2,1,0:T(8,128)(2,1)S(1)}, bf16[2,2,16,4096]{3,2,1,0:T(8,128)(2,1)S(1)}, u32[]{:S(2)}, u32[]{:S(2)}) collective-permute-start(bf16[2,2,16,4096]{3,2,1,0:T(8,128)(2,1)S(1)} %get-tuple-element.37), channel_id=1, source_target_pairs={{0,48},{64,67},{1,49},{65,64},{2,50},{66,65},{3,51},{67,66},{16,0}... | collective-permute-start | bytes 1572872 | tf_op jit(solution)/shard_map/ppermute | solution.py:49
  90.7 4.6 %collective-permute-done.8.refs_1_ = bf16[2,2,16,4096]{3,2,1,0:T(8,128)(2,1)S(1)} collective-permute-done((bf16[2,2,16,4096]{3,2,1,0:T(8,128)(2,1)S(1)}, bf16[2,2,16,4096]{3,2,1,0:T(8,128)(2,1)S(1)}, u32[]{:S(2)}, u32[]{:S(2)}) %collective-permute-start.8) | collective-permute-done | bytes 524320 | tf_op jit(solution)/shard_map/ppermute | solution.py:45
  95.4 1.5 collective-permute-done.9.refs_3_
  96.8 0.2 shard_map.83
  97.0 13.9 %all_to_all.22.got_ref = bf16[4,2,16,4096]{3,2,1,0:T(8,128)(2,1)S(1)} all-to-all(bf16[4,2,16,4096]{3,2,1,0:T(8,128)(2,1)S(1)} %shard_map.83), channel_id=1, replica_groups={{0,1,2,3},{16,17,18,19},{32,33,34,35},{48,49,50,51},{4,5,6,7},{20,21,22..., dimensions={0} | all-to-all | bytes 2097152 | tf_op jit(solution)/shard_map/all_to_all | solution.py:250
  110.9 0.1 shard_map.84
  111.1 9.0 %all_to_all.23.got_ref = bf16[4,2,4,4096]{3,2,1,0:T(4,128)(2,1)S(1)} all-to-all(bf16[4,2,4,4096]{3,2,1,0:T(4,128)(2,1)S(1)} %shard_map.84), channel_id=1, replica_groups=mesh['zh'=4,'c'=2,'y'=4,'zl'=4,'x'=4] {'zl'}, dimensions={0} | all-to-all | bytes 524288 | tf_op jit(solution)/shard_map/all_to_all | solution.py:250
  120.1 0.1 shard_map.85
  120.2 41.0 %all-gather = bf16[16,4,4096]{2,1,0:T(4,128)(2,1)S(1)} all-gather(bf16[2,4,4096]{2,1,0:T(4,128)(2,1)S(1)} %shard_map.85), channel_id=2, replica_groups=mesh['zh'=4,'c'=2,'y'=4,'zl'=4,'x'=4] {'zh','c'}, dimensions={0}, use_global_device_ids=true | all-gather | bytes 589824 | tf_op jit(solution)/shard_map/all_gather | solution.py:258
  161.2 1.0 shard_map.86
  (2 shorter events, 0.1 us)
Async XLA Ops:
  0.6 0.7 copy-start.5
  1.3 0.9 copy-start.3
  2.2 0.9 copy-start.4
  15.7 38.5 %copy-start.2 = (bf16[1,128,4096]{2,1,0:T(8,128)(2,1)S(1)}, bf16[1,128,4096]{2,1,0:T(8,128)(2,1)}, u32[]{:S(2)}) copy-start(bf16[1,128,4096]{2,1,0:T(8,128)(2,1)} %param.11) | copy-start | bytes 3145732
  30.8 23.4 %copy-start = (bf16[1,4096,128]{2,1,0:T(8,128)(2,1)S(1)}, bf16[1,4096,128]{2,1,0:T(8,128)(2,1)}, u32[]{:S(2)}) copy-start(bf16[1,4096,128]{2,1,0:T(8,128)(2,1)} %param.9) | copy-start | bytes 3145732
  30.8 23.4 %copy-start.1 = (bf16[1,4096,128]{2,1,0:T(8,128)(2,1)S(1)}, bf16[1,4096,128]{2,1,0:T(8,128)(2,1)}, u32[]{:S(2)}) copy-start(bf16[1,4096,128]{2,1,0:T(8,128)(2,1)} %param.10) | copy-start | bytes 3145732
  30.8 16.1 %collective-permute-start.2 = (bf16[4,2,16,4096]{3,2,1,0:T(8,128)(2,1)S(1)}, bf16[4,2,16,4096]{3,2,1,0:T(8,128)(2,1)S(1)}, u32[]{:S(2)}, u32[]{:S(2)}) collective-permute-start(bf16[4,2,16,4096]{3,2,1,0:T(8,128)(2,1)S(1)} %all_to_all.21.refs_0_), channel_id=1, source_target_pairs={{0,48},{64,67},{1,49},{65,64},{2,50},{66,65},{3,51},{67,66},{16,0}... | collective-permute-start | bytes 3145736 | tf_op jit(solution)/shard_map/ppermute | solution.py:49
  35.1 17.1 %collective-permute-start = (bf16[4,2,16,4096]{3,2,1,0:T(8,128)(2,1)S(1)}, bf16[4,2,16,4096]{3,2,1,0:T(8,128)(2,1)S(1)}, u32[]{:S(2)}, u32[]{:S(2)}) collective-permute-start(bf16[4,2,16,4096]{3,2,1,0:T(8,128)(2,1)S(1)} %all_to_all.21.refs_0_), channel_id=1, source_target_pairs={{0,16},{64,65},{1,17},{65,66},{2,18},{66,67},{3,19},{67,64},{16,32... | collective-permute-start | bytes 3145736 | tf_op jit(solution)/shard_map/ppermute | solution.py:45
  46.9 11.4 %collective-permute-start.3 = (bf16[2,2,16,4096]{3,2,1,0:T(8,128)(2,1)S(1)}, bf16[2,2,16,4096]{3,2,1,0:T(8,128)(2,1)S(1)}, u32[]{:S(2)}, u32[]{:S(2)}) collective-permute-start(bf16[2,2,16,4096]{3,2,1,0:T(8,128)(2,1)S(1)} %slice.9), channel_id=1, source_target_pairs={{0,48},{64,67},{1,49},{65,64},{2,50},{66,65},{3,51},{67,66},{16,0}... | collective-permute-start | bytes 1572872 | tf_op jit(solution)/shard_map/ppermute | solution.py:49
  52.2 11.1 %collective-permute-start.1 = (bf16[2,2,16,4096]{3,2,1,0:T(8,128)(2,1)S(1)}, bf16[2,2,16,4096]{3,2,1,0:T(8,128)(2,1)S(1)}, u32[]{:S(2)}, u32[]{:S(2)}) collective-permute-start(bf16[2,2,16,4096]{3,2,1,0:T(8,128)(2,1)S(1)} %slice.8), channel_id=1, source_target_pairs={{0,16},{64,65},{1,17},{65,66},{2,18},{66,67},{3,19},{67,64},{16,32... | collective-permute-start | bytes 1572872 | tf_op jit(solution)/shard_map/ppermute | solution.py:45
  63.4 15.3 %collective-permute-start.6 = (bf16[2,2,16,4096]{3,2,1,0:T(8,128)(2,1)S(1)}, bf16[2,2,16,4096]{3,2,1,0:T(8,128)(2,1)S(1)}, u32[]{:S(2)}, u32[]{:S(2)}) collective-permute-start(bf16[2,2,16,4096]{3,2,1,0:T(8,128)(2,1)S(1)} %get-tuple-element.31), channel_id=1, source_target_pairs={{0,48},{64,67},{1,49},{65,64},{2,50},{66,65},{3,51},{67,66},{16,0}... | collective-permute-start | bytes 1572872 | tf_op jit(solution)/shard_map/ppermute | solution.py:49
  65.3 13.4 %collective-permute-start.7 = (bf16[2,2,16,4096]{3,2,1,0:T(8,128)(2,1)S(1)}, bf16[2,2,16,4096]{3,2,1,0:T(8,128)(2,1)S(1)}, u32[]{:S(2)}, u32[]{:S(2)}) collective-permute-start(bf16[2,2,16,4096]{3,2,1,0:T(8,128)(2,1)S(1)} %get-tuple-element.33), channel_id=1, source_target_pairs={{0,16},{64,65},{1,17},{65,66},{2,18},{66,67},{3,19},{67,64},{16,32... | collective-permute-start | bytes 1572872 | tf_op jit(solution)/shard_map/ppermute | solution.py:45
  70.4 11.9 %collective-permute-start.4 = (bf16[2,2,16,4096]{3,2,1,0:T(8,128)(2,1)S(1)}, bf16[2,2,16,4096]{3,2,1,0:T(8,128)(2,1)S(1)}, u32[]{:S(2)}, u32[]{:S(2)}) collective-permute-start(bf16[2,2,16,4096]{3,2,1,0:T(8,128)(2,1)S(1)} %get-tuple-element.27), channel_id=1, source_target_pairs={{0,16},{64,65},{1,17},{65,66},{2,18},{66,67},{3,19},{67,64},{16,32... | collective-permute-start | bytes 1572872 | tf_op jit(solution)/shard_map/ppermute | solution.py:45
  72.4 10.7 %collective-permute-start.5 = (bf16[2,2,16,4096]{3,2,1,0:T(8,128)(2,1)S(1)}, bf16[2,2,16,4096]{3,2,1,0:T(8,128)(2,1)S(1)}, u32[]{:S(2)}, u32[]{:S(2)}) collective-permute-start(bf16[2,2,16,4096]{3,2,1,0:T(8,128)(2,1)S(1)} %get-tuple-element.29), channel_id=1, source_target_pairs={{0,48},{64,67},{1,49},{65,64},{2,50},{66,65},{3,51},{67,66},{16,0}... | collective-permute-start | bytes 1572872 | tf_op jit(solution)/shard_map/ppermute | solution.py:49
  83.5 11.9 %collective-permute-start.8 = (bf16[2,2,16,4096]{3,2,1,0:T(8,128)(2,1)S(1)}, bf16[2,2,16,4096]{3,2,1,0:T(8,128)(2,1)S(1)}, u32[]{:S(2)}, u32[]{:S(2)}) collective-permute-start(bf16[2,2,16,4096]{3,2,1,0:T(8,128)(2,1)S(1)} %get-tuple-element.35), channel_id=1, source_target_pairs={{0,16},{64,65},{1,17},{65,66},{2,18},{66,67},{3,19},{67,64},{16,32... | collective-permute-start | bytes 1572872 | tf_op jit(solution)/shard_map/ppermute | solution.py:45
  85.6 11.3 %collective-permute-start.9 = (bf16[2,2,16,4096]{3,2,1,0:T(8,128)(2,1)S(1)}, bf16[2,2,16,4096]{3,2,1,0:T(8,128)(2,1)S(1)}, u32[]{:S(2)}, u32[]{:S(2)}) collective-permute-start(bf16[2,2,16,4096]{3,2,1,0:T(8,128)(2,1)S(1)} %get-tuple-element.37), channel_id=1, source_target_pairs={{0,48},{64,67},{1,49},{65,64},{2,50},{66,65},{3,51},{67,66},{16,0}... | collective-permute-start | bytes 1572872 | tf_op jit(solution)/shard_map/ppermute | solution.py:49

commit v4 on v3

--- a/solution.py
+++ b/solution.py
@@ -49,8 +49,9 @@
     return lax.ppermute(block, AXES, along(3))
 
 
-def block_kernel(number, *refs):
-    ins, (wg_ref, wu_ref, wd_ref), outs = refs[:number], refs[number : number + 3], refs[number + 3 :]
+def block_kernel(number, after, *refs):
+    ins, (wg_ref, wu_ref, wd_ref) = refs[:number], refs[number : number + 3]
+    outs = refs[number + 3 + after :]
     width, hidden = wg_ref.shape
     chunk = 1024
     deep = ins[0].shape[0] * 16
@@ -86,13 +87,13 @@
             ref[:, 1, :, k : k + chunk] = din[rows].astype(jnp.bfloat16).reshape(-1, 16, chunk)
 
 
-def experts(blocks, weights):
+def experts(blocks, weights, after=()):
     number = len(blocks)
     width, hidden = weights[0].shape
     count = number * blocks[0].shape[0] * 16
     return pl.pallas_call(
-        functools.partial(block_kernel, number),
-        in_specs=[INSIDE] * (number + 3),
+        functools.partial(block_kernel, number, len(after)),
+        in_specs=[INSIDE] * (number + 3) + [pl.BlockSpec(memory_space=pl.ANY)] * len(after),
         out_specs=[INSIDE] * (count // 32),
         out_shape=[jax.ShapeDtypeStruct((2,) + blocks[0].shape[1:], jnp.bfloat16)] * (count // 32),
         compiler_params=pltpu.CompilerParams(vmem_limit_bytes=24 << 20),
@@ -101,7 +102,7 @@
             bytes_accessed=(3 << 20) + 4 * count * width * 2,
             transcendentals=count * hidden,
         ),
-    )(*blocks, *weights)
+    )(*blocks, *weights, *after)
 
 
 def add_kernel(groups, *refs):
@@ -132,7 +133,9 @@
     ins, out = refs[:-1], refs[-1]
     half = ins[0].shape[0]
     for k in range(2):
-        total = ins[2 * k][...].astype(jnp.float32) + ins[2 * k + 1][...].astype(jnp.float32)
+        total = ins[3 * k][...].astype(jnp.float32)
+        for ref in ins[3 * k + 1 : 3 * k + 3]:
+            total += ref[...].astype(jnp.float32)
         out[k * half : (k + 1) * half] = total.astype(out.dtype)
 
 
@@ -221,24 +224,26 @@
 
 
 def large_stage(block, weights):
-    from_left, from_right = right(block), left(block)
-    far_one, far_two = right(from_left[:2]), left(from_right[2:])
+    one, two = block[:2], block[2:]
+    from_left_one, from_right_two = right(one), left(two)
+    from_left_two, from_right_one = right(two), left(one)
+    far_one, far_two = right(from_left_one), left(from_right_two)
     own_one, own_two = experts([block], weights)
-    left_one, left_two, right_one, right_two = experts([from_left, from_right], weights)
-    far_one, far_two, left_one, left_two, right_one, right_two = lax.optimization_barrier(
-        (far_one, far_two, left_one, left_two, right_one, right_two)
-    )
-    to_far_one, to_far_two = experts([far_one, far_two], weights)
+    left_one, left_two, right_one, right_two = experts(
+        [from_left_one, from_left_two, from_right_one, from_right_two], weights
+    )
+    to_far_one, to_far_two = experts([far_one, far_two], weights, (right_two,))
     two_from_left, one_from_right = right(right_two), left(left_one)
     got_one, got_two = right(to_far_one), left(to_far_two)
-    sum_one, sum_two, one, two = added(
-        [right_one, got_one, jnp.bfloat16],
-        [left_two, got_two, jnp.bfloat16],
-        [own_one, one_from_right, jnp.float32],
-        [own_two, two_from_left, jnp.float32],
+    sum_one, sum_two = added(
+        [right_one, got_one, jnp.bfloat16], [left_two, got_two, jnp.bfloat16]
     )
     one_from_left, two_from_right = right(sum_one), left(sum_two)
-    return small(join_kernel, like(*block.shape), one, one_from_left, two, two_from_right)
+    return small(
+        join_kernel,
+        like(*block.shape),
+        own_one, one_from_left, one_from_right, own_two, two_from_left, two_from_right,
+    )
 
 
 def shards(tokens, cotangent, expert_id, gate_weight, up_weight, down_weight):
@@ -249,7 +254,19 @@
     def exchange(blocks, axis, groups=None):
         return lax.all_to_all(blocks, axis, 0, 0, axis_index_groups=groups, tiled=True)
 
-    part = exchange(small(pick_kernel, like(4, 2, SEND, width), ids, tokens, cotangent), "zl")
+    own = pl.pallas_call(
+        pick_kernel,
+        grid=(1,),
+        in_specs=[
+            pl.BlockSpec((1, count), lambda i: (0, 0)),
+            pl.BlockSpec((count, width), lambda i: (0, 0)),
+            pl.BlockSpec((count, width), lambda i: (0, 0)),
+        ],
+        out_specs=pl.BlockSpec((4, 2, SEND, width), lambda i: (0, 0, 0, 0)),
+        out_shape=like(4, 2, SEND, width),
+        compiler_params=pltpu.CompilerParams(vmem_limit_bytes=24 << 20),
+    )(ids, tokens, cotangent)
+    part = exchange(own, "zl")
     part = exchange(small(widen_kernel, like(4, 2, 16, width), part), AXES, first)
     part = large_stage(part, (gate_weight[0], up_weight[0], down_weight[0]))
     part = exchange(part, AXES, first)

time: 163 us -> 153 us (0.939)
  waiting for transfers between devices: 27.6 us -> 11.7 us
  starting transfers between devices: 32.5 us -> 40.1 us
  blocking collectives: 91.3 us -> 89.6 us
    ppermute x5 -> x6, waiting for transfers between devices: 14.2 us -> 4.05 us  [left(): return lax.ppermute(block, AXES, along(3))]
    ppermute x5 -> x6, starting transfers between devices: 21.3 us -> 27.6 us  [left(): return lax.ppermute(block, AXES, along(3))]
    ppermute x5 -> x6, waiting for transfers between devices: 13.3 us -> 7.63 us  [right(): return lax.ppermute(block, AXES, along(1))]
    ppermute x5 -> x6, starting transfers between devices: 11.2 us -> 12.6 us  [right(): return lax.ppermute(block, AXES, along(1))]
    pallas_call x3 -> x4, Pallas kernels: 5.31 us -> 5.61 us  [the longest x3 5.32 us: experts(): pl.pallas_call(functools.partial(block_kernel, number, len(after)), in_sp...]
  transfers between devices with their start and end apart: 10 -> 12, of which waited for: 7 -> 4; matrix products, arithmetic and copies ran while one was open for 0% -> 0% of each run, Pallas kernels for 3% -> 2%
where the time goes in v4:
time: 153 us; the launch traced here: 152 us
  blocking collectives  89.6 us (59%)
  starting transfers between devices  40.1 us (26%)
  waiting for transfers between devices  11.7 us (8%)
  Pallas kernels  7.54 us (5%)
  local copies, waits for them, and re-layouts  2.56 us (2%)
    all_to_all x4, blocking collectives, exchange(): lax.all_to_all(blocks, axis, 0, 0, axis_index_groups=groups, tiled=True)  49.7 us
    all_gather x1, blocking collectives, shards(): every = lax.all_gather(mine, ('zh', 'c'), axis=0)  39.9 us
    ppermute x6, starting transfers between devices, left(): return lax.ppermute(block, AXES, along(3))  27.6 us
    ppermute x6, starting transfers between devices, right(): return lax.ppermute(block, AXES, along(1))  12.6 us
    ppermute x6, waiting for transfers between devices, right(): return lax.ppermute(block, AXES, along(1))  7.63 us
    pallas_call x3, Pallas kernels, experts(): pl.pallas_call(functools.partial(block_kernel, number, len(after)), in_sp...  5.32 us
    ppermute x6, waiting for transfers between devices, left(): return lax.ppermute(block, AXES, along(3))  4.05 us
  transfers between devices with their start and end apart: 12, of which 4 were waited for; matrix products, arithmetic and copies ran while one was open for 0% of the time, Pallas kernels for 2%

profile of v4, /device:TPU:1, one launch (start us, length us, event | category | flops | bytes accessed | tf_op | source)
XLA Modules:
  0.0 152.4 jit_solution(13634902563041640594)
XLA Ops:
  0.6 0.0 copy-start.5
  0.6 0.6 copy-done.5
  1.3 0.9 copy-done.3
  2.2 0.9 copy-done.4
  3.1 0.3 shard_map.77
  3.4 12.2 %all_to_all.20.got_ref = bf16[4,2,4,4096]{3,2,1,0:T(4,128)(2,1)S(1)} all-to-all(bf16[4,2,4,4096]{3,2,1,0:T(4,128)(2,1)S(1)} %shard_map.77), channel_id=1, replica_groups=mesh['zh'=4,'c'=2,'y'=4,'zl'=4,'x'=4] {'zl'}, dimensions={0} | all-to-all | bytes 524288 | tf_op jit(solution)/shard_map/all_to_all | solution.py:255
  15.6 0.1 shard_map.78
  15.7 0.0 copy-start.2
  15.7 15.1 %all_to_all.21.refs_0_ = bf16[4,2,16,4096]{3,2,1,0:T(8,128)(2,1)S(1)} all-to-all(bf16[4,2,16,4096]{3,2,1,0:T(8,128)(2,1)S(1)} %shard_map.78), channel_id=1, replica_groups={{0,1,2,3},{16,17,18,19},{32,33,34,35},{48,49,50,51},{4,5,6,7},{20,21,22..., dimensions={0} | all-to-all | bytes 2097152 | tf_op jit(solution)/shard_map/all_to_all | solution.py:255
  30.8 0.1 fusion
  30.9 3.0 %collective-permute-start = (bf16[2,2,16,4096]{3,2,1,0:T(8,128)(2,1)S(1)}, bf16[2,2,16,4096]{3,2,1,0:T(8,128)(2,1)S(1)}, u32[]{:S(2)}, u32[]{:S(2)}) collective-permute-start(bf16[2,2,16,4096]{3,2,1,0:T(8,128)(2,1)S(1)} %get-tuple-element.23), channel_id=1, source_target_pairs={{0,16},{64,65},{1,17},{65,66},{2,18},{66,67},{3,19},{67,64},{16,32... | collective-permute-start | bytes 1572872 | tf_op jit(solution)/shard_map/ppermute | solution.py:45
  33.8 3.7 %collective-permute-start.3 = (bf16[2,2,16,4096]{3,2,1,0:T(8,128)(2,1)S(1)}, bf16[2,2,16,4096]{3,2,1,0:T(8,128)(2,1)S(1)}, u32[]{:S(2)}, u32[]{:S(2)}) collective-permute-start(bf16[2,2,16,4096]{3,2,1,0:T(8,128)(2,1)S(1)} %get-tuple-element.22), channel_id=1, source_target_pairs={{0,48},{64,67},{1,49},{65,64},{2,50},{66,65},{3,51},{67,66},{16,0}... | collective-permute-start | bytes 1572872 | tf_op jit(solution)/shard_map/ppermute | solution.py:49
  37.5 1.9 %collective-permute-start.1 = (bf16[2,2,16,4096]{3,2,1,0:T(8,128)(2,1)S(1)}, bf16[2,2,16,4096]{3,2,1,0:T(8,128)(2,1)S(1)}, u32[]{:S(2)}, u32[]{:S(2)}) collective-permute-start(bf16[2,2,16,4096]{3,2,1,0:T(8,128)(2,1)S(1)} %get-tuple-element.22), channel_id=1, source_target_pairs={{0,16},{64,65},{1,17},{65,66},{2,18},{66,67},{3,19},{67,64},{16,32... | collective-permute-start | bytes 1572872 | tf_op jit(solution)/shard_map/ppermute | solution.py:45
  39.4 4.6 %collective-permute-start.2 = (bf16[2,2,16,4096]{3,2,1,0:T(8,128)(2,1)S(1)}, bf16[2,2,16,4096]{3,2,1,0:T(8,128)(2,1)S(1)}, u32[]{:S(2)}, u32[]{:S(2)}) collective-permute-start(bf16[2,2,16,4096]{3,2,1,0:T(8,128)(2,1)S(1)} %get-tuple-element.23), channel_id=1, source_target_pairs={{0,48},{64,67},{1,49},{65,64},{2,50},{66,65},{3,51},{67,66},{16,0}... | collective-permute-start | bytes 1572872 | tf_op jit(solution)/shard_map/ppermute | solution.py:49
  44.0 0.0 collective-permute-done.refs_0_
  44.0 1.9 %collective-permute-start.4 = (bf16[2,2,16,4096]{3,2,1,0:T(8,128)(2,1)S(1)}, bf16[2,2,16,4096]{3,2,1,0:T(8,128)(2,1)S(1)}, u32[]{:S(2)}, u32[]{:S(2)}) collective-permute-start(bf16[2,2,16,4096]{3,2,1,0:T(8,128)(2,1)S(1)} %collective-permute-done.refs_0_), channel_id=1, source_target_pairs={{0,16},{64,65},{1,17},{65,66},{2,18},{66,67},{3,19},{67,64},{16,32... | collective-permute-start | bytes 1572872 | tf_op jit(solution)/shard_map/ppermute | solution.py:45
  46.0 0.0 collective-permute-done.3.refs_3_
  46.0 4.6 %collective-permute-start.5 = (bf16[2,2,16,4096]{3,2,1,0:T(8,128)(2,1)S(1)}, bf16[2,2,16,4096]{3,2,1,0:T(8,128)(2,1)S(1)}, u32[]{:S(2)}, u32[]{:S(2)}) collective-permute-start(bf16[2,2,16,4096]{3,2,1,0:T(8,128)(2,1)S(1)} %collective-permute-done.3.refs_3_), channel_id=1, source_target_pairs={{0,48},{64,67},{1,49},{65,64},{2,50},{66,65},{3,51},{67,66},{16,0}... | collective-permute-start | bytes 1572872 | tf_op jit(solution)/shard_map/ppermute | solution.py:49
  50.5 0.0 collective-permute-done.1.refs_1_
  50.6 0.0 collective-permute-done.2.refs_2_
  50.6 0.0 copy-done.2
  50.6 0.0 copy-done
  50.6 0.0 copy-done.1
  50.6 1.8 %shard_map.80 = (bf16[2,2,16,4096]{3,2,1,0:T(8,128)(2,1)S(1)}, bf16[2,2,16,4096]{3,2,1,0:T(8,128)(2,1)S(1)}, bf16[2,2,16,4096]{3,2,1,0:T(8,128)(2,1)S(1)}, bf16[2,2,16,4096]{3,2,1,0:T(8,128)(2,1)S(1)}) custom-call(bf16[2,2,16,4096]{3,2,1,0:T(8,128)(2,1)S(1)} %collective-permute-done.refs_0_, bf16[2,2,16,4096]{3,2,1,0:T(8,128)(2,1)S(1)} %collective-permute-done.1.refs_1_, ...), custom_call_target="tpu_custom_call" | custom-call | flops 805306368 | bytes 7340032 | tf_op jit(solution)/shard_map/pallas_call | solution.py:94
  52.4 3.0 %collective-permute-done.4.refs_0_ = bf16[2,2,16,4096]{3,2,1,0:T(8,128)(2,1)S(1)} collective-permute-done((bf16[2,2,16,4096]{3,2,1,0:T(8,128)(2,1)S(1)}, bf16[2,2,16,4096]{3,2,1,0:T(8,128)(2,1)S(1)}, u32[]{:S(2)}, u32[]{:S(2)}) %collective-permute-start.4) | collective-permute-done | bytes 524320 | tf_op jit(solution)/shard_map/ppermute | solution.py:45
  55.5 1.2 collective-permute-done.5.refs_1_
  56.6 1.8 %shard_map.81 = (bf16[2,2,16,4096]{3,2,1,0:T(8,128)(2,1)S(1)}, bf16[2,2,16,4096]{3,2,1,0:T(8,128)(2,1)S(1)}) custom-call(bf16[2,2,16,4096]{3,2,1,0:T(8,128)(2,1)S(1)} %collective-permute-done.4.refs_0_, bf16[2,2,16,4096]{3,2,1,0:T(8,128)(2,1)S(1)} %collective-permute-done.5.refs_1_, bf16[4096,128]{1,0:T(8,128)(2,1)S(1)} %bitcast.6, ...), custom_call_target="tpu_custom_call" | custom-call | flops 402653184 | bytes 5242880 | tf_op jit(solution)/shard_map/pallas_call | solution.py:94
  58.4 1.9 %collective-permute-start.6 = (bf16[2,2,16,4096]{3,2,1,0:T(8,128)(2,1)S(1)}, bf16[2,2,16,4096]{3,2,1,0:T(8,128)(2,1)S(1)}, u32[]{:S(2)}, u32[]{:S(2)}) collective-permute-start(bf16[2,2,16,4096]{3,2,1,0:T(8,128)(2,1)S(1)} %get-tuple-element.15), channel_id=1, source_target_pairs={{0,16},{64,65},{1,17},{65,66},{2,18},{66,67},{3,19},{67,64},{16,32... | collective-permute-start | bytes 1572872 | tf_op jit(solution)/shard_map/ppermute | solution.py:45
  60.3 5.3 %collective-permute-start.7 = (bf16[2,2,16,4096]{3,2,1,0:T(8,128)(2,1)S(1)}, bf16[2,2,16,4096]{3,2,1,0:T(8,128)(2,1)S(1)}, u32[]{:S(2)}, u32[]{:S(2)}) collective-permute-start(bf16[2,2,16,4096]{3,2,1,0:T(8,128)(2,1)S(1)} %get-tuple-element.17), channel_id=1, source_target_pairs={{0,48},{64,67},{1,49},{65,64},{2,50},{66,65},{3,51},{67,66},{16,0}... | collective-permute-start | bytes 1572872 | tf_op jit(solution)/shard_map/ppermute | solution.py:49
  65.7 1.9 %collective-permute-start.10 = (bf16[2,2,16,4096]{3,2,1,0:T(8,128)(2,1)S(1)}, bf16[2,2,16,4096]{3,2,1,0:T(8,128)(2,1)S(1)}, u32[]{:S(2)}, u32[]{:S(2)}) collective-permute-start(bf16[2,2,16,4096]{3,2,1,0:T(8,128)(2,1)S(1)} %get-tuple-element.14.refs_5_), channel_id=1, source_target_pairs={{0,16},{64,65},{1,17},{65,66},{2,18},{66,67},{3,19},{67,64},{16,32... | collective-permute-start | bytes 1572872 | tf_op jit(solution)/shard_map/ppermute | solution.py:45
  67.6 4.6 %collective-permute-start.9 = (bf16[2,2,16,4096]{3,2,1,0:T(8,128)(2,1)S(1)}, bf16[2,2,16,4096]{3,2,1,0:T(8,128)(2,1)S(1)}, u32[]{:S(2)}, u32[]{:S(2)}) collective-permute-start(bf16[2,2,16,4096]{3,2,1,0:T(8,128)(2,1)S(1)} %get-tuple-element.19), channel_id=1, source_target_pairs={{0,48},{64,67},{1,49},{65,64},{2,50},{66,65},{3,51},{67,66},{16,0}... | collective-permute-start | bytes 1572872 | tf_op jit(solution)/shard_map/ppermute | solution.py:49
  72.2 0.0 collective-permute-done.6.refs_1_
  72.2 0.0 collective-permute-done.7.refs_3_
  72.2 0.2 shard_map.82
  72.4 4.9 %collective-permute-start.11 = (bf16[2,2,16,4096]{3,2,1,0:T(8,128)(2,1)S(1)}, bf16[2,2,16,4096]{3,2,1,0:T(8,128)(2,1)S(1)}, u32[]{:S(2)}, u32[]{:S(2)}) collective-permute-start(bf16[2,2,16,4096]{3,2,1,0:T(8,128)(2,1)S(1)} %get-tuple-element.21), channel_id=1, source_target_pairs={{0,48},{64,67},{1,49},{65,64},{2,50},{66,65},{3,51},{67,66},{16,0}... | collective-permute-start | bytes 1572872 | tf_op jit(solution)/shard_map/ppermute | solution.py:49
  77.3 1.9 %collective-permute-start.8 = (bf16[2,2,16,4096]{3,2,1,0:T(8,128)(2,1)S(1)}, bf16[2,2,16,4096]{3,2,1,0:T(8,128)(2,1)S(1)}, u32[]{:S(2)}, u32[]{:S(2)}) collective-permute-start(bf16[2,2,16,4096]{3,2,1,0:T(8,128)(2,1)S(1)} %get-tuple-element.18), channel_id=1, source_target_pairs={{0,16},{64,65},{1,17},{65,66},{2,18},{66,67},{3,19},{67,64},{16,32... | collective-permute-start | bytes 1572872 | tf_op jit(solution)/shard_map/ppermute | solution.py:45
  79.3 1.8 %shard_map.79 = (bf16[2,2,16,4096]{3,2,1,0:T(8,128)(2,1)S(1)}, bf16[2,2,16,4096]{3,2,1,0:T(8,128)(2,1)S(1)}) custom-call(bf16[4,2,16,4096]{3,2,1,0:T(8,128)(2,1)S(1)} %all_to_all.21.refs_0_, bf16[4096,128]{1,0:T(8,128)(2,1)S(1)} %bitcast.7, bf16[4096,128]{1,0:T(8,128)(2,1)S(1)} %bitcast.10, bf16[128,4096]{1,0:T(8,128)(2,1)S(1)} %bitcast.13), custom_call_target="tpu_custom_call" | custom-call | flops 402653184 | bytes 5242880 | tf_op jit(solution)/shard_map/pallas_call | solution.py:94
  81.0 0.0 collective-permute-done.10.refs_4_
  81.0 0.0 collective-permute-done.9.refs_2_
  81.0 2.8 %collective-permute-done.11.refs_5_ = bf16[2,2,16,4096]{3,2,1,0:T(8,128)(2,1)S(1)} collective-permute-done((bf16[2,2,16,4096]{3,2,1,0:T(8,128)(2,1)S(1)}, bf16[2,2,16,4096]{3,2,1,0:T(8,128)(2,1)S(1)}, u32[]{:S(2)}, u32[]{:S(2)}) %collective-permute-start.11) | collective-permute-done | bytes 524320 | tf_op jit(solution)/shard_map/ppermute | solution.py:49
  83.9 4.6 %collective-permute-done.8.refs_1_ = bf16[2,2,16,4096]{3,2,1,0:T(8,128)(2,1)S(1)} collective-permute-done((bf16[2,2,16,4096]{3,2,1,0:T(8,128)(2,1)S(1)}, bf16[2,2,16,4096]{3,2,1,0:T(8,128)(2,1)S(1)}, u32[]{:S(2)}, u32[]{:S(2)}) %collective-permute-start.8) | collective-permute-done | bytes 524320 | tf_op jit(solution)/shard_map/ppermute | solution.py:45
  88.5 0.4 shard_map.83
  88.8 13.0 %all_to_all.22.got_ref = bf16[4,2,16,4096]{3,2,1,0:T(8,128)(2,1)S(1)} all-to-all(bf16[4,2,16,4096]{3,2,1,0:T(8,128)(2,1)S(1)} %shard_map.83), channel_id=1, replica_groups={{0,1,2,3},{16,17,18,19},{32,33,34,35},{48,49,50,51},{4,5,6,7},{20,21,22..., dimensions={0} | all-to-all | bytes 2097152 | tf_op jit(solution)/shard_map/all_to_all | solution.py:255
  101.9 0.1 shard_map.84
  102.0 9.5 %all_to_all.23.got_ref = bf16[4,2,4,4096]{3,2,1,0:T(4,128)(2,1)S(1)} all-to-all(bf16[4,2,4,4096]{3,2,1,0:T(4,128)(2,1)S(1)} %shard_map.84), channel_id=1, replica_groups=mesh['zh'=4,'c'=2,'y'=4,'zl'=4,'x'=4] {'zl'}, dimensions={0} | all-to-all | bytes 524288 | tf_op jit(solution)/shard_map/all_to_all | solution.py:255
  111.5 0.1 shard_map.85
  111.5 39.9 %all-gather = bf16[16,4,4096]{2,1,0:T(4,128)(2,1)S(1)} all-gather(bf16[2,4,4096]{2,1,0:T(4,128)(2,1)S(1)} %shard_map.85), channel_id=2, replica_groups=mesh['zh'=4,'c'=2,'y'=4,'zl'=4,'x'=4] {'zh','c'}, dimensions={0}, use_global_device_ids=true | all-gather | bytes 589824 | tf_op jit(solution)/shard_map/all_gather | solution.py:275
  151.4 1.0 shard_map.86
  (4 shorter events, 0.0 us)
Async XLA Ops:
  0.6 0.7 copy-start.5
  1.3 0.9 copy-start.3
  2.2 0.9 copy-start.4
  15.7 34.9 %copy-start.2 = (bf16[1,128,4096]{2,1,0:T(8,128)(2,1)S(1)}, bf16[1,128,4096]{2,1,0:T(8,128)(2,1)}, u32[]{:S(2)}) copy-start(bf16[1,128,4096]{2,1,0:T(8,128)(2,1)} %param.11) | copy-start | bytes 3145732
  30.8 19.8 %copy-start = (bf16[1,4096,128]{2,1,0:T(8,128)(2,1)S(1)}, bf16[1,4096,128]{2,1,0:T(8,128)(2,1)}, u32[]{:S(2)}) copy-start(bf16[1,4096,128]{2,1,0:T(8,128)(2,1)} %param.9) | copy-start | bytes 3145732
  30.8 19.8 %copy-start.1 = (bf16[1,4096,128]{2,1,0:T(8,128)(2,1)S(1)}, bf16[1,4096,128]{2,1,0:T(8,128)(2,1)}, u32[]{:S(2)}) copy-start(bf16[1,4096,128]{2,1,0:T(8,128)(2,1)} %param.10) | copy-start | bytes 3145732
  30.9 13.2 %collective-permute-start = (bf16[2,2,16,4096]{3,2,1,0:T(8,128)(2,1)S(1)}, bf16[2,2,16,4096]{3,2,1,0:T(8,128)(2,1)S(1)}, u32[]{:S(2)}, u32[]{:S(2)}) collective-permute-start(bf16[2,2,16,4096]{3,2,1,0:T(8,128)(2,1)S(1)} %get-tuple-element.23), channel_id=1, source_target_pairs={{0,16},{64,65},{1,17},{65,66},{2,18},{66,67},{3,19},{67,64},{16,32... | collective-permute-start | bytes 1572872 | tf_op jit(solution)/shard_map/ppermute | solution.py:45
  33.8 12.1 %collective-permute-start.3 = (bf16[2,2,16,4096]{3,2,1,0:T(8,128)(2,1)S(1)}, bf16[2,2,16,4096]{3,2,1,0:T(8,128)(2,1)S(1)}, u32[]{:S(2)}, u32[]{:S(2)}) collective-permute-start(bf16[2,2,16,4096]{3,2,1,0:T(8,128)(2,1)S(1)} %get-tuple-element.22), channel_id=1, source_target_pairs={{0,48},{64,67},{1,49},{65,64},{2,50},{66,65},{3,51},{67,66},{16,0}... | collective-permute-start | bytes 1572872 | tf_op jit(solution)/shard_map/ppermute | solution.py:49
  37.5 13.0 %collective-permute-start.1 = (bf16[2,2,16,4096]{3,2,1,0:T(8,128)(2,1)S(1)}, bf16[2,2,16,4096]{3,2,1,0:T(8,128)(2,1)S(1)}, u32[]{:S(2)}, u32[]{:S(2)}) collective-permute-start(bf16[2,2,16,4096]{3,2,1,0:T(8,128)(2,1)S(1)} %get-tuple-element.22), channel_id=1, source_target_pairs={{0,16},{64,65},{1,17},{65,66},{2,18},{66,67},{3,19},{67,64},{16,32... | collective-permute-start | bytes 1572872 | tf_op jit(solution)/shard_map/ppermute | solution.py:45
  39.4 11.1 %collective-permute-start.2 = (bf16[2,2,16,4096]{3,2,1,0:T(8,128)(2,1)S(1)}, bf16[2,2,16,4096]{3,2,1,0:T(8,128)(2,1)S(1)}, u32[]{:S(2)}, u32[]{:S(2)}) collective-permute-start(bf16[2,2,16,4096]{3,2,1,0:T(8,128)(2,1)S(1)} %get-tuple-element.23), channel_id=1, source_target_pairs={{0,48},{64,67},{1,49},{65,64},{2,50},{66,65},{3,51},{67,66},{16,0}... | collective-permute-start | bytes 1572872 | tf_op jit(solution)/shard_map/ppermute | solution.py:49
  44.0 11.4 %collective-permute-start.4 = (bf16[2,2,16,4096]{3,2,1,0:T(8,128)(2,1)S(1)}, bf16[2,2,16,4096]{3,2,1,0:T(8,128)(2,1)S(1)}, u32[]{:S(2)}, u32[]{:S(2)}) collective-permute-start(bf16[2,2,16,4096]{3,2,1,0:T(8,128)(2,1)S(1)} %collective-permute-done.refs_0_), channel_id=1, source_target_pairs={{0,16},{64,65},{1,17},{65,66},{2,18},{66,67},{3,19},{67,64},{16,32... | collective-permute-start | bytes 1572872 | tf_op jit(solution)/shard_map/ppermute | solution.py:45
  46.0 10.7 %collective-permute-start.5 = (bf16[2,2,16,4096]{3,2,1,0:T(8,128)(2,1)S(1)}, bf16[2,2,16,4096]{3,2,1,0:T(8,128)(2,1)S(1)}, u32[]{:S(2)}, u32[]{:S(2)}) collective-permute-start(bf16[2,2,16,4096]{3,2,1,0:T(8,128)(2,1)S(1)} %collective-permute-done.3.refs_3_), channel_id=1, source_target_pairs={{0,48},{64,67},{1,49},{65,64},{2,50},{66,65},{3,51},{67,66},{16,0}... | collective-permute-start | bytes 1572872 | tf_op jit(solution)/shard_map/ppermute | solution.py:49
  58.4 13.8 %collective-permute-start.6 = (bf16[2,2,16,4096]{3,2,1,0:T(8,128)(2,1)S(1)}, bf16[2,2,16,4096]{3,2,1,0:T(8,128)(2,1)S(1)}, u32[]{:S(2)}, u32[]{:S(2)}) collective-permute-start(bf16[2,2,16,4096]{3,2,1,0:T(8,128)(2,1)S(1)} %get-tuple-element.15), channel_id=1, source_target_pairs={{0,16},{64,65},{1,17},{65,66},{2,18},{66,67},{3,19},{67,64},{16,32... | collective-permute-start | bytes 1572872 | tf_op jit(solution)/shard_map/ppermute | solution.py:45
  60.3 11.8 %collective-permute-start.7 = (bf16[2,2,16,4096]{3,2,1,0:T(8,128)(2,1)S(1)}, bf16[2,2,16,4096]{3,2,1,0:T(8,128)(2,1)S(1)}, u32[]{:S(2)}, u32[]{:S(2)}) collective-permute-start(bf16[2,2,16,4096]{3,2,1,0:T(8,128)(2,1)S(1)} %get-tuple-element.17), channel_id=1, source_target_pairs={{0,48},{64,67},{1,49},{65,64},{2,50},{66,65},{3,51},{67,66},{16,0}... | collective-permute-start | bytes 1572872 | tf_op jit(solution)/shard_map/ppermute | solution.py:49
  65.7 15.4 %collective-permute-start.10 = (bf16[2,2,16,4096]{3,2,1,0:T(8,128)(2,1)S(1)}, bf16[2,2,16,4096]{3,2,1,0:T(8,128)(2,1)S(1)}, u32[]{:S(2)}, u32[]{:S(2)}) collective-permute-start(bf16[2,2,16,4096]{3,2,1,0:T(8,128)(2,1)S(1)} %get-tuple-element.14.refs_5_), channel_id=1, source_target_pairs={{0,16},{64,65},{1,17},{65,66},{2,18},{66,67},{3,19},{67,64},{16,32... | collective-permute-start | bytes 1572872 | tf_op jit(solution)/shard_map/ppermute | solution.py:45
  67.6 13.4 %collective-permute-start.9 = (bf16[2,2,16,4096]{3,2,1,0:T(8,128)(2,1)S(1)}, bf16[2,2,16,4096]{3,2,1,0:T(8,128)(2,1)S(1)}, u32[]{:S(2)}, u32[]{:S(2)}) collective-permute-start(bf16[2,2,16,4096]{3,2,1,0:T(8,128)(2,1)S(1)} %get-tuple-element.19), channel_id=1, source_target_pairs={{0,48},{64,67},{1,49},{65,64},{2,50},{66,65},{3,51},{67,66},{16,0}... | collective-permute-start | bytes 1572872 | tf_op jit(solution)/shard_map/ppermute | solution.py:49
  72.4 11.5 %collective-permute-start.11 = (bf16[2,2,16,4096]{3,2,1,0:T(8,128)(2,1)S(1)}, bf16[2,2,16,4096]{3,2,1,0:T(8,128)(2,1)S(1)}, u32[]{:S(2)}, u32[]{:S(2)}) collective-permute-start(bf16[2,2,16,4096]{3,2,1,0:T(8,128)(2,1)S(1)} %get-tuple-element.21), channel_id=1, source_target_pairs={{0,48},{64,67},{1,49},{65,64},{2,50},{66,65},{3,51},{67,66},{16,0}... | collective-permute-start | bytes 1572872 | tf_op jit(solution)/shard_map/ppermute | solution.py:49
  77.3 11.1 %collective-permute-start.8 = (bf16[2,2,16,4096]{3,2,1,0:T(8,128)(2,1)S(1)}, bf16[2,2,16,4096]{3,2,1,0:T(8,128)(2,1)S(1)}, u32[]{:S(2)}, u32[]{:S(2)}) collective-permute-start(bf16[2,2,16,4096]{3,2,1,0:T(8,128)(2,1)S(1)} %get-tuple-element.18), channel_id=1, source_target_pairs={{0,16},{64,65},{1,17},{65,66},{2,18},{66,67},{3,19},{67,64},{16,32... | collective-permute-start | bytes 1572872 | tf_op jit(solution)/shard_map/ppermute | solution.py:45

commit v5 on v4

v5 whole, which is shorter than its diff:
```python
import functools

import jax
import jax.numpy as jnp
from jax import lax
from jax.experimental import pallas as pl
from jax.experimental.pallas import tpu as pltpu
from jax.sharding import Mesh, PartitionSpec as P

SEND = 4
AXES = ("zh", "c", "y", "zl", "x")
SIZES = (4, 2, 4, 4, 4)
INSIDE = pl.BlockSpec(memory_space=pltpu.VMEM)


def device(zh, c, y, zl, x):
    return (((zh * 2 + c) * 4 + y) * 4 + zl) * 4 + x


def mixed_groups(first):
    groups = []
    for zh in range(4):
        for c in range(2):
            for zl in range(4):
                for still in range(4):
                    if (c == 0) == (first == "x"):
                        groups.append([device(zh, c, still, zl, k) for k in range(4)])
                    else:
                        groups.append([device(zh, c, k, zl, still) for k in range(4)])
    return groups


def ring_pairs(partner):
    pairs = []
    for zh in range(4):
        for zl in range(4):
            for p in range(4):
                for still in range(4):
                    q = partner(p)
                    pairs.append((device(zh, 0, p, zl, still), device(zh, 0, q, zl, still)))
                    pairs.append((device(zh, 1, still, zl, p), device(zh, 1, still, zl, q)))
    return pairs


def from_mate(array):
    return lax.ppermute(array, AXES, ring_pairs(lambda p: p ^ 1))


def from_other(array):
    return lax.ppermute(array, AXES, ring_pairs(lambda p: 3 - p))


def block_kernel(rows_ref, *refs):
    weights, out_ref = refs[:6], refs[-1]
    gates, ups, downs = weights[0::3], weights[1::3], weights[2::3]
    width, hidden = gates[0].shape
    chunk = 1024
    deep = rows_ref.shape[0] * 16
    pieces = range(0, width, chunk)
    gates_of, ups_of, dhids_of = [], [], []
    for wg_ref, wu_ref, wd_ref in zip(gates, ups, downs):
        gu = dh = None
        for k in pieces:
            tok = rows_ref[:, 0, :, k : k + chunk].reshape(deep, chunk)
            cot = rows_ref[:, 1, :, k : k + chunk].reshape(deep, chunk)
            both = jnp.concatenate([wg_ref[k : k + chunk, :], wu_ref[k : k + chunk, :]], axis=1)
            one = jnp.dot(tok, both, preferred_element_type=jnp.float32)
            two = lax.dot_general(
                cot,
                wd_ref[:, k : k + chunk],
                (((1,), (1,)), ((), ())),
                preferred_element_type=jnp.float32,
            )
            gu, dh = (one, two) if gu is None else (gu + one, dh + two)
        gates_of.append(gu[:, :hidden])
        ups_of.append(gu[:, hidden:])
        dhids_of.append(dh)
    gate = jnp.concatenate(gates_of, axis=1)
    upper = jnp.concatenate(ups_of, axis=1)
    dhid = jnp.concatenate(dhids_of, axis=1)
    s = jax.nn.sigmoid(gate)
    hid = (gate * s * upper).astype(jnp.bfloat16)
    dgate = (dhid * upper * s * (1.0 + gate * (1.0 - s))).astype(jnp.bfloat16)
    dup = (dhid * gate * s).astype(jnp.bfloat16)
    for k in pieces:
        cut = slice(k, k + chunk)
        down = jnp.concatenate([ref[:, cut] for ref in downs])
        out = jnp.dot(hid, down, preferred_element_type=jnp.float32)
        out_ref[:, 0, :, cut] = out.astype(jnp.bfloat16).reshape(-1, 16, chunk)
        din = None
        for rows, refs_of in ((dgate, gates), (dup, ups)):
            both = jnp.concatenate([ref[cut, :] for ref in refs_of], axis=1)
            one = lax.dot_general(
                rows, both, (((1,), (1,)), ((), ())), preferred_element_type=jnp.float32
            )
            din = one if din is None else din + one
        out_ref[:, 1, :, cut] = din.astype(jnp.bfloat16).reshape(-1, 16, chunk)


def experts(block, weights):
    width, hidden = weights[0].shape
    count = block.shape[0] * 16
    return pl.pallas_call(
        block_kernel,
        in_specs=[INSIDE] * 7,
        out_specs=INSIDE,
        out_shape=like(*block.shape),
        compiler_params=pltpu.CompilerParams(vmem_limit_bytes=24 << 20),
        cost_estimate=pl.CostEstimate(
            flops=24 * count * width * hidden,
            bytes_accessed=(6 << 20) + 8 * count * width,
            transcendentals=2 * count * hidden,
        ),
    )(block, *weights)


def add_kernel(one_ref, two_ref, out_ref):
    total = one_ref[...].astype(jnp.float32) + two_ref[...].astype(jnp.float32)
    out_ref[...] = total.astype(jnp.bfloat16)


def light_kernel(got_ref, out_ref):
    for i in range(2):
        total = got_ref[0, i].astype(jnp.float32)
        for k in range(1, 4):
            total += got_ref[k, i].astype(jnp.float32)
        for z in range(4):
            out_ref[z, i] = total[4 * z : 4 * z + 4].astype(jnp.bfloat16)


def last_kernel(got_ref, out_ref):
    for i in range(2):
        total = got_ref[0, i].astype(jnp.float32)
        for k in range(1, 4):
            total += got_ref[k, i].astype(jnp.float32)
        out_ref[i] = total.astype(jnp.bfloat16)


def widen_kernel(got_ref, _, out_ref):
    for i in range(2):
        rows = jnp.concatenate([got_ref[z, i].astype(jnp.float32) for z in range(4)])
        rows = rows.astype(jnp.bfloat16)
        for k in range(4):
            out_ref[k, i] = rows


def columns_of(row):
    count = row.shape[1]
    at = lax.broadcasted_iota(jnp.int32, (count, count), 0)
    to = lax.broadcasted_iota(jnp.int32, (count, count), 1)
    return jnp.sum(jnp.where(at == to, row, 0), axis=1, keepdims=True)


def pick_kernel(id_ref, tokens_ref, grads_ref, out_ref):
    expert = lax.axis_index("zh") * 2 + lax.axis_index("c")
    row = id_ref[...]
    count = row.shape[1]
    at = lax.broadcasted_iota(jnp.int32, (count, count), 0)
    to = lax.broadcasted_iota(jnp.int32, (count, count), 1)
    same = (columns_of(row) == row) & (at < to)
    slot = jnp.sum(same.astype(jnp.int32), axis=0, keepdims=True)
    place = jnp.where(row == expert, slot, -1)
    wanted = lax.broadcasted_iota(jnp.int32, (8, count), 0)
    table = (wanted == place).astype(jnp.float32).astype(jnp.bfloat16)
    for i, ref in enumerate((tokens_ref, grads_ref)):
        rows = jnp.dot(table, ref[...], preferred_element_type=jnp.float32)
        for k in range(4):
            out_ref[k, i] = rows[:SEND].astype(jnp.bfloat16)


def back_kernel(id_ref, got_ref, *outs):
    row = id_ref[...]
    count = row.shape[1]
    column = columns_of(row)
    at = lax.broadcasted_iota(jnp.int32, (count, count), 0)
    to = lax.broadcasted_iota(jnp.int32, (count, count), 1)
    same = (column == row) & (to < at)
    slot = jnp.sum(same.astype(jnp.int32), axis=1, keepdims=True)
    cells = got_ref.shape[0] * SEND
    place = column * SEND + slot
    table = lax.broadcasted_iota(jnp.int32, (count, cells), 1) == place
    table = table.astype(jnp.float32).astype(jnp.bfloat16)
    for i, out in enumerate(outs):
        rows = jnp.concatenate([got_ref[e, i].astype(jnp.float32) for e in range(got_ref.shape[0])])
        out[...] = jnp.dot(
            table, rows.astype(jnp.bfloat16), preferred_element_type=jnp.float32
        ).astype(jnp.bfloat16)


def small(kernel, shapes, *arrays, after=()):
    size = sum(array.size for array in arrays)
    return pl.pallas_call(
        kernel,
        in_specs=[INSIDE] * len(arrays) + [pl.BlockSpec(memory_space=pl.ANY)] * len(after),
        out_specs=jax.tree.map(lambda _: INSIDE, shapes),
        out_shape=jax.tree.map(lambda shape: jax.ShapeDtypeStruct(shape.shape, jnp.bfloat16), shapes),
        compiler_params=pltpu.CompilerParams(vmem_limit_bytes=24 << 20),
        cost_estimate=pl.CostEstimate(flops=size, bytes_accessed=3 * size, transcendentals=0),
    )(*arrays, *after)


def like(*shape):
    return jax.ShapeDtypeStruct(shape, jnp.bfloat16)


def large_stage(block, weights):
    other = from_other(block)
    to_other = experts(other, weights)
    got = from_other(to_other)
    own = experts(block, weights)
    return small(add_kernel, like(*block.shape), own, got)


def shards(tokens, cotangent, expert_id, gate_weight, up_weight, down_weight):
    count, width = tokens.shape
    ids = expert_id.reshape(1, count)
    first = mixed_groups("x")
    held = [gate_weight[0], up_weight[0], down_weight[0]]
    mates = [from_mate(weight) for weight in held]

    def exchange(blocks, axis, groups=None):
        return lax.all_to_all(blocks, axis, 0, 0, axis_index_groups=groups, tiled=True)

    own = pl.pallas_call(
        pick_kernel,
        grid=(1,),
        in_specs=[
            pl.BlockSpec((1, count), lambda i: (0, 0)),
            pl.BlockSpec((count, width), lambda i: (0, 0)),
            pl.BlockSpec((count, width), lambda i: (0, 0)),
        ],
        out_specs=pl.BlockSpec((4, 2, SEND, width), lambda i: (0, 0, 0, 0)),
        out_shape=like(4, 2, SEND, width),
        compiler_params=pltpu.CompilerParams(vmem_limit_bytes=24 << 20),
    )(ids, tokens, cotangent)
    part = exchange(own, "zl")
    part = small(widen_kernel, like(4, 2, 16, width), part, after=mates[:1])
    part, mates[1] = lax.optimization_barrier((exchange(part, AXES, first), mates[1]))
    part = large_stage(part, held + mates)
    part = exchange(part, AXES, first)
    part = exchange(small(light_kernel, like(4, 2, SEND, width), part), "zl")
    mine = small(last_kernel, like(2, SEND, width), part)
    every = lax.all_gather(mine, ("zh", "c"), axis=0)
    return tuple(small(back_kernel, [like(count, width)] * 2, ids, every))


def solution(mesh):
    fine = Mesh(mesh.devices.reshape(SIZES), AXES)
    tensor, expert = ("y", "zl", "x"), ("zh", "c")
    placed = (
        P(tensor, None),
        P(tensor, None),
        P(tensor),
        P(expert, None, tensor),
        P(expert, None, tensor),
        P(expert, tensor, None),
    )
    return jax.shard_map(
        shards,
        mesh=fine,
        in_specs=placed,
        out_specs=(P(tensor, None), P(tensor, None)),
        check_vma=False,
    )
```

time: 153 us -> 142 us (0.928)
  blocking collectives: 89.6 us -> 59.6 us
  waiting for transfers between devices: 11.7 us -> 37 us
  starting transfers between devices: 40.1 us -> 27.7 us
  Pallas kernels: 7.54 us -> 13.8 us
    all_to_all x4 -> x2, blocking collectives: 49.7 us -> 22.9 us  [exchange(): lax.all_to_all(blocks, axis, 0, 0, axis_index_groups=groups, tiled=True)]
    ppermute x12 -> x5, starting transfers between devices: 40.1 us -> 15.8 us  [the longest x3 8.01 us: from_mate(): return lax.ppermute(array, AXES, ring_pairs(lambda p: p ^ 1))]
    all_to_all x0 -> x2, waiting for transfers between devices: none -> 14.6 us  [exchange(): lax.all_to_all(blocks, axis, 0, 0, axis_index_groups=groups, tiled=True)]
    all_to_all x0 -> x2, starting transfers between devices: none -> 11.9 us  [exchange(): lax.all_to_all(blocks, axis, 0, 0, axis_index_groups=groups, tiled=True)]
    ppermute x12 -> x5, waiting for transfers between devices: 11.7 us -> 22.4 us  [the longest x2 17.6 us: from_other(): return lax.ppermute(array, AXES, ring_pairs(lambda p: 3 - p))]
    pallas_call x9 -> x7, Pallas kernels: 7.25 us -> 12.8 us  [the longest x2 10.3 us: experts(): pl.pallas_call(block_kernel, in_specs=[INSIDE] * 7, out_specs=INSIDE, out...]
    all_gather x1, blocking collectives: 39.9 us -> 36.7 us  [shards(): every = lax.all_gather(mine, ('zh', 'c'), axis=0)]
  transfers between devices with their start and end apart: 12 -> 7, of which waited for: 4 -> 6; matrix products, arithmetic and copies ran while one was open for 0% -> 0% of each run, Pallas kernels for 2% -> 5%
where the time goes in v5:
time: 142 us
  blocking collectives  59.6 us (42%)
  waiting for transfers between devices  37 us (26%)
  starting transfers between devices  27.7 us (20%)
  Pallas kernels  13.8 us (10%)
  local copies, waits for them, and re-layouts  3.03 us (2%)
    all_gather x1, blocking collectives, shards(): every = lax.all_gather(mine, ('zh', 'c'), axis=0)  36.7 us
    all_to_all x2, blocking collectives, exchange(): lax.all_to_all(blocks, axis, 0, 0, axis_index_groups=groups, tiled=True)  22.9 us
    ppermute x2, waiting for transfers between devices, from_other(): return lax.ppermute(array, AXES, ring_pairs(lambda p: 3 - p))  17.6 us
    all_to_all x2, waiting for transfers between devices, exchange(): lax.all_to_all(blocks, axis, 0, 0, axis_index_groups=groups, tiled=True)  14.6 us
    all_to_all x2, starting transfers between devices, exchange(): lax.all_to_all(blocks, axis, 0, 0, axis_index_groups=groups, tiled=True)  11.9 us
    pallas_call x2, Pallas kernels, experts(): pl.pallas_call(block_kernel, in_specs=[INSIDE] * 7, out_specs=INSIDE, out...  10.3 us
    ppermute x3, starting transfers between devices, from_mate(): return lax.ppermute(array, AXES, ring_pairs(lambda p: p ^ 1))  8.01 us
    ppermute x2, starting transfers between devices, from_other(): return lax.ppermute(array, AXES, ring_pairs(lambda p: 3 - p))  7.81 us
  transfers between devices with their start and end apart: 7, of which 6 were waited for; matrix products, arithmetic and copies ran while one was open for 0% of the time, Pallas kernels for 5%

profile of v5, /device:TPU:1, one launch (start us, length us, event | category | flops | bytes accessed | tf_op | source)
XLA Modules:
  0.0 141.9 jit_solution(8073444949833004101)
XLA Ops:
  0.6 0.0 copy-start.4
  0.6 4.0 %collective-permute-start = (bf16[4096,128]{1,0:T(8,128)(2,1)}, bf16[4096,128]{1,0:T(8,128)(2,1)S(1)}, u32[]{:S(2)}, u32[]{:S(2)}) collective-permute-start(bf16[4096,128]{1,0:T(8,128)(2,1)} %bitcast.5), channel_id=1, source_target_pairs={{0,16},{64,65},{1,17},{80,81},{2,18},{96,97},{3,19},{112,113},{16,... | collective-permute-start | bytes 3145736 | tf_op jit(solution)/shard_map/ppermute | solution.py:46
  4.6 0.0 copy-done.4
  4.6 0.0 copy-start.2
  4.6 0.9 copy-done.2
  5.5 0.0 copy-start.3
  5.5 0.9 copy-done.3
  6.4 1.0 shard_map.77
  7.4 5.6 %all-to-all-start = ((bf16[4,2,4,4096]{3,2,1,0:T(4,128)(2,1)}), bf16[4,2,4,4096]{3,2,1,0:T(4,128)(2,1)S(1)}, u32[]{:S(2)}, u32[]{:S(2)}) async-start(bf16[4,2,4,4096]{3,2,1,0:T(4,128)(2,1)} %shard_map.77), calls=%async_computation | async-start | bytes 524288 | tf_op jit(solution)/shard_map/all_to_all | solution.py:222
  13.1 2.1 %collective-permute-start.1 = (bf16[4096,128]{1,0:T(8,128)(2,1)}, bf16[4096,128]{1,0:T(8,128)(2,1)}, u32[]{:S(2)}, u32[]{:S(2)}) collective-permute-start(bf16[4096,128]{1,0:T(8,128)(2,1)} %bitcast.2.refs_1_), channel_id=1, source_target_pairs={{0,16},{64,65},{1,17},{80,81},{2,18},{96,97},{3,19},{112,113},{16,... | collective-permute-start | bytes 3145736 | tf_op jit(solution)/shard_map/ppermute | solution.py:46
  15.2 3.5 %all-to-all-done.got_ref = bf16[4,2,4,4096]{3,2,1,0:T(4,128)(2,1)S(1)} async-done(((bf16[4,2,4,4096]{3,2,1,0:T(4,128)(2,1)}), bf16[4,2,4,4096]{3,2,1,0:T(4,128)(2,1)S(1)}, u32[]{:S(2)}, u32[]{:S(2)}) %all-to-all-start) | async-done | bytes 262176 | tf_op jit(solution)/shard_map/all_to_all | solution.py:222
  18.7 0.0 collective-permute-done._.refs_3_
  18.7 1.0 shard_map.78
  19.7 0.0 copy-start
  19.7 6.3 %all-to-all-start.1 = ((bf16[4,2,16,4096]{3,2,1,0:T(8,128)(2,1)}), bf16[4,2,16,4096]{3,2,1,0:T(8,128)(2,1)S(1)}, u32[]{:S(2)}, u32[]{:S(2)}) async-start(bf16[4,2,16,4096]{3,2,1,0:T(8,128)(2,1)} %shard_map.78), calls=%async_computation.1 | async-start | bytes 2097152 | tf_op jit(solution)/shard_map/all_to_all | solution.py:222
  26.0 1.9 %collective-permute-start.2 = (bf16[128,4096]{1,0:T(8,128)(2,1)}, bf16[128,4096]{1,0:T(8,128)(2,1)}, u32[]{:S(2)}, u32[]{:S(2)}) collective-permute-start(bf16[128,4096]{1,0:T(8,128)(2,1)} %bitcast.8), channel_id=1, source_target_pairs={{0,16},{64,65},{1,17},{80,81},{2,18},{96,97},{3,19},{112,113},{16,... | collective-permute-start | bytes 3145736 | tf_op jit(solution)/shard_map/ppermute | solution.py:46
  27.9 1.3 collective-permute-done.1.refs_4_
  29.2 11.1 %all-to-all-done.1.rows_ref = bf16[4,2,16,4096]{3,2,1,0:T(8,128)(2,1)S(1)} async-done(((bf16[4,2,16,4096]{3,2,1,0:T(8,128)(2,1)}), bf16[4,2,16,4096]{3,2,1,0:T(8,128)(2,1)S(1)}, u32[]{:S(2)}, u32[]{:S(2)}) %all-to-all-start.1) | async-done | bytes 1048608 | tf_op jit(solution)/shard_map/all_to_all | solution.py:222
  40.3 3.9 %collective-permute-start.3 = (bf16[4,2,16,4096]{3,2,1,0:T(8,128)(2,1)S(1)}, bf16[4,2,16,4096]{3,2,1,0:T(8,128)(2,1)S(1)}, u32[]{:S(2)}, u32[]{:S(2)}) collective-permute-start(bf16[4,2,16,4096]{3,2,1,0:T(8,128)(2,1)S(1)} %all-to-all-done.1.rows_ref), channel_id=1, source_target_pairs={{0,48},{64,67},{1,49},{80,83},{2,50},{96,99},{3,51},{112,115},{16,... | collective-permute-start | bytes 3145736 | tf_op jit(solution)/shard_map/ppermute | solution.py:50
  44.2 3.5 %collective-permute-done.2.refs_5_ = bf16[128,4096]{1,0:T(8,128)(2,1)} collective-permute-done((bf16[128,4096]{1,0:T(8,128)(2,1)}, bf16[128,4096]{1,0:T(8,128)(2,1)}, u32[]{:S(2)}, u32[]{:S(2)}) %collective-permute-start.2) | collective-permute-done | bytes 1048608 | tf_op jit(solution)/shard_map/ppermute | solution.py:46
  47.7 9.6 %collective-permute-done.3.rows_ref = bf16[4,2,16,4096]{3,2,1,0:T(8,128)(2,1)S(1)} collective-permute-done((bf16[4,2,16,4096]{3,2,1,0:T(8,128)(2,1)S(1)}, bf16[4,2,16,4096]{3,2,1,0:T(8,128)(2,1)S(1)}, u32[]{:S(2)}, u32[]{:S(2)}) %collective-permute-start.3) | collective-permute-done | bytes 1048608 | tf_op jit(solution)/shard_map/ppermute | solution.py:50
  57.4 0.0 copy-done
  57.4 0.0 copy-start.1
  57.4 1.2 copy-done.1
  58.6 5.1 %shard_map.80 = bf16[4,2,16,4096]{3,2,1,0:T(8,128)(2,1)S(1)} custom-call(bf16[4,2,16,4096]{3,2,1,0:T(8,128)(2,1)S(1)} %collective-permute-done.3.rows_ref, bf16[4096,128]{1,0:T(8,128)(2,1)S(1)} %bitcast.6, bf16[4096,128]{1,0:T(8,128)(2,1)} %bitcast.2.refs_1_, bf16[128,4096]{1,0:T(8,128)(2,1)S(1)} %bitcast.9, ...), custom_call_target="tpu_custom_call" | custom-call | flops 805306368 | bytes 8388608 | tf_op jit(solution)/shard_map/pallas_call | solution.py:103
  63.7 3.9 %collective-permute-start.4 = (bf16[4,2,16,4096]{3,2,1,0:T(8,128)(2,1)S(1)}, bf16[4,2,16,4096]{3,2,1,0:T(8,128)(2,1)S(1)}, u32[]{:S(2)}, u32[]{:S(2)}) collective-permute-start(bf16[4,2,16,4096]{3,2,1,0:T(8,128)(2,1)S(1)} %shard_map.80), channel_id=1, source_target_pairs={{0,48},{64,67},{1,49},{80,83},{2,50},{96,99},{3,51},{112,115},{16,... | collective-permute-start | bytes 3145736 | tf_op jit(solution)/shard_map/ppermute | solution.py:50
  67.6 5.1 %shard_map.79.one_ref = bf16[4,2,16,4096]{3,2,1,0:T(8,128)(2,1)S(1)} custom-call(bf16[4,2,16,4096]{3,2,1,0:T(8,128)(2,1)S(1)} %all-to-all-done.1.rows_ref, bf16[4096,128]{1,0:T(8,128)(2,1)S(1)} %bitcast.7, bf16[4096,128]{1,0:T(8,128)(2,1)} %bitcast.2.refs_1_, bf16[128,4096]{1,0:T(8,128)(2,1)S(1)} %bitcast.10, ...), custom_call_target="tpu_custom_call" | custom-call | flops 805306368 | bytes 8388608 | tf_op jit(solution)/shard_map/pallas_call | solution.py:103
  72.8 8.0 %collective-permute-done.4.two_ref = bf16[4,2,16,4096]{3,2,1,0:T(8,128)(2,1)S(1)} collective-permute-done((bf16[4,2,16,4096]{3,2,1,0:T(8,128)(2,1)S(1)}, bf16[4,2,16,4096]{3,2,1,0:T(8,128)(2,1)S(1)}, u32[]{:S(2)}, u32[]{:S(2)}) %collective-permute-start.4) | collective-permute-done | bytes 1048608 | tf_op jit(solution)/shard_map/ppermute | solution.py:50
  80.8 0.2 shard_map.81
  81.0 13.1 %all_to_all.20.got_ref = bf16[4,2,16,4096]{3,2,1,0:T(8,128)(2,1)S(1)} all-to-all(bf16[4,2,16,4096]{3,2,1,0:T(8,128)(2,1)S(1)} %shard_map.81), channel_id=1, replica_groups={{0,1,2,3},{16,17,18,19},{32,33,34,35},{48,49,50,51},{4,5,6,7},{20,21,22..., dimensions={0} | all-to-all | bytes 2097152 | tf_op jit(solution)/shard_map/all_to_all | solution.py:222
  94.1 0.1 shard_map.82
  94.2 9.8 %all_to_all.21.got_ref = bf16[4,2,4,4096]{3,2,1,0:T(4,128)(2,1)S(1)} all-to-all(bf16[4,2,4,4096]{3,2,1,0:T(4,128)(2,1)S(1)} %shard_map.82), channel_id=1, replica_groups=mesh['zh'=4,'c'=2,'y'=4,'zl'=4,'x'=4] {'zl'}, dimensions={0} | all-to-all | bytes 524288 | tf_op jit(solution)/shard_map/all_to_all | solution.py:222
  104.0 0.1 shard_map.83
  104.1 36.7 %all-gather = bf16[16,4,4096]{2,1,0:T(4,128)(2,1)S(1)} all-gather(bf16[2,4,4096]{2,1,0:T(4,128)(2,1)S(1)} %shard_map.83), channel_id=2, replica_groups=mesh['zh'=4,'c'=2,'y'=4,'zl'=4,'x'=4] {'zh','c'}, dimensions={0}, use_global_device_ids=true | all-gather | bytes 589824 | tf_op jit(solution)/shard_map/all_gather | solution.py:243
  140.8 1.0 shard_map.84
Async XLA Ops:
  0.6 4.0 %copy-start.4 = (s32[16]{0:T(128)S(1)}, s32[16]{0:T(128)}, u32[]{:S(2)}) copy-start(s32[16]{0:T(128)} %param.8) | copy-start | bytes 196
  0.6 18.0 %collective-permute-start = (bf16[4096,128]{1,0:T(8,128)(2,1)}, bf16[4096,128]{1,0:T(8,128)(2,1)S(1)}, u32[]{:S(2)}, u32[]{:S(2)}) collective-permute-start(bf16[4096,128]{1,0:T(8,128)(2,1)} %bitcast.5), channel_id=1, source_target_pairs={{0,16},{64,65},{1,17},{80,81},{2,18},{96,97},{3,19},{112,113},{16,... | collective-permute-start | bytes 3145736 | tf_op jit(solution)/shard_map/ppermute | solution.py:46
  4.6 0.9 copy-start.2
  5.5 0.9 copy-start.3
  7.4 11.2 %all-to-all-start = ((bf16[4,2,4,4096]{3,2,1,0:T(4,128)(2,1)}), bf16[4,2,4,4096]{3,2,1,0:T(4,128)(2,1)S(1)}, u32[]{:S(2)}, u32[]{:S(2)}) async-start(bf16[4,2,4,4096]{3,2,1,0:T(4,128)(2,1)} %shard_map.77), calls=%async_computation | async-start | bytes 524288 | tf_op jit(solution)/shard_map/all_to_all | solution.py:222
  13.1 16.1 %collective-permute-start.1 = (bf16[4096,128]{1,0:T(8,128)(2,1)}, bf16[4096,128]{1,0:T(8,128)(2,1)}, u32[]{:S(2)}, u32[]{:S(2)}) collective-permute-start(bf16[4096,128]{1,0:T(8,128)(2,1)} %bitcast.2.refs_1_), channel_id=1, source_target_pairs={{0,16},{64,65},{1,17},{80,81},{2,18},{96,97},{3,19},{112,113},{16,... | collective-permute-start | bytes 3145736 | tf_op jit(solution)/shard_map/ppermute | solution.py:46
  19.7 37.6 %copy-start = (bf16[1,4096,128]{2,1,0:T(8,128)(2,1)S(1)}, bf16[1,4096,128]{2,1,0:T(8,128)(2,1)}, u32[]{:S(2)}) copy-start(bf16[1,4096,128]{2,1,0:T(8,128)(2,1)} %param.9) | copy-start | bytes 3145732
  19.7 20.6 %all-to-all-start.1 = ((bf16[4,2,16,4096]{3,2,1,0:T(8,128)(2,1)}), bf16[4,2,16,4096]{3,2,1,0:T(8,128)(2,1)S(1)}, u32[]{:S(2)}, u32[]{:S(2)}) async-start(bf16[4,2,16,4096]{3,2,1,0:T(8,128)(2,1)} %shard_map.78), calls=%async_computation.1 | async-start | bytes 2097152 | tf_op jit(solution)/shard_map/all_to_all | solution.py:222
  26.0 21.8 %collective-permute-start.2 = (bf16[128,4096]{1,0:T(8,128)(2,1)}, bf16[128,4096]{1,0:T(8,128)(2,1)}, u32[]{:S(2)}, u32[]{:S(2)}) collective-permute-start(bf16[128,4096]{1,0:T(8,128)(2,1)} %bitcast.8), channel_id=1, source_target_pairs={{0,16},{64,65},{1,17},{80,81},{2,18},{96,97},{3,19},{112,113},{16,... | collective-permute-start | bytes 3145736 | tf_op jit(solution)/shard_map/ppermute | solution.py:46
  40.3 17.0 %collective-permute-start.3 = (bf16[4,2,16,4096]{3,2,1,0:T(8,128)(2,1)S(1)}, bf16[4,2,16,4096]{3,2,1,0:T(8,128)(2,1)S(1)}, u32[]{:S(2)}, u32[]{:S(2)}) collective-permute-start(bf16[4,2,16,4096]{3,2,1,0:T(8,128)(2,1)S(1)} %all-to-all-done.1.rows_ref), channel_id=1, source_target_pairs={{0,48},{64,67},{1,49},{80,83},{2,50},{96,99},{3,51},{112,115},{16,... | collective-permute-start | bytes 3145736 | tf_op jit(solution)/shard_map/ppermute | solution.py:50
  57.4 1.2 copy-start.1
  63.7 17.0 %collective-permute-start.4 = (bf16[4,2,16,4096]{3,2,1,0:T(8,128)(2,1)S(1)}, bf16[4,2,16,4096]{3,2,1,0:T(8,128)(2,1)S(1)}, u32[]{:S(2)}, u32[]{:S(2)}) collective-permute-start(bf16[4,2,16,4096]{3,2,1,0:T(8,128)(2,1)S(1)} %shard_map.80), channel_id=1, source_target_pairs={{0,48},{64,67},{1,49},{80,83},{2,50},{96,99},{3,51},{112,115},{16,... | collective-permute-start | bytes 3145736 | tf_op jit(solution)/shard_map/ppermute | solution.py:50

commit v6 on v5

--- a/solution.py
+++ b/solution.py
@@ -114,16 +114,29 @@
     )(block, *weights)
 
 
-def add_kernel(one_ref, two_ref, out_ref):
-    total = one_ref[...].astype(jnp.float32) + two_ref[...].astype(jnp.float32)
-    out_ref[...] = total.astype(jnp.bfloat16)
-
-
-def light_kernel(got_ref, out_ref):
+def rows_kernel(got_ref, _, out_ref):
     for i in range(2):
+        rows = jnp.concatenate([got_ref[z, i].astype(jnp.float32) for z in range(4)])
+        out_ref[i] = rows.astype(jnp.bfloat16)
+
+
+def widen_kernel(own_ref, other_ref, _, out_ref):
+    for k in range(4):
+        out_ref[k, 0] = own_ref[...]
+        out_ref[k, 1] = other_ref[...]
+
+
+def light_kernel(got_ref, own_ref, other_ref):
+    for i, out_ref in enumerate((own_ref, other_ref)):
         total = got_ref[0, i].astype(jnp.float32)
         for k in range(1, 4):
             total += got_ref[k, i].astype(jnp.float32)
+        out_ref[...] = total.astype(out_ref.dtype)
+
+
+def pair_kernel(own_ref, got_ref, out_ref):
+    for i in range(2):
+        total = own_ref[i].astype(jnp.float32) + got_ref[i].astype(jnp.float32)
         for z in range(4):
             out_ref[z, i] = total[4 * z : 4 * z + 4].astype(jnp.bfloat16)
 
@@ -134,14 +147,6 @@
         for k in range(1, 4):
             total += got_ref[k, i].astype(jnp.float32)
         out_ref[i] = total.astype(jnp.bfloat16)
-
-
-def widen_kernel(got_ref, _, out_ref):
-    for i in range(2):
-        rows = jnp.concatenate([got_ref[z, i].astype(jnp.float32) for z in range(4)])
-        rows = rows.astype(jnp.bfloat16)
-        for k in range(4):
-            out_ref[k, i] = rows
 
 
 def columns_of(row):
@@ -193,7 +198,7 @@
         kernel,
         in_specs=[INSIDE] * len(arrays) + [pl.BlockSpec(memory_space=pl.ANY)] * len(after),
         out_specs=jax.tree.map(lambda _: INSIDE, shapes),
-        out_shape=jax.tree.map(lambda shape: jax.ShapeDtypeStruct(shape.shape, jnp.bfloat16), shapes),
+        out_shape=shapes,
         compiler_params=pltpu.CompilerParams(vmem_limit_bytes=24 << 20),
         cost_estimate=pl.CostEstimate(flops=size, bytes_accessed=3 * size, transcendentals=0),
     )(*arrays, *after)
@@ -201,14 +206,6 @@
 
 def like(*shape):
     return jax.ShapeDtypeStruct(shape, jnp.bfloat16)
-
-
-def large_stage(block, weights):
-    other = from_other(block)
-    to_other = experts(other, weights)
-    got = from_other(to_other)
-    own = experts(block, weights)
-    return small(add_kernel, like(*block.shape), own, got)
 
 
 def shards(tokens, cotangent, expert_id, gate_weight, up_weight, down_weight):
@@ -234,11 +231,16 @@
         compiler_params=pltpu.CompilerParams(vmem_limit_bytes=24 << 20),
     )(ids, tokens, cotangent)
     part = exchange(own, "zl")
-    part = small(widen_kernel, like(4, 2, 16, width), part, after=mates[:1])
-    part, mates[1] = lax.optimization_barrier((exchange(part, AXES, first), mates[1]))
-    part = large_stage(part, held + mates)
-    part = exchange(part, AXES, first)
-    part = exchange(small(light_kernel, like(4, 2, SEND, width), part), "zl")
+    block = small(rows_kernel, like(2, 16, width), part, after=mates[:1])
+    part = small(
+        widen_kernel, like(4, 2, 2, 16, width), block, from_other(block), after=mates[1:2]
+    )
+    part = exchange(part, AXES, first).reshape(8, 2, 16, width)
+    part = experts(part, held + mates).reshape(4, 2, 2, 16, width)
+    total = jax.ShapeDtypeStruct((2, 16, width), jnp.float32)
+    own, other = small(light_kernel, [total, like(2, 16, width)], exchange(part, AXES, first))
+    part = small(pair_kernel, like(4, 2, SEND, width), own, from_other(other))
+    part = exchange(part, "zl")
     mine = small(last_kernel, like(2, SEND, width), part)
     every = lax.all_gather(mine, ("zh", "c"), axis=0)
     return tuple(small(back_kernel, [like(count, width)] * 2, ids, every))

time: 142 us -> 144 us (1.014)
  Pallas kernels: 13.8 us -> 5.62 us
  local copies, waits for them, and re-layouts: 3.03 us -> 10.9 us
  blocking collectives: 59.6 us -> 64.8 us
  starting transfers between devices: 27.7 us -> 25.4 us
    ppermute x3, waiting for transfers between devices: 4.81 us -> 27.7 us  [from_mate(): return lax.ppermute(array, AXES, ring_pairs(lambda p: p ^ 1))]
    ppermute x2, waiting for transfers between devices: 17.6 us -> 5.07 us  [from_other(): return lax.ppermute(array, AXES, ring_pairs(lambda p: 3 - p))]
    all_to_all x2, waiting for transfers between devices: 14.6 us -> 3.46 us  [exchange(): lax.all_to_all(blocks, axis, 0, 0, axis_index_groups=groups, tiled=True)]
    all_to_all x2, blocking collectives: 22.9 us -> 33.6 us  [exchange(): lax.all_to_all(blocks, axis, 0, 0, axis_index_groups=groups, tiled=True)]
    unnamed x10 -> x24, local copies, waits for them, and re-layouts: 3.03 us -> 10.9 us
    pallas_call x2 -> x1, Pallas kernels: 10.3 us -> 3.03 us  [experts(): pl.pallas_call(block_kernel, in_specs=[INSIDE] * 7, out_specs=INSIDE, out...]
    all_gather x1, blocking collectives: 36.7 us -> 31.3 us  [shards(): every = lax.all_gather(mine, ('zh', 'c'), axis=0)]
    all_to_all x2, starting transfers between devices: 11.9 us -> 9.8 us  [exchange(): lax.all_to_all(blocks, axis, 0, 0, axis_index_groups=groups, tiled=True)]
  transfers between devices with their start and end apart: 7 -> 7, of which waited for: 6 -> 4; matrix products, arithmetic and copies ran while one was open for 0% -> 0% of each run, Pallas kernels for 5% -> 1%
where the time goes in v6:
time: 144 us
  blocking collectives  64.8 us (45%)
  waiting for transfers between devices  36.2 us (25%)
  starting transfers between devices  25.4 us (18%)
  local copies, waits for them, and re-layouts  10.9 us (8%)
  Pallas kernels  5.62 us (4%)
    all_to_all x2, blocking collectives, exchange(): lax.all_to_all(blocks, axis, 0, 0, axis_index_groups=groups, tiled=True)  33.6 us
    all_gather x1, blocking collectives, shards(): every = lax.all_gather(mine, ('zh', 'c'), axis=0)  31.3 us
    ppermute x3, waiting for transfers between devices, from_mate(): return lax.ppermute(array, AXES, ring_pairs(lambda p: p ^ 1))  27.7 us
    unnamed x24, local copies, waits for them, and re-layouts  10.9 us
    all_to_all x2, starting transfers between devices, exchange(): lax.all_to_all(blocks, axis, 0, 0, axis_index_groups=groups, tiled=True)  9.8 us
    ppermute x3, starting transfers between devices, from_mate(): return lax.ppermute(array, AXES, ring_pairs(lambda p: p ^ 1))  8.26 us
    ppermute x2, starting transfers between devices, from_other(): return lax.ppermute(array, AXES, ring_pairs(lambda p: 3 - p))  7.32 us
    ppermute x2, waiting for transfers between devices, from_other(): return lax.ppermute(array, AXES, ring_pairs(lambda p: 3 - p))  5.07 us
  transfers between devices with their start and end apart: 7, of which 4 were waited for; matrix products, arithmetic and copies ran while one was open for 0% of the time, Pallas kernels for 1%

profile of v6, /device:TPU:1, one launch (start us, length us, event | category | flops | bytes accessed | tf_op | source)
XLA Modules:
  0.0 143.7 jit_solution(5788796153881119405)
XLA Ops:
  0.6 4.0 %collective-permute-start = (bf16[4096,128]{1,0:T(8,128)(2,1)}, bf16[4096,128]{1,0:T(8,128)(2,1)S(1)}, u32[]{:S(2)}, u32[]{:S(2)}) collective-permute-start(bf16[4096,128]{1,0:T(8,128)(2,1)} %bitcast.10), channel_id=1, source_target_pairs={{0,16},{64,65},{1,17},{80,81},{2,18},{96,97},{3,19},{112,113},{16,... | collective-permute-start | bytes 3145736 | tf_op jit(solution)/shard_map/ppermute | solution.py:46
  4.6 0.0 copy-start.8
  4.6 0.9 copy-done.8
  5.5 0.0 copy-start.9
  5.5 0.9 copy-done.9
  6.4 0.0 copy-start.10
  6.4 0.7 copy-done.10
  7.1 1.0 shard_map.77
  8.0 5.6 %all-to-all-start = ((bf16[4,2,4,4096]{3,2,1,0:T(4,128)(2,1)}), bf16[4,2,4,4096]{3,2,1,0:T(4,128)(2,1)S(1)}, u32[]{:S(2)}, u32[]{:S(2)}) async-start(bf16[4,2,4,4096]{3,2,1,0:T(4,128)(2,1)} %shard_map.77), calls=%async_computation | async-start | bytes 524288 | tf_op jit(solution)/shard_map/all_to_all | solution.py:219
  13.7 2.2 %collective-permute-start.2 = (bf16[4096,128]{1,0:T(8,128)(2,1)}, bf16[4096,128]{1,0:T(8,128)(2,1)S(1)}, u32[]{:S(2)}, u32[]{:S(2)}) collective-permute-start(bf16[4096,128]{1,0:T(8,128)(2,1)} %bitcast.12), channel_id=1, source_target_pairs={{0,16},{64,65},{1,17},{80,81},{2,18},{96,97},{3,19},{112,113},{16,... | collective-permute-start | bytes 3145736 | tf_op jit(solution)/shard_map/ppermute | solution.py:46
  15.8 3.5 %all-to-all-done.got_ref = bf16[4,2,4,4096]{3,2,1,0:T(4,128)(2,1)S(1)} async-done(((bf16[4,2,4,4096]{3,2,1,0:T(4,128)(2,1)}), bf16[4,2,4,4096]{3,2,1,0:T(4,128)(2,1)S(1)}, u32[]{:S(2)}, u32[]{:S(2)}) %all-to-all-start) | async-done | bytes 262176 | tf_op jit(solution)/shard_map/all_to_all | solution.py:219
  19.3 0.0 collective-permute-done._.refs_3_
  19.3 0.0 copy-start.1
  19.3 0.1 shard_map.78.own_ref
  19.4 3.8 %collective-permute-start.1 = (bf16[2,16,4096]{2,1,0:T(8,128)(2,1)S(1)}, bf16[2,16,4096]{2,1,0:T(8,128)(2,1)S(1)}, u32[]{:S(2)}, u32[]{:S(2)}) collective-permute-start(bf16[2,16,4096]{2,1,0:T(8,128)(2,1)S(1)} %shard_map.78.own_ref), channel_id=1, source_target_pairs={{0,48},{64,67},{1,49},{80,83},{2,50},{96,99},{3,51},{112,115},{16,... | collective-permute-start | bytes 786440 | tf_op jit(solution)/shard_map/ppermute | solution.py:50
  23.1 6.6 %collective-permute-done.2._.refs_4_ = bf16[4096,128]{1,0:T(8,128)(2,1)S(1)} collective-permute-done((bf16[4096,128]{1,0:T(8,128)(2,1)}, bf16[4096,128]{1,0:T(8,128)(2,1)S(1)}, u32[]{:S(2)}, u32[]{:S(2)}) %collective-permute-start.2) | collective-permute-done | bytes 1048608 | tf_op jit(solution)/shard_map/ppermute | solution.py:46
  29.7 0.0 collective-permute-done.1.other_ref
  29.7 0.1 shard_map.79
  29.8 0.0 copy-done.1
  29.9 0.0 copy-start
  29.9 1.3 copy-done
  31.2 4.2 %all-to-all-start.1 = ((bf16[4,2,2,16,4096]{4,3,2,1,0:T(8,128)(2,1)}), bf16[4,2,2,16,4096]{4,3,2,1,0:T(8,128)(2,1)S(1)}, u32[]{:S(2)}, u32[]{:S(2)}) async-start(bf16[4,2,2,16,4096]{4,3,2,1,0:T(8,128)(2,1)} %copy-done), calls=%async_computation.1 | async-start | bytes 4194304 | tf_op jit(solution)/shard_map/all_to_all | solution.py:219
  35.4 2.1 %collective-permute-start.3 = (bf16[128,4096]{1,0:T(8,128)(2,1)}, bf16[128,4096]{1,0:T(8,128)(2,1)S(1)}, u32[]{:S(2)}, u32[]{:S(2)}) collective-permute-start(bf16[128,4096]{1,0:T(8,128)(2,1)} %bitcast.14), channel_id=1, source_target_pairs={{0,16},{64,65},{1,17},{80,81},{2,18},{96,97},{3,19},{112,113},{16,... | collective-permute-start | bytes 3145736 | tf_op jit(solution)/shard_map/ppermute | solution.py:46
  37.5 21.1 %collective-permute-done.3.refs_5_ = bf16[128,4096]{1,0:T(8,128)(2,1)S(1)} collective-permute-done((bf16[128,4096]{1,0:T(8,128)(2,1)}, bf16[128,4096]{1,0:T(8,128)(2,1)S(1)}, u32[]{:S(2)}, u32[]{:S(2)}) %collective-permute-start.3) | collective-permute-done | bytes 1048608 | tf_op jit(solution)/shard_map/ppermute | solution.py:46
  58.7 0.0 copy-start.6
  58.7 1.0 copy-done.6
  59.6 0.0 all-to-all-done.1
  59.7 0.0 copy-start.2
  59.7 1.2 copy-done.2
  60.9 0.0 copy-start.3
  60.9 1.2 copy-done.3
  62.1 0.0 copy-start.4
  62.1 1.2 copy-done.4
  63.3 0.0 copy-start.5
  63.3 1.2 copy-done.5
  64.6 0.0 copy-start.7
  64.6 1.2 copy-done.7
  65.8 3.0 %shard_map.80 = bf16[8,2,16,4096]{3,2,1,0:T(8,128)(2,1)S(1)} custom-call(bf16[8,2,16,4096]{3,2,1,0:T(8,128)(2,1)S(1)} %bitcast.7, bf16[4096,128]{1,0:T(8,128)(2,1)S(1)} %bitcast.11, bf16[4096,128]{1,0:T(8,128)(2,1)S(1)} %bitcast.13, bf16[128,4096]{1,0:T(8,128)(2,1)S(1)} %bitcast.15, bf16[4096,128]{1,0:T(8,128)(2,1)S(1)} %copy-done.2, ...), custom_call_target="tpu_custom_call" | custom-call | flops 1610612736 | bytes 10485760 | tf_op jit(solution)/shard_map/pallas_call | solution.py:103
  68.8 23.2 %all_to_all.20.got_ref = bf16[4,2,2,16,4096]{4,3,2,1,0:T(8,128)(2,1)S(1)} all-to-all(bf16[4,2,2,16,4096]{4,3,2,1,0:T(8,128)(2,1)S(1)} %bitcast.8), channel_id=1, replica_groups={{0,1,2,3},{16,17,18,19},{32,33,34,35},{48,49,50,51},{4,5,6,7},{20,21,22..., dimensions={0} | all-to-all | bytes 4194304 | tf_op jit(solution)/shard_map/all_to_all | solution.py:219
  92.1 0.2 shard_map.81
  92.3 3.5 %collective-permute-start.4 = (bf16[2,16,4096]{2,1,0:T(8,128)(2,1)S(1)}, bf16[2,16,4096]{2,1,0:T(8,128)(2,1)S(1)}, u32[]{:S(2)}, u32[]{:S(2)}) collective-permute-start(bf16[2,16,4096]{2,1,0:T(8,128)(2,1)S(1)} %get-tuple-element.5), channel_id=1, source_target_pairs={{0,48},{64,67},{1,49},{80,83},{2,50},{96,99},{3,51},{112,115},{16,... | collective-permute-start | bytes 786440 | tf_op jit(solution)/shard_map/ppermute | solution.py:50
  95.9 5.1 %collective-permute-done.4.got_ref = bf16[2,16,4096]{2,1,0:T(8,128)(2,1)S(1)} collective-permute-done((bf16[2,16,4096]{2,1,0:T(8,128)(2,1)S(1)}, bf16[2,16,4096]{2,1,0:T(8,128)(2,1)S(1)}, u32[]{:S(2)}, u32[]{:S(2)}) %collective-permute-start.4) | collective-permute-done | bytes 262176 | tf_op jit(solution)/shard_map/ppermute | solution.py:50
  100.9 0.1 shard_map.82
  101.0 10.3 %all_to_all.21.got_ref = bf16[4,2,4,4096]{3,2,1,0:T(4,128)(2,1)S(1)} all-to-all(bf16[4,2,4,4096]{3,2,1,0:T(4,128)(2,1)S(1)} %shard_map.82), channel_id=1, replica_groups=mesh['zh'=4,'c'=2,'y'=4,'zl'=4,'x'=4] {'zl'}, dimensions={0} | all-to-all | bytes 524288 | tf_op jit(solution)/shard_map/all_to_all | solution.py:219
  111.3 0.1 shard_map.83
  111.4 31.3 %all-gather = bf16[16,4,4096]{2,1,0:T(4,128)(2,1)S(1)} all-gather(bf16[2,4,4096]{2,1,0:T(4,128)(2,1)S(1)} %shard_map.83), channel_id=2, replica_groups=mesh['zh'=4,'c'=2,'y'=4,'zl'=4,'x'=4] {'zh','c'}, dimensions={0}, use_global_device_ids=true | all-gather | bytes 589824 | tf_op jit(solution)/shard_map/all_gather | solution.py:245
  142.7 0.0 copy-done.11
  142.7 1.0 shard_map.84
  (1 shorter events, 0.0 us)
Async XLA Ops:
  0.6 18.7 %collective-permute-start = (bf16[4096,128]{1,0:T(8,128)(2,1)}, bf16[4096,128]{1,0:T(8,128)(2,1)S(1)}, u32[]{:S(2)}, u32[]{:S(2)}) collective-permute-start(bf16[4096,128]{1,0:T(8,128)(2,1)} %bitcast.10), channel_id=1, source_target_pairs={{0,16},{64,65},{1,17},{80,81},{2,18},{96,97},{3,19},{112,113},{16,... | collective-permute-start | bytes 3145736 | tf_op jit(solution)/shard_map/ppermute | solution.py:46
  4.6 0.9 copy-start.8
  5.5 0.9 copy-start.9
  6.4 0.7 copy-start.10
  8.0 11.2 %all-to-all-start = ((bf16[4,2,4,4096]{3,2,1,0:T(4,128)(2,1)}), bf16[4,2,4,4096]{3,2,1,0:T(4,128)(2,1)S(1)}, u32[]{:S(2)}, u32[]{:S(2)}) async-start(bf16[4,2,4,4096]{3,2,1,0:T(4,128)(2,1)} %shard_map.77), calls=%async_computation | async-start | bytes 524288 | tf_op jit(solution)/shard_map/all_to_all | solution.py:219
  13.7 16.0 %collective-permute-start.2 = (bf16[4096,128]{1,0:T(8,128)(2,1)}, bf16[4096,128]{1,0:T(8,128)(2,1)S(1)}, u32[]{:S(2)}, u32[]{:S(2)}) collective-permute-start(bf16[4096,128]{1,0:T(8,128)(2,1)} %bitcast.12), channel_id=1, source_target_pairs={{0,16},{64,65},{1,17},{80,81},{2,18},{96,97},{3,19},{112,113},{16,... | collective-permute-start | bytes 3145736 | tf_op jit(solution)/shard_map/ppermute | solution.py:46
  19.3 10.6 %copy-start.1 = (bf16[4096,128]{1,0:T(8,128)(2,1)}, bf16[4096,128]{1,0:T(8,128)(2,1)S(1)}, u32[]{:S(2)}) copy-start(bf16[4096,128]{1,0:T(8,128)(2,1)S(1)} %collective-permute-done._.refs_3_) | copy-start | bytes 3145732
  19.4 10.3 %collective-permute-start.1 = (bf16[2,16,4096]{2,1,0:T(8,128)(2,1)S(1)}, bf16[2,16,4096]{2,1,0:T(8,128)(2,1)S(1)}, u32[]{:S(2)}, u32[]{:S(2)}) collective-permute-start(bf16[2,16,4096]{2,1,0:T(8,128)(2,1)S(1)} %shard_map.78.own_ref), channel_id=1, source_target_pairs={{0,48},{64,67},{1,49},{80,83},{2,50},{96,99},{3,51},{112,115},{16,... | collective-permute-start | bytes 786440 | tf_op jit(solution)/shard_map/ppermute | solution.py:50
  29.9 1.3 copy-start
  31.2 28.5 %all-to-all-start.1 = ((bf16[4,2,2,16,4096]{4,3,2,1,0:T(8,128)(2,1)}), bf16[4,2,2,16,4096]{4,3,2,1,0:T(8,128)(2,1)S(1)}, u32[]{:S(2)}, u32[]{:S(2)}) async-start(bf16[4,2,2,16,4096]{4,3,2,1,0:T(8,128)(2,1)} %copy-done), calls=%async_computation.1 | async-start | bytes 4194304 | tf_op jit(solution)/shard_map/all_to_all | solution.py:219
  35.4 23.3 %collective-permute-start.3 = (bf16[128,4096]{1,0:T(8,128)(2,1)}, bf16[128,4096]{1,0:T(8,128)(2,1)S(1)}, u32[]{:S(2)}, u32[]{:S(2)}) collective-permute-start(bf16[128,4096]{1,0:T(8,128)(2,1)} %bitcast.14), channel_id=1, source_target_pairs={{0,16},{64,65},{1,17},{80,81},{2,18},{96,97},{3,19},{112,113},{16,... | collective-permute-start | bytes 3145736 | tf_op jit(solution)/shard_map/ppermute | solution.py:46
  58.7 1.0 copy-start.6
  59.7 1.2 copy-start.2
  60.9 1.2 copy-start.3
  62.1 1.2 copy-start.4
  63.3 1.2 copy-start.5
  64.6 1.2 copy-start.7
  92.0 50.6 %copy-start.11 = (s32[16]{0:T(128)S(1)}, s32[16]{0:T(128)}, u32[]{:S(2)}) copy-start(s32[16]{0:T(128)} %param.8) | copy-start | bytes 196
  92.3 8.6 %collective-permute-start.4 = (bf16[2,16,4096]{2,1,0:T(8,128)(2,1)S(1)}, bf16[2,16,4096]{2,1,0:T(8,128)(2,1)S(1)}, u32[]{:S(2)}, u32[]{:S(2)}) collective-permute-start(bf16[2,16,4096]{2,1,0:T(8,128)(2,1)S(1)} %get-tuple-element.5), channel_id=1, source_target_pairs={{0,48},{64,67},{1,49},{80,83},{2,50},{96,99},{3,51},{112,115},{16,... | collective-permute-start | bytes 786440 | tf_op jit(solution)/shard_map/ppermute | solution.py:50

commit v7 on v6

--- a/solution.py
+++ b/solution.py
@@ -10,6 +10,7 @@
 SEND = 4
 AXES = ("zh", "c", "y", "zl", "x")
 SIZES = (4, 2, 4, 4, 4)
+SCRATCH = 4 << 20
 INSIDE = pl.BlockSpec(memory_space=pltpu.VMEM)
 
 
@@ -105,7 +106,7 @@
         in_specs=[INSIDE] * 7,
         out_specs=INSIDE,
         out_shape=like(*block.shape),
-        compiler_params=pltpu.CompilerParams(vmem_limit_bytes=24 << 20),
+        compiler_params=pltpu.CompilerParams(vmem_limit_bytes=SCRATCH),
         cost_estimate=pl.CostEstimate(
             flops=24 * count * width * hidden,
             bytes_accessed=(6 << 20) + 8 * count * width,
@@ -199,7 +200,7 @@
         in_specs=[INSIDE] * len(arrays) + [pl.BlockSpec(memory_space=pl.ANY)] * len(after),
         out_specs=jax.tree.map(lambda _: INSIDE, shapes),
         out_shape=shapes,
-        compiler_params=pltpu.CompilerParams(vmem_limit_bytes=24 << 20),
+        compiler_params=pltpu.CompilerParams(vmem_limit_bytes=SCRATCH),
         cost_estimate=pl.CostEstimate(flops=size, bytes_accessed=3 * size, transcendentals=0),
     )(*arrays, *after)
 
@@ -228,7 +229,7 @@
         ],
         out_specs=pl.BlockSpec((4, 2, SEND, width), lambda i: (0, 0, 0, 0)),
         out_shape=like(4, 2, SEND, width),
-        compiler_params=pltpu.CompilerParams(vmem_limit_bytes=24 << 20),
+        compiler_params=pltpu.CompilerParams(vmem_limit_bytes=SCRATCH),
     )(ids, tokens, cotangent)
     part = exchange(own, "zl")
     block = small(rows_kernel, like(2, 16, width), part, after=mates[:1])

time: 144 us -> 144 us (level)
  no operation moved by 1% of the time
where the time goes in v7:
time: 144 us
  blocking collectives  64.8 us (45%)
  waiting for transfers between devices  36.2 us (25%)
  starting transfers between devices  25.4 us (18%)
  local copies, waits for them, and re-layouts  10.9 us (8%)
  Pallas kernels  5.62 us (4%)
    all_to_all x2, blocking collectives, exchange(): lax.all_to_all(blocks, axis, 0, 0, axis_index_groups=groups, tiled=True)  33.6 us
    all_gather x1, blocking collectives, shards(): every = lax.all_gather(mine, ('zh', 'c'), axis=0)  31.3 us
    ppermute x3, waiting for transfers between devices, from_mate(): return lax.ppermute(array, AXES, ring_pairs(lambda p: p ^ 1))  27.7 us
    unnamed x24, local copies, waits for them, and re-layouts  10.9 us
    all_to_all x2, starting transfers between devices, exchange(): lax.all_to_all(blocks, axis, 0, 0, axis_index_groups=groups, tiled=True)  9.8 us
    ppermute x3, starting transfers between devices, from_mate(): return lax.ppermute(array, AXES, ring_pairs(lambda p: p ^ 1))  8.26 us
    ppermute x2, starting transfers between devices, from_other(): return lax.ppermute(array, AXES, ring_pairs(lambda p: 3 - p))  7.32 us
    ppermute x2, waiting for transfers between devices, from_other(): return lax.ppermute(array, AXES, ring_pairs(lambda p: 3 - p))  5.07 us
  transfers between devices with their start and end apart: 7, of which 4 were waited for; matrix products, arithmetic and copies ran while one was open for 0% of the time, Pallas kernels for 1%

profile of v7, /device:TPU:1, one launch (start us, length us, event | category | flops | bytes accessed | tf_op | source)
XLA Modules:
  0.0 143.7 jit_solution(16406804477302622870)
XLA Ops:
  0.6 4.0 %collective-permute-start = (bf16[4096,128]{1,0:T(8,128)(2,1)}, bf16[4096,128]{1,0:T(8,128)(2,1)S(1)}, u32[]{:S(2)}, u32[]{:S(2)}) collective-permute-start(bf16[4096,128]{1,0:T(8,128)(2,1)} %bitcast.10), channel_id=1, source_target_pairs={{0,16},{64,65},{1,17},{80,81},{2,18},{96,97},{3,19},{112,113},{16,... | collective-permute-start | bytes 3145736 | tf_op jit(solution)/shard_map/ppermute | solution.py:47
  4.6 0.0 copy-start.8
  4.6 0.9 copy-done.8
  5.5 0.0 copy-start.9
  5.5 0.9 copy-done.9
  6.4 0.0 copy-start.10
  6.4 0.7 copy-done.10
  7.1 1.0 shard_map.77
  8.0 5.6 %all-to-all-start = ((bf16[4,2,4,4096]{3,2,1,0:T(4,128)(2,1)}), bf16[4,2,4,4096]{3,2,1,0:T(4,128)(2,1)S(1)}, u32[]{:S(2)}, u32[]{:S(2)}) async-start(bf16[4,2,4,4096]{3,2,1,0:T(4,128)(2,1)} %shard_map.77), calls=%async_computation | async-start | bytes 524288 | tf_op jit(solution)/shard_map/all_to_all | solution.py:220
  13.7 2.2 %collective-permute-start.2 = (bf16[4096,128]{1,0:T(8,128)(2,1)}, bf16[4096,128]{1,0:T(8,128)(2,1)S(1)}, u32[]{:S(2)}, u32[]{:S(2)}) collective-permute-start(bf16[4096,128]{1,0:T(8,128)(2,1)} %bitcast.12), channel_id=1, source_target_pairs={{0,16},{64,65},{1,17},{80,81},{2,18},{96,97},{3,19},{112,113},{16,... | collective-permute-start | bytes 3145736 | tf_op jit(solution)/shard_map/ppermute | solution.py:47
  15.8 3.5 %all-to-all-done.got_ref = bf16[4,2,4,4096]{3,2,1,0:T(4,128)(2,1)S(1)} async-done(((bf16[4,2,4,4096]{3,2,1,0:T(4,128)(2,1)}), bf16[4,2,4,4096]{3,2,1,0:T(4,128)(2,1)S(1)}, u32[]{:S(2)}, u32[]{:S(2)}) %all-to-all-start) | async-done | bytes 262176 | tf_op jit(solution)/shard_map/all_to_all | solution.py:220
  19.3 0.0 collective-permute-done._.refs_3_
  19.3 0.0 copy-start.1
  19.3 0.1 shard_map.78.own_ref
  19.4 3.8 %collective-permute-start.1 = (bf16[2,16,4096]{2,1,0:T(8,128)(2,1)S(1)}, bf16[2,16,4096]{2,1,0:T(8,128)(2,1)S(1)}, u32[]{:S(2)}, u32[]{:S(2)}) collective-permute-start(bf16[2,16,4096]{2,1,0:T(8,128)(2,1)S(1)} %shard_map.78.own_ref), channel_id=1, source_target_pairs={{0,48},{64,67},{1,49},{80,83},{2,50},{96,99},{3,51},{112,115},{16,... | collective-permute-start | bytes 786440 | tf_op jit(solution)/shard_map/ppermute | solution.py:51
  23.1 6.6 %collective-permute-done.2._.refs_4_ = bf16[4096,128]{1,0:T(8,128)(2,1)S(1)} collective-permute-done((bf16[4096,128]{1,0:T(8,128)(2,1)}, bf16[4096,128]{1,0:T(8,128)(2,1)S(1)}, u32[]{:S(2)}, u32[]{:S(2)}) %collective-permute-start.2) | collective-permute-done | bytes 1048608 | tf_op jit(solution)/shard_map/ppermute | solution.py:47
  29.7 0.0 collective-permute-done.1.other_ref
  29.7 0.1 shard_map.79
  29.8 0.0 copy-done.1
  29.9 0.0 copy-start
  29.9 1.3 copy-done
  31.2 4.2 %all-to-all-start.1 = ((bf16[4,2,2,16,4096]{4,3,2,1,0:T(8,128)(2,1)}), bf16[4,2,2,16,4096]{4,3,2,1,0:T(8,128)(2,1)S(1)}, u32[]{:S(2)}, u32[]{:S(2)}) async-start(bf16[4,2,2,16,4096]{4,3,2,1,0:T(8,128)(2,1)} %copy-done), calls=%async_computation.1 | async-start | bytes 4194304 | tf_op jit(solution)/shard_map/all_to_all | solution.py:220
  35.4 2.1 %collective-permute-start.3 = (bf16[128,4096]{1,0:T(8,128)(2,1)}, bf16[128,4096]{1,0:T(8,128)(2,1)S(1)}, u32[]{:S(2)}, u32[]{:S(2)}) collective-permute-start(bf16[128,4096]{1,0:T(8,128)(2,1)} %bitcast.14), channel_id=1, source_target_pairs={{0,16},{64,65},{1,17},{80,81},{2,18},{96,97},{3,19},{112,113},{16,... | collective-permute-start | bytes 3145736 | tf_op jit(solution)/shard_map/ppermute | solution.py:47
  37.5 21.1 %collective-permute-done.3.refs_5_ = bf16[128,4096]{1,0:T(8,128)(2,1)S(1)} collective-permute-done((bf16[128,4096]{1,0:T(8,128)(2,1)}, bf16[128,4096]{1,0:T(8,128)(2,1)S(1)}, u32[]{:S(2)}, u32[]{:S(2)}) %collective-permute-start.3) | collective-permute-done | bytes 1048608 | tf_op jit(solution)/shard_map/ppermute | solution.py:47
  58.7 0.0 copy-start.6
  58.7 1.0 copy-done.6
  59.6 0.0 all-to-all-done.1
  59.7 0.0 copy-start.2
  59.7 1.2 copy-done.2
  60.9 0.0 copy-start.3
  60.9 1.2 copy-done.3
  62.1 0.0 copy-start.4
  62.1 1.2 copy-done.4
  63.3 0.0 copy-start.5
  63.3 1.2 copy-done.5
  64.6 0.0 copy-start.7
  64.6 1.2 copy-done.7
  65.8 3.0 %shard_map.80 = bf16[8,2,16,4096]{3,2,1,0:T(8,128)(2,1)S(1)} custom-call(bf16[8,2,16,4096]{3,2,1,0:T(8,128)(2,1)S(1)} %bitcast.7, bf16[4096,128]{1,0:T(8,128)(2,1)S(1)} %bitcast.11, bf16[4096,128]{1,0:T(8,128)(2,1)S(1)} %bitcast.13, bf16[128,4096]{1,0:T(8,128)(2,1)S(1)} %bitcast.15, bf16[4096,128]{1,0:T(8,128)(2,1)S(1)} %copy-done.2, ...), custom_call_target="tpu_custom_call" | custom-call | flops 1610612736 | bytes 10485760 | tf_op jit(solution)/shard_map/pallas_call | solution.py:104
  68.8 23.2 %all_to_all.20.got_ref = bf16[4,2,2,16,4096]{4,3,2,1,0:T(8,128)(2,1)S(1)} all-to-all(bf16[4,2,2,16,4096]{4,3,2,1,0:T(8,128)(2,1)S(1)} %bitcast.8), channel_id=1, replica_groups={{0,1,2,3},{16,17,18,19},{32,33,34,35},{48,49,50,51},{4,5,6,7},{20,21,22..., dimensions={0} | all-to-all | bytes 4194304 | tf_op jit(solution)/shard_map/all_to_all | solution.py:220
  92.1 0.2 shard_map.81
  92.3 3.5 %collective-permute-start.4 = (bf16[2,16,4096]{2,1,0:T(8,128)(2,1)S(1)}, bf16[2,16,4096]{2,1,0:T(8,128)(2,1)S(1)}, u32[]{:S(2)}, u32[]{:S(2)}) collective-permute-start(bf16[2,16,4096]{2,1,0:T(8,128)(2,1)S(1)} %get-tuple-element.5), channel_id=1, source_target_pairs={{0,48},{64,67},{1,49},{80,83},{2,50},{96,99},{3,51},{112,115},{16,... | collective-permute-start | bytes 786440 | tf_op jit(solution)/shard_map/ppermute | solution.py:51
  95.9 5.1 %collective-permute-done.4.got_ref = bf16[2,16,4096]{2,1,0:T(8,128)(2,1)S(1)} collective-permute-done((bf16[2,16,4096]{2,1,0:T(8,128)(2,1)S(1)}, bf16[2,16,4096]{2,1,0:T(8,128)(2,1)S(1)}, u32[]{:S(2)}, u32[]{:S(2)}) %collective-permute-start.4) | collective-permute-done | bytes 262176 | tf_op jit(solution)/shard_map/ppermute | solution.py:51
  100.9 0.1 shard_map.82
  101.0 10.3 %all_to_all.21.got_ref = bf16[4,2,4,4096]{3,2,1,0:T(4,128)(2,1)S(1)} all-to-all(bf16[4,2,4,4096]{3,2,1,0:T(4,128)(2,1)S(1)} %shard_map.82), channel_id=1, replica_groups=mesh['zh'=4,'c'=2,'y'=4,'zl'=4,'x'=4] {'zl'}, dimensions={0} | all-to-all | bytes 524288 | tf_op jit(solution)/shard_map/all_to_all | solution.py:220
  111.3 0.1 shard_map.83
  111.4 31.3 %all-gather = bf16[16,4,4096]{2,1,0:T(4,128)(2,1)S(1)} all-gather(bf16[2,4,4096]{2,1,0:T(4,128)(2,1)S(1)} %shard_map.83), channel_id=2, replica_groups=mesh['zh'=4,'c'=2,'y'=4,'zl'=4,'x'=4] {'zh','c'}, dimensions={0}, use_global_device_ids=true | all-gather | bytes 589824 | tf_op jit(solution)/shard_map/all_gather | solution.py:246
  142.7 0.0 copy-done.11
  142.7 1.0 shard_map.84
  (1 shorter events, 0.0 us)
Async XLA Ops:
  0.6 18.7 %collective-permute-start = (bf16[4096,128]{1,0:T(8,128)(2,1)}, bf16[4096,128]{1,0:T(8,128)(2,1)S(1)}, u32[]{:S(2)}, u32[]{:S(2)}) collective-permute-start(bf16[4096,128]{1,0:T(8,128)(2,1)} %bitcast.10), channel_id=1, source_target_pairs={{0,16},{64,65},{1,17},{80,81},{2,18},{96,97},{3,19},{112,113},{16,... | collective-permute-start | bytes 3145736 | tf_op jit(solution)/shard_map/ppermute | solution.py:47
  4.6 0.9 copy-start.8
  5.5 0.9 copy-start.9
  6.4 0.7 copy-start.10
  8.0 11.2 %all-to-all-start = ((bf16[4,2,4,4096]{3,2,1,0:T(4,128)(2,1)}), bf16[4,2,4,4096]{3,2,1,0:T(4,128)(2,1)S(1)}, u32[]{:S(2)}, u32[]{:S(2)}) async-start(bf16[4,2,4,4096]{3,2,1,0:T(4,128)(2,1)} %shard_map.77), calls=%async_computation | async-start | bytes 524288 | tf_op jit(solution)/shard_map/all_to_all | solution.py:220
  13.7 16.0 %collective-permute-start.2 = (bf16[4096,128]{1,0:T(8,128)(2,1)}, bf16[4096,128]{1,0:T(8,128)(2,1)S(1)}, u32[]{:S(2)}, u32[]{:S(2)}) collective-permute-start(bf16[4096,128]{1,0:T(8,128)(2,1)} %bitcast.12), channel_id=1, source_target_pairs={{0,16},{64,65},{1,17},{80,81},{2,18},{96,97},{3,19},{112,113},{16,... | collective-permute-start | bytes 3145736 | tf_op jit(solution)/shard_map/ppermute | solution.py:47
  19.3 10.6 %copy-start.1 = (bf16[4096,128]{1,0:T(8,128)(2,1)}, bf16[4096,128]{1,0:T(8,128)(2,1)S(1)}, u32[]{:S(2)}) copy-start(bf16[4096,128]{1,0:T(8,128)(2,1)S(1)} %collective-permute-done._.refs_3_) | copy-start | bytes 3145732
  19.4 10.3 %collective-permute-start.1 = (bf16[2,16,4096]{2,1,0:T(8,128)(2,1)S(1)}, bf16[2,16,4096]{2,1,0:T(8,128)(2,1)S(1)}, u32[]{:S(2)}, u32[]{:S(2)}) collective-permute-start(bf16[2,16,4096]{2,1,0:T(8,128)(2,1)S(1)} %shard_map.78.own_ref), channel_id=1, source_target_pairs={{0,48},{64,67},{1,49},{80,83},{2,50},{96,99},{3,51},{112,115},{16,... | collective-permute-start | bytes 786440 | tf_op jit(solution)/shard_map/ppermute | solution.py:51
  29.9 1.3 copy-start
  31.2 28.5 %all-to-all-start.1 = ((bf16[4,2,2,16,4096]{4,3,2,1,0:T(8,128)(2,1)}), bf16[4,2,2,16,4096]{4,3,2,1,0:T(8,128)(2,1)S(1)}, u32[]{:S(2)}, u32[]{:S(2)}) async-start(bf16[4,2,2,16,4096]{4,3,2,1,0:T(8,128)(2,1)} %copy-done), calls=%async_computation.1 | async-start | bytes 4194304 | tf_op jit(solution)/shard_map/all_to_all | solution.py:220
  35.4 23.3 %collective-permute-start.3 = (bf16[128,4096]{1,0:T(8,128)(2,1)}, bf16[128,4096]{1,0:T(8,128)(2,1)S(1)}, u32[]{:S(2)}, u32[]{:S(2)}) collective-permute-start(bf16[128,4096]{1,0:T(8,128)(2,1)} %bitcast.14), channel_id=1, source_target_pairs={{0,16},{64,65},{1,17},{80,81},{2,18},{96,97},{3,19},{112,113},{16,... | collective-permute-start | bytes 3145736 | tf_op jit(solution)/shard_map/ppermute | solution.py:47
  58.7 1.0 copy-start.6
  59.7 1.2 copy-start.2
  60.9 1.2 copy-start.3
  62.1 1.2 copy-start.4
  63.3 1.2 copy-start.5
  64.6 1.2 copy-start.7
  92.0 50.6 %copy-start.11 = (s32[16]{0:T(128)S(1)}, s32[16]{0:T(128)}, u32[]{:S(2)}) copy-start(s32[16]{0:T(128)} %param.8) | copy-start | bytes 196
  92.3 8.6 %collective-permute-start.4 = (bf16[2,16,4096]{2,1,0:T(8,128)(2,1)S(1)}, bf16[2,16,4096]{2,1,0:T(8,128)(2,1)S(1)}, u32[]{:S(2)}, u32[]{:S(2)}) collective-permute-start(bf16[2,16,4096]{2,1,0:T(8,128)(2,1)S(1)} %get-tuple-element.5), channel_id=1, source_target_pairs={{0,48},{64,67},{1,49},{80,83},{2,50},{96,99},{3,51},{112,115},{16,... | collective-permute-start | bytes 786440 | tf_op jit(solution)/shard_map/ppermute | solution.py:51

commit v8 on v7

--- a/solution.py
+++ b/solution.py
@@ -52,14 +52,23 @@
 
 
 def block_kernel(rows_ref, *refs):
-    weights, out_ref = refs[:6], refs[-1]
-    gates, ups, downs = weights[0::3], weights[1::3], weights[2::3]
-    width, hidden = gates[0].shape
+    weights, out_ref, tall, wide, sems = refs[:6], refs[6], refs[7], refs[8], refs[9]
+    places = [tall.at[0], tall.at[1], wide.at[0], tall.at[2], tall.at[3], wide.at[1]]
+    copies = [
+        pltpu.make_async_copy(ref, place, sems.at[i])
+        for i, (ref, place) in enumerate(zip(weights, places))
+    ]
+    for copy in copies:
+        copy.start()
+    gates, ups, downs = places[0::3], places[1::3], places[2::3]
+    width, hidden = tall.shape[1:]
     chunk = 1024
     deep = rows_ref.shape[0] * 16
     pieces = range(0, width, chunk)
     gates_of, ups_of, dhids_of = [], [], []
-    for wg_ref, wu_ref, wd_ref in zip(gates, ups, downs):
+    for i, (wg_ref, wu_ref, wd_ref) in enumerate(zip(gates, ups, downs)):
+        for copy in copies[3 * i : 3 * i + 3]:
+            copy.wait()
         gu = dh = None
         for k in pieces:
             tok = rows_ref[:, 0, :, k : k + chunk].reshape(deep, chunk)
@@ -103,10 +112,15 @@
     count = block.shape[0] * 16
     return pl.pallas_call(
         block_kernel,
-        in_specs=[INSIDE] * 7,
+        in_specs=[INSIDE] + [pl.BlockSpec(memory_space=pl.ANY)] * 6,
         out_specs=INSIDE,
         out_shape=like(*block.shape),
-        compiler_params=pltpu.CompilerParams(vmem_limit_bytes=SCRATCH),
+        scratch_shapes=[
+            pltpu.VMEM((4, width, hidden), jnp.bfloat16),
+            pltpu.VMEM((2, hidden, width), jnp.bfloat16),
+            pltpu.SemaphoreType.DMA((6,)),
+        ],
+        compiler_params=pltpu.CompilerParams(vmem_limit_bytes=58 << 20),
         cost_estimate=pl.CostEstimate(
             flops=24 * count * width * hidden,
             bytes_accessed=(6 << 20) + 8 * count * width,

time: 144 us -> 145 us (level)
  local copies, waits for them, and re-layouts: 10.9 us -> 4.19 us
  Pallas kernels: 5.62 us -> 12.3 us
    unnamed x24 -> x16, local copies, waits for them, and re-layouts: 10.9 us -> 4.19 us
    pallas_call x1, Pallas kernels: 3.03 us -> 8.27 us  [experts(): pl.pallas_call(block_kernel, in_specs=[INSIDE] + [pl.BlockSpec(memory_spa...]
where the time goes in v8:
time: 145 us; the launch traced here: 144 us
  blocking collectives  66 us (46%)
  waiting for transfers between devices  35.4 us (24%)
  starting transfers between devices  25.9 us (18%)
  Pallas kernels  12.3 us (8%)
  local copies, waits for them, and re-layouts  4.19 us (3%)
    all_to_all x2, blocking collectives, exchange(): lax.all_to_all(blocks, axis, 0, 0, axis_index_groups=groups, tiled=True)  33.9 us
    all_gather x1, blocking collectives, shards(): every = lax.all_gather(mine, ('zh', 'c'), axis=0)  32.1 us
    ppermute x3, waiting for transfers between devices, from_mate(): return lax.ppermute(array, AXES, ring_pairs(lambda p: p ^ 1))  27.7 us
    all_to_all x2, starting transfers between devices, exchange(): lax.all_to_all(blocks, axis, 0, 0, axis_index_groups=groups, tiled=True)  9.8 us
    pallas_call x1, Pallas kernels, experts(): pl.pallas_call(block_kernel, in_specs=[INSIDE] + [pl.BlockSpec(memory_spa...  8.27 us
    ppermute x3, starting transfers between devices, from_mate(): return lax.ppermute(array, AXES, ring_pairs(lambda p: p ^ 1))  8.27 us
    ppermute x2, starting transfers between devices, from_other(): return lax.ppermute(array, AXES, ring_pairs(lambda p: 3 - p))  7.79 us
    ppermute x2, waiting for transfers between devices, from_other(): return lax.ppermute(array, AXES, ring_pairs(lambda p: 3 - p))  4.3 us
  transfers between devices with their start and end apart: 7, of which 4 were waited for; matrix products, arithmetic and copies ran while one was open for 0% of the time, Pallas kernels for 1%

profile of v8, /device:TPU:1, one launch (start us, length us, event | category | flops | bytes accessed | tf_op | source)
XLA Modules:
  0.0 144.5 jit_solution(15632143569774298487)
XLA Ops:
  0.6 4.0 %collective-permute-start = (bf16[4096,128]{1,0:T(8,128)(2,1)}, bf16[4096,128]{1,0:T(8,128)(2,1)S(1)}, u32[]{:S(2)}, u32[]{:S(2)}) collective-permute-start(bf16[4096,128]{1,0:T(8,128)(2,1)} %bitcast.12), channel_id=1, source_target_pairs={{0,16},{64,65},{1,17},{80,81},{2,18},{96,97},{3,19},{112,113},{16,... | collective-permute-start | bytes 3145736 | tf_op jit(solution)/shard_map/ppermute | solution.py:47
  4.6 0.0 copy-start.2
  4.6 0.9 copy-done.2
  5.5 0.0 copy-start.3
  5.5 0.9 copy-done.3
  6.4 0.0 copy-start.4
  6.4 0.7 copy-done.4
  7.1 1.0 shard_map.77
  8.0 5.6 %all-to-all-start = ((bf16[4,2,4,4096]{3,2,1,0:T(4,128)(2,1)}), bf16[4,2,4,4096]{3,2,1,0:T(4,128)(2,1)S(1)}, u32[]{:S(2)}, u32[]{:S(2)}) async-start(bf16[4,2,4,4096]{3,2,1,0:T(4,128)(2,1)} %shard_map.77), calls=%async_computation | async-start | bytes 524288 | tf_op jit(solution)/shard_map/all_to_all | solution.py:234
  13.7 2.2 %collective-permute-start.2 = (bf16[4096,128]{1,0:T(8,128)(2,1)}, bf16[4096,128]{1,0:T(8,128)(2,1)S(1)}, u32[]{:S(2)}, u32[]{:S(2)}) collective-permute-start(bf16[4096,128]{1,0:T(8,128)(2,1)} %bitcast.14), channel_id=1, source_target_pairs={{0,16},{64,65},{1,17},{80,81},{2,18},{96,97},{3,19},{112,113},{16,... | collective-permute-start | bytes 3145736 | tf_op jit(solution)/shard_map/ppermute | solution.py:47
  15.8 3.5 %all-to-all-done.got_ref = bf16[4,2,4,4096]{3,2,1,0:T(4,128)(2,1)S(1)} async-done(((bf16[4,2,4,4096]{3,2,1,0:T(4,128)(2,1)}), bf16[4,2,4,4096]{3,2,1,0:T(4,128)(2,1)S(1)}, u32[]{:S(2)}, u32[]{:S(2)}) %all-to-all-start) | async-done | bytes 262176 | tf_op jit(solution)/shard_map/all_to_all | solution.py:234
  19.3 0.0 collective-permute-done._.refs_3_
  19.3 0.0 copy-start.1
  19.3 0.1 shard_map.78.own_ref
  19.4 3.8 %collective-permute-start.1 = (bf16[2,16,4096]{2,1,0:T(8,128)(2,1)S(1)}, bf16[2,16,4096]{2,1,0:T(8,128)(2,1)S(1)}, u32[]{:S(2)}, u32[]{:S(2)}) collective-permute-start(bf16[2,16,4096]{2,1,0:T(8,128)(2,1)S(1)} %shard_map.78.own_ref), channel_id=1, source_target_pairs={{0,48},{64,67},{1,49},{80,83},{2,50},{96,99},{3,51},{112,115},{16,... | collective-permute-start | bytes 786440 | tf_op jit(solution)/shard_map/ppermute | solution.py:51
  23.1 6.6 %collective-permute-done.2._.refs_4_ = bf16[4096,128]{1,0:T(8,128)(2,1)S(1)} collective-permute-done((bf16[4096,128]{1,0:T(8,128)(2,1)}, bf16[4096,128]{1,0:T(8,128)(2,1)S(1)}, u32[]{:S(2)}, u32[]{:S(2)}) %collective-permute-start.2) | collective-permute-done | bytes 1048608 | tf_op jit(solution)/shard_map/ppermute | solution.py:47
  29.7 0.0 copy-start
  29.7 0.0 collective-permute-done.1.other_ref
  29.7 1.6 %shard_map.79 = bf16[4,2,2,16,4096]{4,3,2,1,0:T(8,128)(2,1)} custom-call(bf16[2,16,4096]{2,1,0:T(8,128)(2,1)S(1)} %shard_map.78.own_ref, bf16[2,16,4096]{2,1,0:T(8,128)(2,1)S(1)} %collective-permute-done.1.other_ref, bf16[4096,128]{1,0:T(8,128)(2,1)S(1)} %collective-permute-done.2._.refs_4_), custom_call_target="tpu_custom_call" | custom-call | flops 262144 | bytes 786432 | tf_op jit(solution)/shard_map/pallas_call | solution.py:212
  31.3 0.0 copy-done.1
  31.3 0.1 copy-done
  31.3 4.2 %all-to-all-start.1 = ((bf16[4,2,2,16,4096]{4,3,2,1,0:T(8,128)(2,1)}), bf16[4,2,2,16,4096]{4,3,2,1,0:T(8,128)(2,1)S(1)}, u32[]{:S(2)}, u32[]{:S(2)}) async-start(bf16[4,2,2,16,4096]{4,3,2,1,0:T(8,128)(2,1)} %shard_map.79), calls=%async_computation.1 | async-start | bytes 4194304 | tf_op jit(solution)/shard_map/all_to_all | solution.py:234
  35.5 2.2 %collective-permute-start.3 = (bf16[128,4096]{1,0:T(8,128)(2,1)}, bf16[128,4096]{1,0:T(8,128)(2,1)S(1)}, u32[]{:S(2)}, u32[]{:S(2)}) collective-permute-start(bf16[128,4096]{1,0:T(8,128)(2,1)} %bitcast.16), channel_id=1, source_target_pairs={{0,16},{64,65},{1,17},{80,81},{2,18},{96,97},{3,19},{112,113},{16,... | collective-permute-start | bytes 3145736 | tf_op jit(solution)/shard_map/ppermute | solution.py:47
  37.7 21.1 %collective-permute-done.3.refs_5_ = bf16[128,4096]{1,0:T(8,128)(2,1)S(1)} collective-permute-done((bf16[128,4096]{1,0:T(8,128)(2,1)}, bf16[128,4096]{1,0:T(8,128)(2,1)S(1)}, u32[]{:S(2)}, u32[]{:S(2)}) %collective-permute-start.3) | collective-permute-done | bytes 1048608 | tf_op jit(solution)/shard_map/ppermute | solution.py:47
  58.8 0.0 copy-start.7
  58.8 0.0 all-to-all-done.1
  58.8 0.0 copy-start.6
  58.8 1.0 copy-done.7
  59.8 0.7 copy-done.6
  60.5 8.3 %shard_map.80 = bf16[8,2,16,4096]{3,2,1,0:T(8,128)(2,1)} custom-call(bf16[8,2,16,4096]{3,2,1,0:T(8,128)(2,1)} %bitcast.10, bf16[4096,128]{1,0:T(8,128)(2,1)} %bitcast.13, bf16[4096,128]{1,0:T(8,128)(2,1)} %bitcast.15, bf16[128,4096]{1,0:T(8,128)(2,1)} %bitcast.17, bf16[4096,128]{1,0:T(8,128)(2,1)} %copy-done.1, bf16[4096,128]{1,0:T(8,128)(2,1)} %copy-done, ...), custom_call_target="tpu_custom_call" | custom-call | flops 1610612736 | bytes 10485760 | tf_op jit(solution)/shard_map/pallas_call | solution.py:113
  68.8 23.2 %all_to_all.20.got_ref = bf16[4,2,2,16,4096]{4,3,2,1,0:T(8,128)(2,1)S(1)} all-to-all(bf16[4,2,2,16,4096]{4,3,2,1,0:T(8,128)(2,1)} %bitcast.11), channel_id=1, replica_groups={{0,1,2,3},{16,17,18,19},{32,33,34,35},{48,49,50,51},{4,5,6,7},{20,21,22..., dimensions={0} | all-to-all | bytes 4194304 | tf_op jit(solution)/shard_map/all_to_all | solution.py:234
  91.9 0.0 copy-start.5
  91.9 0.2 shard_map.81
  92.2 4.0 %collective-permute-start.4 = (bf16[2,16,4096]{2,1,0:T(8,128)(2,1)S(1)}, bf16[2,16,4096]{2,1,0:T(8,128)(2,1)S(1)}, u32[]{:S(2)}, u32[]{:S(2)}) collective-permute-start(bf16[2,16,4096]{2,1,0:T(8,128)(2,1)S(1)} %get-tuple-element.5), channel_id=1, source_target_pairs={{0,48},{64,67},{1,49},{80,83},{2,50},{96,99},{3,51},{112,115},{16,... | collective-permute-start | bytes 786440 | tf_op jit(solution)/shard_map/ppermute | solution.py:51
  96.2 4.3 %collective-permute-done.4.got_ref = bf16[2,16,4096]{2,1,0:T(8,128)(2,1)S(1)} collective-permute-done((bf16[2,16,4096]{2,1,0:T(8,128)(2,1)S(1)}, bf16[2,16,4096]{2,1,0:T(8,128)(2,1)S(1)}, u32[]{:S(2)}, u32[]{:S(2)}) %collective-permute-start.4) | collective-permute-done | bytes 262176 | tf_op jit(solution)/shard_map/ppermute | solution.py:51
  100.5 0.1 shard_map.82
  100.6 10.7 %all_to_all.21.got_ref = bf16[4,2,4,4096]{3,2,1,0:T(4,128)(2,1)S(1)} all-to-all(bf16[4,2,4,4096]{3,2,1,0:T(4,128)(2,1)S(1)} %shard_map.82), channel_id=1, replica_groups=mesh['zh'=4,'c'=2,'y'=4,'zl'=4,'x'=4] {'zl'}, dimensions={0} | all-to-all | bytes 524288 | tf_op jit(solution)/shard_map/all_to_all | solution.py:234
  111.3 0.1 shard_map.83
  111.4 32.1 %all-gather = bf16[16,4,4096]{2,1,0:T(4,128)(2,1)S(1)} all-gather(bf16[2,4,4096]{2,1,0:T(4,128)(2,1)S(1)} %shard_map.83), channel_id=2, replica_groups=mesh['zh'=4,'c'=2,'y'=4,'zl'=4,'x'=4] {'zh','c'}, dimensions={0}, use_global_device_ids=true | all-gather | bytes 589824 | tf_op jit(solution)/shard_map/all_gather | solution.py:260
  143.5 0.0 copy-done.5
  143.5 1.0 shard_map.84
Async XLA Ops:
  0.6 18.7 %collective-permute-start = (bf16[4096,128]{1,0:T(8,128)(2,1)}, bf16[4096,128]{1,0:T(8,128)(2,1)S(1)}, u32[]{:S(2)}, u32[]{:S(2)}) collective-permute-start(bf16[4096,128]{1,0:T(8,128)(2,1)} %bitcast.12), channel_id=1, source_target_pairs={{0,16},{64,65},{1,17},{80,81},{2,18},{96,97},{3,19},{112,113},{16,... | collective-permute-start | bytes 3145736 | tf_op jit(solution)/shard_map/ppermute | solution.py:47
  4.6 0.9 copy-start.2
  5.5 0.9 copy-start.3
  6.4 0.7 copy-start.4
  8.0 11.2 %all-to-all-start = ((bf16[4,2,4,4096]{3,2,1,0:T(4,128)(2,1)}), bf16[4,2,4,4096]{3,2,1,0:T(4,128)(2,1)S(1)}, u32[]{:S(2)}, u32[]{:S(2)}) async-start(bf16[4,2,4,4096]{3,2,1,0:T(4,128)(2,1)} %shard_map.77), calls=%async_computation | async-start | bytes 524288 | tf_op jit(solution)/shard_map/all_to_all | solution.py:234
  13.7 16.0 %collective-permute-start.2 = (bf16[4096,128]{1,0:T(8,128)(2,1)}, bf16[4096,128]{1,0:T(8,128)(2,1)S(1)}, u32[]{:S(2)}, u32[]{:S(2)}) collective-permute-start(bf16[4096,128]{1,0:T(8,128)(2,1)} %bitcast.14), channel_id=1, source_target_pairs={{0,16},{64,65},{1,17},{80,81},{2,18},{96,97},{3,19},{112,113},{16,... | collective-permute-start | bytes 3145736 | tf_op jit(solution)/shard_map/ppermute | solution.py:47
  19.3 12.0 %copy-start.1 = (bf16[4096,128]{1,0:T(8,128)(2,1)}, bf16[4096,128]{1,0:T(8,128)(2,1)S(1)}, u32[]{:S(2)}) copy-start(bf16[4096,128]{1,0:T(8,128)(2,1)S(1)} %collective-permute-done._.refs_3_) | copy-start | bytes 3145732
  19.4 10.3 %collective-permute-start.1 = (bf16[2,16,4096]{2,1,0:T(8,128)(2,1)S(1)}, bf16[2,16,4096]{2,1,0:T(8,128)(2,1)S(1)}, u32[]{:S(2)}, u32[]{:S(2)}) collective-permute-start(bf16[2,16,4096]{2,1,0:T(8,128)(2,1)S(1)} %shard_map.78.own_ref), channel_id=1, source_target_pairs={{0,48},{64,67},{1,49},{80,83},{2,50},{96,99},{3,51},{112,115},{16,... | collective-permute-start | bytes 786440 | tf_op jit(solution)/shard_map/ppermute | solution.py:51
  29.7 1.6 %copy-start = (bf16[4096,128]{1,0:T(8,128)(2,1)}, bf16[4096,128]{1,0:T(8,128)(2,1)S(1)}, u32[]{:S(2)}) copy-start(bf16[4096,128]{1,0:T(8,128)(2,1)S(1)} %collective-permute-done.2._.refs_4_) | copy-start | bytes 3145732
  31.3 27.5 %all-to-all-start.1 = ((bf16[4,2,2,16,4096]{4,3,2,1,0:T(8,128)(2,1)}), bf16[4,2,2,16,4096]{4,3,2,1,0:T(8,128)(2,1)S(1)}, u32[]{:S(2)}, u32[]{:S(2)}) async-start(bf16[4,2,2,16,4096]{4,3,2,1,0:T(8,128)(2,1)} %shard_map.79), calls=%async_computation.1 | async-start | bytes 4194304 | tf_op jit(solution)/shard_map/all_to_all | solution.py:234
  35.5 23.3 %collective-permute-start.3 = (bf16[128,4096]{1,0:T(8,128)(2,1)}, bf16[128,4096]{1,0:T(8,128)(2,1)S(1)}, u32[]{:S(2)}, u32[]{:S(2)}) collective-permute-start(bf16[128,4096]{1,0:T(8,128)(2,1)} %bitcast.16), channel_id=1, source_target_pairs={{0,16},{64,65},{1,17},{80,81},{2,18},{96,97},{3,19},{112,113},{16,... | collective-permute-start | bytes 3145736 | tf_op jit(solution)/shard_map/ppermute | solution.py:47
  58.8 1.0 copy-start.7
  58.8 1.7 %copy-start.6 = (bf16[4,2,2,16,4096]{4,3,2,1,0:T(8,128)(2,1)}, bf16[4,2,2,16,4096]{4,3,2,1,0:T(8,128)(2,1)S(1)}, u32[]{:S(2)}) copy-start(bf16[4,2,2,16,4096]{4,3,2,1,0:T(8,128)(2,1)S(1)} %all-to-all-done.1) | copy-start | bytes 6291460
  91.9 51.5 %copy-start.5 = (s32[16]{0:T(128)S(1)}, s32[16]{0:T(128)}, u32[]{:S(2)}) copy-start(s32[16]{0:T(128)} %param.8) | copy-start | bytes 196
  92.2 8.3 %collective-permute-start.4 = (bf16[2,16,4096]{2,1,0:T(8,128)(2,1)S(1)}, bf16[2,16,4096]{2,1,0:T(8,128)(2,1)S(1)}, u32[]{:S(2)}, u32[]{:S(2)}) collective-permute-start(bf16[2,16,4096]{2,1,0:T(8,128)(2,1)S(1)} %get-tuple-element.5), channel_id=1, source_target_pairs={{0,48},{64,67},{1,49},{80,83},{2,50},{96,99},{3,51},{112,115},{16,... | collective-permute-start | bytes 786440 | tf_op jit(solution)/shard_map/ppermute | solution.py:51

commit v9 on v8

--- a/solution.py
+++ b/solution.py
@@ -51,74 +51,93 @@
     return lax.ppermute(array, AXES, ring_pairs(lambda p: 3 - p))
 
 
-def block_kernel(rows_ref, *refs):
-    weights, out_ref, tall, wide, sems = refs[:6], refs[6], refs[7], refs[8], refs[9]
-    places = [tall.at[0], tall.at[1], wide.at[0], tall.at[2], tall.at[3], wide.at[1]]
-    copies = [
-        pltpu.make_async_copy(ref, place, sems.at[i])
-        for i, (ref, place) in enumerate(zip(weights, places))
-    ]
-    for copy in copies:
-        copy.start()
-    gates, ups, downs = places[0::3], places[1::3], places[2::3]
+def block_kernel(from_ref, *refs):
+    weights, to_ref, rows_ref, out_ref, tall, wide, sems, out_sems = refs[:6], *refs[6:]
     width, hidden = tall.shape[1:]
     chunk = 1024
+    pieces = range(0, width, chunk)
     deep = rows_ref.shape[0] * 16
-    pieces = range(0, width, chunk)
-    gates_of, ups_of, dhids_of = [], [], []
-    for i, (wg_ref, wu_ref, wd_ref) in enumerate(zip(gates, ups, downs)):
-        for copy in copies[3 * i : 3 * i + 3]:
+    coming = []
+    for i, k in enumerate(pieces):
+        cut = pl.ds(k, chunk)
+        pairs = [(from_ref.at[:, :, :, cut], rows_ref.at[:, :, :, cut])]
+        for n in range(2):
+            gate, up, down = weights[3 * n : 3 * n + 3]
+            pairs.append((gate.at[cut, :], tall.at[2 * n, cut, :]))
+            pairs.append((up.at[cut, :], tall.at[2 * n + 1, cut, :]))
+            pairs.append((down.at[:, cut], wide.at[n, :, cut]))
+        copies = [
+            pltpu.make_async_copy(one, two, sems.at[i, n]) for n, (one, two) in enumerate(pairs)
+        ]
+        for copy in copies:
+            copy.start()
+        coming.append(copies)
+    gu, dh = [None, None], [None, None]
+    for copies, k in zip(coming, pieces):
+        for copy in copies:
             copy.wait()
-        gu = dh = None
-        for k in pieces:
-            tok = rows_ref[:, 0, :, k : k + chunk].reshape(deep, chunk)
-            cot = rows_ref[:, 1, :, k : k + chunk].reshape(deep, chunk)
-            both = jnp.concatenate([wg_ref[k : k + chunk, :], wu_ref[k : k + chunk, :]], axis=1)
+        tok = rows_ref[:, 0, :, k : k + chunk].reshape(deep, chunk)
+        cot = rows_ref[:, 1, :, k : k + chunk].reshape(deep, chunk)
+        for n in range(2):
+            both = jnp.concatenate(
+                [tall[2 * n, k : k + chunk, :], tall[2 * n + 1, k : k + chunk, :]], axis=1
+            )
             one = jnp.dot(tok, both, preferred_element_type=jnp.float32)
             two = lax.dot_general(
                 cot,
-                wd_ref[:, k : k + chunk],
+                wide[n, :, k : k + chunk],
                 (((1,), (1,)), ((), ())),
                 preferred_element_type=jnp.float32,
             )
-            gu, dh = (one, two) if gu is None else (gu + one, dh + two)
-        gates_of.append(gu[:, :hidden])
-        ups_of.append(gu[:, hidden:])
-        dhids_of.append(dh)
-    gate = jnp.concatenate(gates_of, axis=1)
-    upper = jnp.concatenate(ups_of, axis=1)
-    dhid = jnp.concatenate(dhids_of, axis=1)
+            gu[n] = one if gu[n] is None else gu[n] + one
+            dh[n] = two if dh[n] is None else dh[n] + two
+    gate = jnp.concatenate([part[:, :hidden] for part in gu], axis=1)
+    upper = jnp.concatenate([part[:, hidden:] for part in gu], axis=1)
+    dhid = jnp.concatenate(dh, axis=1)
     s = jax.nn.sigmoid(gate)
     hid = (gate * s * upper).astype(jnp.bfloat16)
     dgate = (dhid * upper * s * (1.0 + gate * (1.0 - s))).astype(jnp.bfloat16)
     dup = (dhid * gate * s).astype(jnp.bfloat16)
-    for k in pieces:
+    going = []
+    for i, k in enumerate(pieces):
         cut = slice(k, k + chunk)
-        down = jnp.concatenate([ref[:, cut] for ref in downs])
+        down = jnp.concatenate([wide[n, :, cut] for n in range(2)])
         out = jnp.dot(hid, down, preferred_element_type=jnp.float32)
         out_ref[:, 0, :, cut] = out.astype(jnp.bfloat16).reshape(-1, 16, chunk)
         din = None
-        for rows, refs_of in ((dgate, gates), (dup, ups)):
-            both = jnp.concatenate([ref[cut, :] for ref in refs_of], axis=1)
+        for m, rows in enumerate((dgate, dup)):
+            both = jnp.concatenate([tall[m, cut, :], tall[2 + m, cut, :]], axis=1)
             one = lax.dot_general(
                 rows, both, (((1,), (1,)), ((), ())), preferred_element_type=jnp.float32
             )
             din = one if din is None else din + one
         out_ref[:, 1, :, cut] = din.astype(jnp.bfloat16).reshape(-1, 16, chunk)
+        place = pl.ds(k, chunk)
+        copy = pltpu.make_async_copy(
+            out_ref.at[:, :, :, place], to_ref.at[:, :, :, place], out_sems.at[i]
+        )
+        copy.start()
+        going.append(copy)
+    for copy in going:
+        copy.wait()
 
 
 def experts(block, weights):
     width, hidden = weights[0].shape
     count = block.shape[0] * 16
+    outside = pl.BlockSpec(memory_space=pl.ANY)
     return pl.pallas_call(
         block_kernel,
-        in_specs=[INSIDE] + [pl.BlockSpec(memory_space=pl.ANY)] * 6,
-        out_specs=INSIDE,
+        in_specs=[outside] * 7,
+        out_specs=outside,
         out_shape=like(*block.shape),
         scratch_shapes=[
+            pltpu.VMEM(block.shape, jnp.bfloat16),
+            pltpu.VMEM(block.shape, jnp.bfloat16),
             pltpu.VMEM((4, width, hidden), jnp.bfloat16),
             pltpu.VMEM((2, hidden, width), jnp.bfloat16),
-            pltpu.SemaphoreType.DMA((6,)),
+            pltpu.SemaphoreType.DMA((width // 1024, 7)),
+            pltpu.SemaphoreType.DMA((width // 1024,)),
         ],
         compiler_params=pltpu.CompilerParams(vmem_limit_bytes=58 << 20),
         cost_estimate=pl.CostEstimate(

time: 145 us -> 143 us (0.986)
  Pallas kernels: 12.3 us -> 10.8 us
    pallas_call x1, Pallas kernels: 8.27 us -> 6.74 us  [experts(): pl.pallas_call(block_kernel, in_specs=[outside] * 7, out_specs=outside, o...]
where the time goes in v9:
time: 143 us
  blocking collectives  65.9 us (46%)
  waiting for transfers between devices  35.4 us (25%)
  starting transfers between devices  25.9 us (18%)
  Pallas kernels  10.8 us (8%)
  local copies, waits for them, and re-layouts  4.19 us (3%)
    all_to_all x2, blocking collectives, exchange(): lax.all_to_all(blocks, axis, 0, 0, axis_index_groups=groups, tiled=True)  33.9 us
    all_gather x1, blocking collectives, shards(): every = lax.all_gather(mine, ('zh', 'c'), axis=0)  32 us
    ppermute x3, waiting for transfers between devices, from_mate(): return lax.ppermute(array, AXES, ring_pairs(lambda p: p ^ 1))  27.7 us
    all_to_all x2, starting transfers between devices, exchange(): lax.all_to_all(blocks, axis, 0, 0, axis_index_groups=groups, tiled=True)  9.8 us
    ppermute x3, starting transfers between devices, from_mate(): return lax.ppermute(array, AXES, ring_pairs(lambda p: p ^ 1))  8.27 us
    ppermute x2, starting transfers between devices, from_other(): return lax.ppermute(array, AXES, ring_pairs(lambda p: 3 - p))  7.8 us
    pallas_call x1, Pallas kernels, experts(): pl.pallas_call(block_kernel, in_specs=[outside] * 7, out_specs=outside, o...  6.74 us
    ppermute x2, waiting for transfers between devices, from_other(): return lax.ppermute(array, AXES, ring_pairs(lambda p: 3 - p))  4.29 us
  transfers between devices with their start and end apart: 7, of which 4 were waited for; matrix products, arithmetic and copies ran while one was open for 0% of the time, Pallas kernels for 1%

profile of v9, /device:TPU:1, one launch (start us, length us, event | category | flops | bytes accessed | tf_op | source)
XLA Modules:
  0.0 142.9 jit_solution(17201169509853415476)
XLA Ops:
  0.6 4.0 %collective-permute-start = (bf16[4096,128]{1,0:T(8,128)(2,1)}, bf16[4096,128]{1,0:T(8,128)(2,1)S(1)}, u32[]{:S(2)}, u32[]{:S(2)}) collective-permute-start(bf16[4096,128]{1,0:T(8,128)(2,1)} %bitcast.12), channel_id=1, source_target_pairs={{0,16},{64,65},{1,17},{80,81},{2,18},{96,97},{3,19},{112,113},{16,... | collective-permute-start | bytes 3145736 | tf_op jit(solution)/shard_map/ppermute | solution.py:47
  4.6 0.0 copy-start.2
  4.6 0.9 copy-done.2
  5.5 0.0 copy-start.3
  5.5 0.9 copy-done.3
  6.4 0.0 copy-start.4
  6.4 0.7 copy-done.4
  7.1 1.0 shard_map.77
  8.0 5.6 %all-to-all-start = ((bf16[4,2,4,4096]{3,2,1,0:T(4,128)(2,1)}), bf16[4,2,4,4096]{3,2,1,0:T(4,128)(2,1)S(1)}, u32[]{:S(2)}, u32[]{:S(2)}) async-start(bf16[4,2,4,4096]{3,2,1,0:T(4,128)(2,1)} %shard_map.77), calls=%async_computation | async-start | bytes 524288 | tf_op jit(solution)/shard_map/all_to_all | solution.py:253
  13.7 2.2 %collective-permute-start.2 = (bf16[4096,128]{1,0:T(8,128)(2,1)}, bf16[4096,128]{1,0:T(8,128)(2,1)S(1)}, u32[]{:S(2)}, u32[]{:S(2)}) collective-permute-start(bf16[4096,128]{1,0:T(8,128)(2,1)} %bitcast.14), channel_id=1, source_target_pairs={{0,16},{64,65},{1,17},{80,81},{2,18},{96,97},{3,19},{112,113},{16,... | collective-permute-start | bytes 3145736 | tf_op jit(solution)/shard_map/ppermute | solution.py:47
  15.8 3.5 %all-to-all-done.got_ref = bf16[4,2,4,4096]{3,2,1,0:T(4,128)(2,1)S(1)} async-done(((bf16[4,2,4,4096]{3,2,1,0:T(4,128)(2,1)}), bf16[4,2,4,4096]{3,2,1,0:T(4,128)(2,1)S(1)}, u32[]{:S(2)}, u32[]{:S(2)}) %all-to-all-start) | async-done | bytes 262176 | tf_op jit(solution)/shard_map/all_to_all | solution.py:253
  19.3 0.0 collective-permute-done._.refs_3_
  19.3 0.0 copy-start.1
  19.3 0.1 shard_map.78.own_ref
  19.4 3.8 %collective-permute-start.1 = (bf16[2,16,4096]{2,1,0:T(8,128)(2,1)S(1)}, bf16[2,16,4096]{2,1,0:T(8,128)(2,1)S(1)}, u32[]{:S(2)}, u32[]{:S(2)}) collective-permute-start(bf16[2,16,4096]{2,1,0:T(8,128)(2,1)S(1)} %shard_map.78.own_ref), channel_id=1, source_target_pairs={{0,48},{64,67},{1,49},{80,83},{2,50},{96,99},{3,51},{112,115},{16,... | collective-permute-start | bytes 786440 | tf_op jit(solution)/shard_map/ppermute | solution.py:51
  23.1 6.6 %collective-permute-done.2._.refs_4_ = bf16[4096,128]{1,0:T(8,128)(2,1)S(1)} collective-permute-done((bf16[4096,128]{1,0:T(8,128)(2,1)}, bf16[4096,128]{1,0:T(8,128)(2,1)S(1)}, u32[]{:S(2)}, u32[]{:S(2)}) %collective-permute-start.2) | collective-permute-done | bytes 1048608 | tf_op jit(solution)/shard_map/ppermute | solution.py:47
  29.7 0.0 copy-start
  29.7 0.0 collective-permute-done.1.other_ref
  29.7 1.6 %shard_map.79 = bf16[4,2,2,16,4096]{4,3,2,1,0:T(8,128)(2,1)} custom-call(bf16[2,16,4096]{2,1,0:T(8,128)(2,1)S(1)} %shard_map.78.own_ref, bf16[2,16,4096]{2,1,0:T(8,128)(2,1)S(1)} %collective-permute-done.1.other_ref, bf16[4096,128]{1,0:T(8,128)(2,1)S(1)} %collective-permute-done.2._.refs_4_), custom_call_target="tpu_custom_call" | custom-call | flops 262144 | bytes 786432 | tf_op jit(solution)/shard_map/pallas_call | solution.py:231
  31.3 0.0 copy-done.1
  31.3 0.1 copy-done
  31.3 4.2 %all-to-all-start.1 = ((bf16[4,2,2,16,4096]{4,3,2,1,0:T(8,128)(2,1)}), bf16[4,2,2,16,4096]{4,3,2,1,0:T(8,128)(2,1)S(1)}, u32[]{:S(2)}, u32[]{:S(2)}) async-start(bf16[4,2,2,16,4096]{4,3,2,1,0:T(8,128)(2,1)} %shard_map.79), calls=%async_computation.1 | async-start | bytes 4194304 | tf_op jit(solution)/shard_map/all_to_all | solution.py:253
  35.5 2.2 %collective-permute-start.3 = (bf16[128,4096]{1,0:T(8,128)(2,1)}, bf16[128,4096]{1,0:T(8,128)(2,1)S(1)}, u32[]{:S(2)}, u32[]{:S(2)}) collective-permute-start(bf16[128,4096]{1,0:T(8,128)(2,1)} %bitcast.16), channel_id=1, source_target_pairs={{0,16},{64,65},{1,17},{80,81},{2,18},{96,97},{3,19},{112,113},{16,... | collective-permute-start | bytes 3145736 | tf_op jit(solution)/shard_map/ppermute | solution.py:47
  37.7 21.1 %collective-permute-done.3.refs_5_ = bf16[128,4096]{1,0:T(8,128)(2,1)S(1)} collective-permute-done((bf16[128,4096]{1,0:T(8,128)(2,1)}, bf16[128,4096]{1,0:T(8,128)(2,1)S(1)}, u32[]{:S(2)}, u32[]{:S(2)}) %collective-permute-start.3) | collective-permute-done | bytes 1048608 | tf_op jit(solution)/shard_map/ppermute | solution.py:47
  58.8 0.0 copy-start.7
  58.8 0.0 all-to-all-done.1
  58.8 0.0 copy-start.6
  58.8 1.0 copy-done.7
  59.8 0.7 copy-done.6
  60.5 6.7 %shard_map.80 = bf16[8,2,16,4096]{3,2,1,0:T(8,128)(2,1)} custom-call(bf16[8,2,16,4096]{3,2,1,0:T(8,128)(2,1)} %bitcast.10, bf16[4096,128]{1,0:T(8,128)(2,1)} %bitcast.13, bf16[4096,128]{1,0:T(8,128)(2,1)} %bitcast.15, bf16[128,4096]{1,0:T(8,128)(2,1)} %bitcast.17, bf16[4096,128]{1,0:T(8,128)(2,1)} %copy-done.1, bf16[4096,128]{1,0:T(8,128)(2,1)} %copy-done, ...), custom_call_target="tpu_custom_call" | custom-call | flops 1610612736 | bytes 10485760 | tf_op jit(solution)/shard_map/pallas_call | solution.py:129
  67.2 23.2 %all_to_all.20.got_ref = bf16[4,2,2,16,4096]{4,3,2,1,0:T(8,128)(2,1)S(1)} all-to-all(bf16[4,2,2,16,4096]{4,3,2,1,0:T(8,128)(2,1)} %bitcast.11), channel_id=1, replica_groups={{0,1,2,3},{16,17,18,19},{32,33,34,35},{48,49,50,51},{4,5,6,7},{20,21,22..., dimensions={0} | all-to-all | bytes 4194304 | tf_op jit(solution)/shard_map/all_to_all | solution.py:253
  90.4 0.0 copy-start.5
  90.4 0.2 shard_map.81
  90.7 4.0 %collective-permute-start.4 = (bf16[2,16,4096]{2,1,0:T(8,128)(2,1)S(1)}, bf16[2,16,4096]{2,1,0:T(8,128)(2,1)S(1)}, u32[]{:S(2)}, u32[]{:S(2)}) collective-permute-start(bf16[2,16,4096]{2,1,0:T(8,128)(2,1)S(1)} %get-tuple-element.5), channel_id=1, source_target_pairs={{0,48},{64,67},{1,49},{80,83},{2,50},{96,99},{3,51},{112,115},{16,... | collective-permute-start | bytes 786440 | tf_op jit(solution)/shard_map/ppermute | solution.py:51
  94.7 4.3 %collective-permute-done.4.got_ref = bf16[2,16,4096]{2,1,0:T(8,128)(2,1)S(1)} collective-permute-done((bf16[2,16,4096]{2,1,0:T(8,128)(2,1)S(1)}, bf16[2,16,4096]{2,1,0:T(8,128)(2,1)S(1)}, u32[]{:S(2)}, u32[]{:S(2)}) %collective-permute-start.4) | collective-permute-done | bytes 262176 | tf_op jit(solution)/shard_map/ppermute | solution.py:51
  99.0 0.1 shard_map.82
  99.1 10.7 %all_to_all.21.got_ref = bf16[4,2,4,4096]{3,2,1,0:T(4,128)(2,1)S(1)} all-to-all(bf16[4,2,4,4096]{3,2,1,0:T(4,128)(2,1)S(1)} %shard_map.82), channel_id=1, replica_groups=mesh['zh'=4,'c'=2,'y'=4,'zl'=4,'x'=4] {'zl'}, dimensions={0} | all-to-all | bytes 524288 | tf_op jit(solution)/shard_map/all_to_all | solution.py:253
  109.8 0.1 shard_map.83
  109.8 32.0 %all-gather = bf16[16,4,4096]{2,1,0:T(4,128)(2,1)S(1)} all-gather(bf16[2,4,4096]{2,1,0:T(4,128)(2,1)S(1)} %shard_map.83), channel_id=2, replica_groups=mesh['zh'=4,'c'=2,'y'=4,'zl'=4,'x'=4] {'zh','c'}, dimensions={0}, use_global_device_ids=true | all-gather | bytes 589824 | tf_op jit(solution)/shard_map/all_gather | solution.py:279
  141.8 0.0 copy-done.5
  141.8 1.0 shard_map.84
Async XLA Ops:
  0.6 18.7 %collective-permute-start = (bf16[4096,128]{1,0:T(8,128)(2,1)}, bf16[4096,128]{1,0:T(8,128)(2,1)S(1)}, u32[]{:S(2)}, u32[]{:S(2)}) collective-permute-start(bf16[4096,128]{1,0:T(8,128)(2,1)} %bitcast.12), channel_id=1, source_target_pairs={{0,16},{64,65},{1,17},{80,81},{2,18},{96,97},{3,19},{112,113},{16,... | collective-permute-start | bytes 3145736 | tf_op jit(solution)/shard_map/ppermute | solution.py:47
  4.6 0.9 copy-start.2
  5.5 0.9 copy-start.3
  6.4 0.7 copy-start.4
  8.0 11.2 %all-to-all-start = ((bf16[4,2,4,4096]{3,2,1,0:T(4,128)(2,1)}), bf16[4,2,4,4096]{3,2,1,0:T(4,128)(2,1)S(1)}, u32[]{:S(2)}, u32[]{:S(2)}) async-start(bf16[4,2,4,4096]{3,2,1,0:T(4,128)(2,1)} %shard_map.77), calls=%async_computation | async-start | bytes 524288 | tf_op jit(solution)/shard_map/all_to_all | solution.py:253
  13.7 16.0 %collective-permute-start.2 = (bf16[4096,128]{1,0:T(8,128)(2,1)}, bf16[4096,128]{1,0:T(8,128)(2,1)S(1)}, u32[]{:S(2)}, u32[]{:S(2)}) collective-permute-start(bf16[4096,128]{1,0:T(8,128)(2,1)} %bitcast.14), channel_id=1, source_target_pairs={{0,16},{64,65},{1,17},{80,81},{2,18},{96,97},{3,19},{112,113},{16,... | collective-permute-start | bytes 3145736 | tf_op jit(solution)/shard_map/ppermute | solution.py:47
  19.3 12.0 %copy-start.1 = (bf16[4096,128]{1,0:T(8,128)(2,1)}, bf16[4096,128]{1,0:T(8,128)(2,1)S(1)}, u32[]{:S(2)}) copy-start(bf16[4096,128]{1,0:T(8,128)(2,1)S(1)} %collective-permute-done._.refs_3_) | copy-start | bytes 3145732
  19.4 10.3 %collective-permute-start.1 = (bf16[2,16,4096]{2,1,0:T(8,128)(2,1)S(1)}, bf16[2,16,4096]{2,1,0:T(8,128)(2,1)S(1)}, u32[]{:S(2)}, u32[]{:S(2)}) collective-permute-start(bf16[2,16,4096]{2,1,0:T(8,128)(2,1)S(1)} %shard_map.78.own_ref), channel_id=1, source_target_pairs={{0,48},{64,67},{1,49},{80,83},{2,50},{96,99},{3,51},{112,115},{16,... | collective-permute-start | bytes 786440 | tf_op jit(solution)/shard_map/ppermute | solution.py:51
  29.7 1.6 %copy-start = (bf16[4096,128]{1,0:T(8,128)(2,1)}, bf16[4096,128]{1,0:T(8,128)(2,1)S(1)}, u32[]{:S(2)}) copy-start(bf16[4096,128]{1,0:T(8,128)(2,1)S(1)} %collective-permute-done.2._.refs_4_) | copy-start | bytes 3145732
  31.3 27.5 %all-to-all-start.1 = ((bf16[4,2,2,16,4096]{4,3,2,1,0:T(8,128)(2,1)}), bf16[4,2,2,16,4096]{4,3,2,1,0:T(8,128)(2,1)S(1)}, u32[]{:S(2)}, u32[]{:S(2)}) async-start(bf16[4,2,2,16,4096]{4,3,2,1,0:T(8,128)(2,1)} %shard_map.79), calls=%async_computation.1 | async-start | bytes 4194304 | tf_op jit(solution)/shard_map/all_to_all | solution.py:253
  35.5 23.3 %collective-permute-start.3 = (bf16[128,4096]{1,0:T(8,128)(2,1)}, bf16[128,4096]{1,0:T(8,128)(2,1)S(1)}, u32[]{:S(2)}, u32[]{:S(2)}) collective-permute-start(bf16[128,4096]{1,0:T(8,128)(2,1)} %bitcast.16), channel_id=1, source_target_pairs={{0,16},{64,65},{1,17},{80,81},{2,18},{96,97},{3,19},{112,113},{16,... | collective-permute-start | bytes 3145736 | tf_op jit(solution)/shard_map/ppermute | solution.py:47
  58.8 1.0 copy-start.7
  58.8 1.7 %copy-start.6 = (bf16[4,2,2,16,4096]{4,3,2,1,0:T(8,128)(2,1)}, bf16[4,2,2,16,4096]{4,3,2,1,0:T(8,128)(2,1)S(1)}, u32[]{:S(2)}) copy-start(bf16[4,2,2,16,4096]{4,3,2,1,0:T(8,128)(2,1)S(1)} %all-to-all-done.1) | copy-start | bytes 6291460
  90.4 51.4 %copy-start.5 = (s32[16]{0:T(128)S(1)}, s32[16]{0:T(128)}, u32[]{:S(2)}) copy-start(s32[16]{0:T(128)} %param.8) | copy-start | bytes 196
  90.7 8.3 %collective-permute-start.4 = (bf16[2,16,4096]{2,1,0:T(8,128)(2,1)S(1)}, bf16[2,16,4096]{2,1,0:T(8,128)(2,1)S(1)}, u32[]{:S(2)}, u32[]{:S(2)}) collective-permute-start(bf16[2,16,4096]{2,1,0:T(8,128)(2,1)S(1)} %get-tuple-element.5), channel_id=1, source_target_pairs={{0,48},{64,67},{1,49},{80,83},{2,50},{96,99},{3,51},{112,115},{16,... | collective-permute-start | bytes 786440 | tf_op jit(solution)/shard_map/ppermute | solution.py:51

commit v10 on v7

--- a/solution.py
+++ b/solution.py
@@ -52,7 +52,10 @@
 
 
 def block_kernel(rows_ref, *refs):
-    weights, out_ref = refs[:6], refs[-1]
+    weights, beside, out_ref = refs[:6], refs[6:-1], refs[-1]
+    for ref in beside:
+        out_ref[:, 0] = ref[...]
+        out_ref = out_ref.at[:, 1]
     gates, ups, downs = weights[0::3], weights[1::3], weights[2::3]
     width, hidden = gates[0].shape
     chunk = 1024
@@ -98,33 +101,29 @@
         out_ref[:, 1, :, cut] = din.astype(jnp.bfloat16).reshape(-1, 16, chunk)
 
 
-def experts(block, weights):
+def experts(block, weights, *beside):
     width, hidden = weights[0].shape
     count = block.shape[0] * 16
     return pl.pallas_call(
         block_kernel,
-        in_specs=[INSIDE] * 7,
+        in_specs=[INSIDE] * (7 + len(beside)),
         out_specs=INSIDE,
-        out_shape=like(*block.shape),
-        compiler_params=pltpu.CompilerParams(vmem_limit_bytes=SCRATCH),
+        out_shape=like(4, *[2] * len(beside), *block.shape[1:]),
+        compiler_params=pltpu.CompilerParams(vmem_limit_bytes=24 << 20),
         cost_estimate=pl.CostEstimate(
             flops=24 * count * width * hidden,
             bytes_accessed=(6 << 20) + 8 * count * width,
             transcendentals=2 * count * hidden,
         ),
-    )(block, *weights)
-
-
-def rows_kernel(got_ref, _, out_ref):
+    )(block, *weights, *beside)
+
+
+def widen_kernel(got_ref, _, out_ref):
     for i in range(2):
         rows = jnp.concatenate([got_ref[z, i].astype(jnp.float32) for z in range(4)])
-        out_ref[i] = rows.astype(jnp.bfloat16)
-
-
-def widen_kernel(own_ref, other_ref, _, out_ref):
-    for k in range(4):
-        out_ref[k, 0] = own_ref[...]
-        out_ref[k, 1] = other_ref[...]
+        rows = rows.astype(jnp.bfloat16)
+        for k in range(4):
+            out_ref[k, i] = rows
 
 
 def light_kernel(got_ref, own_ref, other_ref):
@@ -232,12 +231,10 @@
         compiler_params=pltpu.CompilerParams(vmem_limit_bytes=SCRATCH),
     )(ids, tokens, cotangent)
     part = exchange(own, "zl")
-    block = small(rows_kernel, like(2, 16, width), part, after=mates[:1])
-    part = small(
-        widen_kernel, like(4, 2, 2, 16, width), block, from_other(block), after=mates[1:2]
-    )
-    part = exchange(part, AXES, first).reshape(8, 2, 16, width)
-    part = experts(part, held + mates).reshape(4, 2, 2, 16, width)
+    part = small(widen_kernel, like(4, 2, 16, width), part, after=mates[:1])
+    block, mates[1] = lax.optimization_barrier((exchange(part, AXES, first), mates[1]))
+    other = from_other(block)
+    part = experts(other, held + mates, experts(block, held + mates))
     total = jax.ShapeDtypeStruct((2, 16, width), jnp.float32)
     own, other = small(light_kernel, [total, like(2, 16, width)], exchange(part, AXES, first))
     part = small(pair_kernel, like(4, 2, SEND, width), own, from_other(other))

time: 144 us -> 136 us (0.944)
  waiting for transfers between devices: 36.2 us -> 28.2 us
  Pallas kernels: 5.62 us -> 13.6 us
  local copies, waits for them, and re-layouts: 10.9 us -> 3.7 us
  blocking collectives: 64.8 us -> 62 us
  starting transfers between devices: 25.4 us -> 26.9 us
    ppermute x3, waiting for transfers between devices: 27.7 us -> 4.66 us  [from_mate(): return lax.ppermute(array, AXES, ring_pairs(lambda p: p ^ 1))]
    all_to_all x2, waiting for transfers between devices: 3.46 us -> 14.5 us  [exchange(): lax.all_to_all(blocks, axis, 0, 0, axis_index_groups=groups, tiled=True)]
    unnamed x24 -> x16, local copies, waits for them, and re-layouts: 10.9 us -> 3.7 us
    pallas_call x1 -> x2, Pallas kernels: 3.03 us -> 10.1 us  [experts(): pl.pallas_call(block_kernel, in_specs=[INSIDE] * (7 + len(beside)), out_s...]
    all_to_all x2, blocking collectives: 33.6 us -> 28 us  [exchange(): lax.all_to_all(blocks, axis, 0, 0, axis_index_groups=groups, tiled=True)]
    ppermute x2, waiting for transfers between devices: 5.07 us -> 8.97 us  [from_other(): return lax.ppermute(array, AXES, ring_pairs(lambda p: 3 - p))]
    all_gather x1, blocking collectives: 31.3 us -> 34 us  [shards(): every = lax.all_gather(mine, ('zh', 'c'), axis=0)]
    all_to_all x2, starting transfers between devices: 9.8 us -> 11.7 us  [exchange(): lax.all_to_all(blocks, axis, 0, 0, axis_index_groups=groups, tiled=True)]
  transfers between devices with their start and end apart: 7 -> 7, of which waited for: 4 -> 6; matrix products, arithmetic and copies ran while one was open for 0% -> 0% of each run, Pallas kernels for 1% -> 5%
where the time goes in v10:
time: 136 us; the launch traced here: 135 us
  blocking collectives  62 us (46%)
  waiting for transfers between devices  28.2 us (21%)
  starting transfers between devices  26.9 us (20%)
  Pallas kernels  13.6 us (10%)
  local copies, waits for them, and re-layouts  3.7 us (3%)
    all_gather x1, blocking collectives, shards(): every = lax.all_gather(mine, ('zh', 'c'), axis=0)  34 us
    all_to_all x2, blocking collectives, exchange(): lax.all_to_all(blocks, axis, 0, 0, axis_index_groups=groups, tiled=True)  28 us
    all_to_all x2, waiting for transfers between devices, exchange(): lax.all_to_all(blocks, axis, 0, 0, axis_index_groups=groups, tiled=True)  14.5 us
    all_to_all x2, starting transfers between devices, exchange(): lax.all_to_all(blocks, axis, 0, 0, axis_index_groups=groups, tiled=True)  11.7 us
    pallas_call x2, Pallas kernels, experts(): pl.pallas_call(block_kernel, in_specs=[INSIDE] * (7 + len(beside)), out_s...  10.1 us
    ppermute x2, waiting for transfers between devices, from_other(): return lax.ppermute(array, AXES, ring_pairs(lambda p: 3 - p))  8.97 us
    ppermute x3, starting transfers between devices, from_mate(): return lax.ppermute(array, AXES, ring_pairs(lambda p: p ^ 1))  8.15 us
    ppermute x2, starting transfers between devices, from_other(): return lax.ppermute(array, AXES, ring_pairs(lambda p: 3 - p))  6.98 us
  transfers between devices with their start and end apart: 7, of which 6 were waited for; matrix products, arithmetic and copies ran while one was open for 0% of the time, Pallas kernels for 5%

profile of v10, /device:TPU:1, one launch (start us, length us, event | category | flops | bytes accessed | tf_op | source)
XLA Modules:
  0.0 135.1 jit_solution(6136947045201432891)
XLA Ops:
  0.6 4.0 %collective-permute-start = (bf16[4096,128]{1,0:T(8,128)(2,1)}, bf16[4096,128]{1,0:T(8,128)(2,1)S(1)}, u32[]{:S(2)}, u32[]{:S(2)}) collective-permute-start(bf16[4096,128]{1,0:T(8,128)(2,1)} %bitcast.5), channel_id=1, source_target_pairs={{0,16},{64,65},{1,17},{80,81},{2,18},{96,97},{3,19},{112,113},{16,... | collective-permute-start | bytes 3145736 | tf_op jit(solution)/shard_map/ppermute | solution.py:47
  4.6 0.0 copy-start.4
  4.6 0.9 copy-done.4
  5.5 0.0 copy-start.5
  5.5 0.9 copy-done.5
  6.4 0.0 copy-start.6
  6.4 0.7 copy-done.6
  7.1 1.0 shard_map.77
  8.1 5.6 %all-to-all-start = ((bf16[4,2,4,4096]{3,2,1,0:T(4,128)(2,1)}), bf16[4,2,4,4096]{3,2,1,0:T(4,128)(2,1)S(1)}, u32[]{:S(2)}, u32[]{:S(2)}) async-start(bf16[4,2,4,4096]{3,2,1,0:T(4,128)(2,1)} %shard_map.77), calls=%async_computation | async-start | bytes 524288 | tf_op jit(solution)/shard_map/all_to_all | solution.py:219
  13.7 0.0 copy-start
  13.7 0.0 copy-start.1
  13.7 2.3 %collective-permute-start.1 = (bf16[4096,128]{1,0:T(8,128)(2,1)}, bf16[4096,128]{1,0:T(8,128)(2,1)}, u32[]{:S(2)}, u32[]{:S(2)}) collective-permute-start(bf16[4096,128]{1,0:T(8,128)(2,1)} %bitcast.8), channel_id=1, source_target_pairs={{0,16},{64,65},{1,17},{80,81},{2,18},{96,97},{3,19},{112,113},{16,... | collective-permute-start | bytes 3145736 | tf_op jit(solution)/shard_map/ppermute | solution.py:47
  16.0 3.3 %all-to-all-done.got_ref = bf16[4,2,4,4096]{3,2,1,0:T(4,128)(2,1)S(1)} async-done(((bf16[4,2,4,4096]{3,2,1,0:T(4,128)(2,1)}), bf16[4,2,4,4096]{3,2,1,0:T(4,128)(2,1)S(1)}, u32[]{:S(2)}, u32[]{:S(2)}) %all-to-all-start) | async-done | bytes 262176 | tf_op jit(solution)/shard_map/all_to_all | solution.py:219
  19.3 0.0 collective-permute-done._.refs_3_
  19.3 1.1 shard_map.78
  20.4 6.1 %all-to-all-start.1 = ((bf16[4,2,16,4096]{3,2,1,0:T(8,128)(2,1)}), bf16[4,2,16,4096]{3,2,1,0:T(8,128)(2,1)}, u32[]{:S(2)}, u32[]{:S(2)}) async-start(bf16[4,2,16,4096]{3,2,1,0:T(8,128)(2,1)} %shard_map.78), calls=%async_computation.1 | async-start | bytes 2097152 | tf_op jit(solution)/shard_map/all_to_all | solution.py:219
  26.5 1.9 %collective-permute-start.3 = (bf16[128,4096]{1,0:T(8,128)(2,1)}, bf16[128,4096]{1,0:T(8,128)(2,1)}, u32[]{:S(2)}, u32[]{:S(2)}) collective-permute-start(bf16[128,4096]{1,0:T(8,128)(2,1)} %bitcast.11), channel_id=1, source_target_pairs={{0,16},{64,65},{1,17},{80,81},{2,18},{96,97},{3,19},{112,113},{16,... | collective-permute-start | bytes 3145736 | tf_op jit(solution)/shard_map/ppermute | solution.py:47
  28.4 1.5 %collective-permute-done.1.refs_4_ = bf16[4096,128]{1,0:T(8,128)(2,1)} collective-permute-done((bf16[4096,128]{1,0:T(8,128)(2,1)}, bf16[4096,128]{1,0:T(8,128)(2,1)}, u32[]{:S(2)}, u32[]{:S(2)}) %collective-permute-start.1) | collective-permute-done | bytes 1048608 | tf_op jit(solution)/shard_map/ppermute | solution.py:47
  30.0 11.2 %all-to-all-done.1.rows_ref = bf16[4,2,16,4096]{3,2,1,0:T(8,128)(2,1)} async-done(((bf16[4,2,16,4096]{3,2,1,0:T(8,128)(2,1)}), bf16[4,2,16,4096]{3,2,1,0:T(8,128)(2,1)}, u32[]{:S(2)}, u32[]{:S(2)}) %all-to-all-start.1) | async-done | bytes 1048608 | tf_op jit(solution)/shard_map/all_to_all | solution.py:219
  41.2 3.9 %collective-permute-start.2 = (bf16[4,2,16,4096]{3,2,1,0:T(8,128)(2,1)}, bf16[4,2,16,4096]{3,2,1,0:T(8,128)(2,1)S(1)}, u32[]{:S(2)}, u32[]{:S(2)}) collective-permute-start(bf16[4,2,16,4096]{3,2,1,0:T(8,128)(2,1)} %all-to-all-done.1.rows_ref), channel_id=1, source_target_pairs={{0,48},{64,67},{1,49},{80,83},{2,50},{96,99},{3,51},{112,115},{16,... | collective-permute-start | bytes 3145736 | tf_op jit(solution)/shard_map/ppermute | solution.py:51
  45.1 3.1 %collective-permute-done.3.refs_5_ = bf16[128,4096]{1,0:T(8,128)(2,1)} collective-permute-done((bf16[128,4096]{1,0:T(8,128)(2,1)}, bf16[128,4096]{1,0:T(8,128)(2,1)}, u32[]{:S(2)}, u32[]{:S(2)}) %collective-permute-start.3) | collective-permute-done | bytes 1048608 | tf_op jit(solution)/shard_map/ppermute | solution.py:47
  48.3 0.0 copy-done
  48.3 0.0 copy-done.1
  48.3 0.0 copy-start.2
  48.3 1.2 copy-done.2
  49.5 0.0 copy-start.3
  49.5 5.2 %shard_map.79.refs_6_ = bf16[4,2,16,4096]{3,2,1,0:T(8,128)(2,1)S(1)} custom-call(bf16[4,2,16,4096]{3,2,1,0:T(8,128)(2,1)} %all-to-all-done.1.rows_ref, bf16[4096,128]{1,0:T(8,128)(2,1)S(1)} %bitcast.6, bf16[4096,128]{1,0:T(8,128)(2,1)S(1)} %bitcast.9, bf16[128,4096]{1,0:T(8,128)(2,1)S(1)} %bitcast.12, bf16[4096,128]{1,0:T(8,128)(2,1)S(1)} %collective-permute-done._.refs_3_, ...), custom_call_target="tpu_custom_call" | custom-call | flops 805306368 | bytes 8388608 | tf_op jit(solution)/shard_map/pallas_call | solution.py:107
  54.8 3.7 %collective-permute-done.2.rows_ref = bf16[4,2,16,4096]{3,2,1,0:T(8,128)(2,1)S(1)} collective-permute-done((bf16[4,2,16,4096]{3,2,1,0:T(8,128)(2,1)}, bf16[4,2,16,4096]{3,2,1,0:T(8,128)(2,1)S(1)}, u32[]{:S(2)}, u32[]{:S(2)}) %collective-permute-start.2) | collective-permute-done | bytes 1048608 | tf_op jit(solution)/shard_map/ppermute | solution.py:51
  58.4 0.0 copy-done.3
  58.4 4.9 %shard_map.80 = bf16[4,2,2,16,4096]{4,3,2,1,0:T(8,128)(2,1)S(1)} custom-call(bf16[4,2,16,4096]{3,2,1,0:T(8,128)(2,1)S(1)} %collective-permute-done.2.rows_ref, bf16[4096,128]{1,0:T(8,128)(2,1)S(1)} %bitcast.7, bf16[4096,128]{1,0:T(8,128)(2,1)S(1)} %bitcast.10, bf16[128,4096]{1,0:T(8,128)(2,1)S(1)} %bitcast.13, ...), custom_call_target="tpu_custom_call" | custom-call | flops 805306368 | bytes 8388608 | tf_op jit(solution)/shard_map/pallas_call | solution.py:107
  63.3 18.8 %all_to_all.20.got_ref = bf16[4,2,2,16,4096]{4,3,2,1,0:T(8,128)(2,1)S(1)} all-to-all(bf16[4,2,2,16,4096]{4,3,2,1,0:T(8,128)(2,1)S(1)} %shard_map.80), channel_id=1, replica_groups={{0,1,2,3},{16,17,18,19},{32,33,34,35},{48,49,50,51},{4,5,6,7},{20,21,22..., dimensions={0} | all-to-all | bytes 4194304 | tf_op jit(solution)/shard_map/all_to_all | solution.py:219
  82.1 0.0 copy-start.7
  82.1 0.2 shard_map.81
  82.4 3.0 %collective-permute-start.4 = (bf16[2,16,4096]{2,1,0:T(8,128)(2,1)S(1)}, bf16[2,16,4096]{2,1,0:T(8,128)(2,1)S(1)}, u32[]{:S(2)}, u32[]{:S(2)}) collective-permute-start(bf16[2,16,4096]{2,1,0:T(8,128)(2,1)S(1)} %get-tuple-element.9), channel_id=1, source_target_pairs={{0,48},{64,67},{1,49},{80,83},{2,50},{96,99},{3,51},{112,115},{16,... | collective-permute-start | bytes 786440 | tf_op jit(solution)/shard_map/ppermute | solution.py:51
  85.4 5.3 %collective-permute-done.4.got_ref = bf16[2,16,4096]{2,1,0:T(8,128)(2,1)S(1)} collective-permute-done((bf16[2,16,4096]{2,1,0:T(8,128)(2,1)S(1)}, bf16[2,16,4096]{2,1,0:T(8,128)(2,1)S(1)}, u32[]{:S(2)}, u32[]{:S(2)}) %collective-permute-start.4) | collective-permute-done | bytes 262176 | tf_op jit(solution)/shard_map/ppermute | solution.py:51
  90.7 0.1 shard_map.82
  90.8 9.3 %all_to_all.21.got_ref = bf16[4,2,4,4096]{3,2,1,0:T(4,128)(2,1)S(1)} all-to-all(bf16[4,2,4,4096]{3,2,1,0:T(4,128)(2,1)S(1)} %shard_map.82), channel_id=1, replica_groups=mesh['zh'=4,'c'=2,'y'=4,'zl'=4,'x'=4] {'zl'}, dimensions={0} | all-to-all | bytes 524288 | tf_op jit(solution)/shard_map/all_to_all | solution.py:219
  100.0 0.1 shard_map.83
  100.1 34.0 %all-gather = bf16[16,4,4096]{2,1,0:T(4,128)(2,1)S(1)} all-gather(bf16[2,4,4096]{2,1,0:T(4,128)(2,1)S(1)} %shard_map.83), channel_id=2, replica_groups=mesh['zh'=4,'c'=2,'y'=4,'zl'=4,'x'=4] {'zh','c'}, dimensions={0}, use_global_device_ids=true | all-gather | bytes 589824 | tf_op jit(solution)/shard_map/all_gather | solution.py:243
  134.1 0.0 copy-done.7
  134.1 1.0 shard_map.84
Async XLA Ops:
  0.6 18.7 %collective-permute-start = (bf16[4096,128]{1,0:T(8,128)(2,1)}, bf16[4096,128]{1,0:T(8,128)(2,1)S(1)}, u32[]{:S(2)}, u32[]{:S(2)}) collective-permute-start(bf16[4096,128]{1,0:T(8,128)(2,1)} %bitcast.5), channel_id=1, source_target_pairs={{0,16},{64,65},{1,17},{80,81},{2,18},{96,97},{3,19},{112,113},{16,... | collective-permute-start | bytes 3145736 | tf_op jit(solution)/shard_map/ppermute | solution.py:47
  4.6 0.9 copy-start.4
  5.5 0.9 copy-start.5
  6.4 0.7 copy-start.6
  8.1 11.2 %all-to-all-start = ((bf16[4,2,4,4096]{3,2,1,0:T(4,128)(2,1)}), bf16[4,2,4,4096]{3,2,1,0:T(4,128)(2,1)S(1)}, u32[]{:S(2)}, u32[]{:S(2)}) async-start(bf16[4,2,4,4096]{3,2,1,0:T(4,128)(2,1)} %shard_map.77), calls=%async_computation | async-start | bytes 524288 | tf_op jit(solution)/shard_map/all_to_all | solution.py:219
  13.7 34.6 %copy-start = (bf16[1,4096,128]{2,1,0:T(8,128)(2,1)S(1)}, bf16[1,4096,128]{2,1,0:T(8,128)(2,1)}, u32[]{:S(2)}) copy-start(bf16[1,4096,128]{2,1,0:T(8,128)(2,1)} %param.9) | copy-start | bytes 3145732
  13.7 34.6 %copy-start.1 = (bf16[1,4096,128]{2,1,0:T(8,128)(2,1)S(1)}, bf16[1,4096,128]{2,1,0:T(8,128)(2,1)}, u32[]{:S(2)}) copy-start(bf16[1,4096,128]{2,1,0:T(8,128)(2,1)} %param.10) | copy-start | bytes 3145732
  13.7 16.3 %collective-permute-start.1 = (bf16[4096,128]{1,0:T(8,128)(2,1)}, bf16[4096,128]{1,0:T(8,128)(2,1)}, u32[]{:S(2)}, u32[]{:S(2)}) collective-permute-start(bf16[4096,128]{1,0:T(8,128)(2,1)} %bitcast.8), channel_id=1, source_target_pairs={{0,16},{64,65},{1,17},{80,81},{2,18},{96,97},{3,19},{112,113},{16,... | collective-permute-start | bytes 3145736 | tf_op jit(solution)/shard_map/ppermute | solution.py:47
  20.4 20.8 %all-to-all-start.1 = ((bf16[4,2,16,4096]{3,2,1,0:T(8,128)(2,1)}), bf16[4,2,16,4096]{3,2,1,0:T(8,128)(2,1)}, u32[]{:S(2)}, u32[]{:S(2)}) async-start(bf16[4,2,16,4096]{3,2,1,0:T(8,128)(2,1)} %shard_map.78), calls=%async_computation.1 | async-start | bytes 2097152 | tf_op jit(solution)/shard_map/all_to_all | solution.py:219
  26.5 21.8 %collective-permute-start.3 = (bf16[128,4096]{1,0:T(8,128)(2,1)}, bf16[128,4096]{1,0:T(8,128)(2,1)}, u32[]{:S(2)}, u32[]{:S(2)}) collective-permute-start(bf16[128,4096]{1,0:T(8,128)(2,1)} %bitcast.11), channel_id=1, source_target_pairs={{0,16},{64,65},{1,17},{80,81},{2,18},{96,97},{3,19},{112,113},{16,... | collective-permute-start | bytes 3145736 | tf_op jit(solution)/shard_map/ppermute | solution.py:47
  41.2 17.2 %collective-permute-start.2 = (bf16[4,2,16,4096]{3,2,1,0:T(8,128)(2,1)}, bf16[4,2,16,4096]{3,2,1,0:T(8,128)(2,1)S(1)}, u32[]{:S(2)}, u32[]{:S(2)}) collective-permute-start(bf16[4,2,16,4096]{3,2,1,0:T(8,128)(2,1)} %all-to-all-done.1.rows_ref), channel_id=1, source_target_pairs={{0,48},{64,67},{1,49},{80,83},{2,50},{96,99},{3,51},{112,115},{16,... | collective-permute-start | bytes 3145736 | tf_op jit(solution)/shard_map/ppermute | solution.py:51
  48.3 1.2 copy-start.2
  49.5 8.9 %copy-start.3 = (bf16[1,128,4096]{2,1,0:T(8,128)(2,1)S(1)}, bf16[1,128,4096]{2,1,0:T(8,128)(2,1)}, u32[]{:S(2)}) copy-start(bf16[1,128,4096]{2,1,0:T(8,128)(2,1)} %param.11) | copy-start | bytes 3145732
  82.1 52.0 %copy-start.7 = (s32[16]{0:T(128)S(1)}, s32[16]{0:T(128)}, u32[]{:S(2)}) copy-start(s32[16]{0:T(128)} %param.8) | copy-start | bytes 196
  82.4 8.3 %collective-permute-start.4 = (bf16[2,16,4096]{2,1,0:T(8,128)(2,1)S(1)}, bf16[2,16,4096]{2,1,0:T(8,128)(2,1)S(1)}, u32[]{:S(2)}, u32[]{:S(2)}) collective-permute-start(bf16[2,16,4096]{2,1,0:T(8,128)(2,1)S(1)} %get-tuple-element.9), channel_id=1, source_target_pairs={{0,48},{64,67},{1,49},{80,83},{2,50},{96,99},{3,51},{112,115},{16,... | collective-permute-start | bytes 786440 | tf_op jit(solution)/shard_map/ppermute | solution.py:51

commit v11 on v10

--- a/solution.py
+++ b/solution.py
@@ -118,7 +118,7 @@
     )(block, *weights, *beside)
 
 
-def widen_kernel(got_ref, _, out_ref):
+def widen_kernel(got_ref, out_ref):
     for i in range(2):
         rows = jnp.concatenate([got_ref[z, i].astype(jnp.float32) for z in range(4)])
         rows = rows.astype(jnp.bfloat16)
@@ -231,8 +231,10 @@
         compiler_params=pltpu.CompilerParams(vmem_limit_bytes=SCRATCH),
     )(ids, tokens, cotangent)
     part = exchange(own, "zl")
-    part = small(widen_kernel, like(4, 2, 16, width), part, after=mates[:1])
-    block, mates[1] = lax.optimization_barrier((exchange(part, AXES, first), mates[1]))
+    part = small(widen_kernel, like(4, 2, 16, width), part)
+    block, mates[0], mates[1] = lax.optimization_barrier(
+        (exchange(part, AXES, first), mates[0], mates[1])
+    )
     other = from_other(block)
     part = experts(other, held + mates, experts(block, held + mates))
     total = jax.ShapeDtypeStruct((2, 16, width), jnp.float32)

time: 136 us -> 140 us (1.029)
  starting transfers between devices: 26.9 us -> 30.3 us
    ppermute x3, waiting for transfers between devices: 4.66 us -> 23.8 us  [from_mate(): return lax.ppermute(array, AXES, ring_pairs(lambda p: p ^ 1))]
    all_to_all x2, waiting for transfers between devices: 14.5 us -> 0.34 us  [exchange(): lax.all_to_all(blocks, axis, 0, 0, axis_index_groups=groups, tiled=True)]
    ppermute x2, waiting for transfers between devices: 8.97 us -> 4.31 us  [from_other(): return lax.ppermute(array, AXES, ring_pairs(lambda p: 3 - p))]
    ppermute x2, starting transfers between devices: 6.98 us -> 8.98 us  [from_other(): return lax.ppermute(array, AXES, ring_pairs(lambda p: 3 - p))]
    all_to_all x2, blocking collectives: 28 us -> 29.7 us  [exchange(): lax.all_to_all(blocks, axis, 0, 0, axis_index_groups=groups, tiled=True)]
where the time goes in v11:
time: 140 us; the launch traced here: 139 us
  blocking collectives  63.3 us (45%)
  starting transfers between devices  30.3 us (22%)
  waiting for transfers between devices  28.5 us (20%)
  Pallas kernels  13.4 us (10%)
  local copies, waits for them, and re-layouts  3.18 us (2%)
    all_gather x1, blocking collectives, shards(): every = lax.all_gather(mine, ('zh', 'c'), axis=0)  33.5 us
    all_to_all x2, blocking collectives, exchange(): lax.all_to_all(blocks, axis, 0, 0, axis_index_groups=groups, tiled=True)  29.7 us
    ppermute x3, waiting for transfers between devices, from_mate(): return lax.ppermute(array, AXES, ring_pairs(lambda p: p ^ 1))  23.8 us
    all_to_all x2, starting transfers between devices, exchange(): lax.all_to_all(blocks, axis, 0, 0, axis_index_groups=groups, tiled=True)  12.8 us
    pallas_call x2, Pallas kernels, experts(): pl.pallas_call(block_kernel, in_specs=[INSIDE] * (7 + len(beside)), out_s...  10.6 us
    ppermute x2, starting transfers between devices, from_other(): return lax.ppermute(array, AXES, ring_pairs(lambda p: 3 - p))  8.98 us
    ppermute x3, starting transfers between devices, from_mate(): return lax.ppermute(array, AXES, ring_pairs(lambda p: p ^ 1))  8.48 us
    ppermute x2, waiting for transfers between devices, from_other(): return lax.ppermute(array, AXES, ring_pairs(lambda p: 3 - p))  4.31 us
  transfers between devices with their start and end apart: 7, of which 6 were waited for; matrix products, arithmetic and copies ran while one was open for 0% of the time, Pallas kernels for 5%

profile of v11, /device:TPU:1, one launch (start us, length us, event | category | flops | bytes accessed | tf_op | source)
XLA Modules:
  0.0 139.3 jit_solution(18261499549945191505)
XLA Ops:
  0.6 0.0 copy-start.4
  0.6 0.9 copy-done.4
  1.5 0.0 copy-start.5
  1.5 0.9 copy-done.5
  2.4 0.0 copy-start.6
  2.4 0.7 copy-done.6
  3.1 0.3 shard_map.77
  3.4 0.0 copy-start.3
  3.4 0.7 copy-done.3
  4.1 0.0 copy-start.2
  4.1 0.0 copy-start
  4.1 0.0 copy-start.1
  4.1 6.7 %all-to-all-start = ((bf16[4,2,4,4096]{3,2,1,0:T(4,128)(2,1)}), bf16[4,2,4,4096]{3,2,1,0:T(4,128)(2,1)S(1)}, u32[]{:S(2)}, u32[]{:S(2)}) async-start(bf16[4,2,4,4096]{3,2,1,0:T(4,128)(2,1)} %copy-done.3), calls=%async_computation | async-start | bytes 524288 | tf_op jit(solution)/shard_map/all_to_all | solution.py:219
  10.8 3.1 %collective-permute-start = (bf16[4096,128]{1,0:T(8,128)(2,1)}, bf16[4096,128]{1,0:T(8,128)(2,1)}, u32[]{:S(2)}, u32[]{:S(2)}) collective-permute-start(bf16[4096,128]{1,0:T(8,128)(2,1)} %bitcast.5), channel_id=1, source_target_pairs={{0,16},{64,65},{1,17},{80,81},{2,18},{96,97},{3,19},{112,113},{16,... | collective-permute-start | bytes 3145736 | tf_op jit(solution)/shard_map/ppermute | solution.py:47
  13.9 2.2 %collective-permute-start.1 = (bf16[4096,128]{1,0:T(8,128)(2,1)}, bf16[4096,128]{1,0:T(8,128)(2,1)}, u32[]{:S(2)}, u32[]{:S(2)}) collective-permute-start(bf16[4096,128]{1,0:T(8,128)(2,1)} %bitcast.8), channel_id=1, source_target_pairs={{0,16},{64,65},{1,17},{80,81},{2,18},{96,97},{3,19},{112,113},{16,... | collective-permute-start | bytes 3145736 | tf_op jit(solution)/shard_map/ppermute | solution.py:47
  16.1 0.3 all-to-all-done.got_ref
  16.4 1.1 shard_map.78
  17.5 6.1 %all-to-all-start.1 = ((bf16[4,2,16,4096]{3,2,1,0:T(8,128)(2,1)}), bf16[4,2,16,4096]{3,2,1,0:T(8,128)(2,1)}, u32[]{:S(2)}, u32[]{:S(2)}) async-start(bf16[4,2,16,4096]{3,2,1,0:T(8,128)(2,1)} %shard_map.78), calls=%async_computation.1 | async-start | bytes 2097152 | tf_op jit(solution)/shard_map/all_to_all | solution.py:219
  23.6 0.0 copy-done.2
  23.6 3.2 %collective-permute-start.3 = (bf16[128,4096]{1,0:T(8,128)(2,1)S(1)}, bf16[128,4096]{1,0:T(8,128)(2,1)}, u32[]{:S(2)}, u32[]{:S(2)}) collective-permute-start(bf16[128,4096]{1,0:T(8,128)(2,1)S(1)} %bitcast.11), channel_id=1, source_target_pairs={{0,16},{64,65},{1,17},{80,81},{2,18},{96,97},{3,19},{112,113},{16,... | collective-permute-start | bytes 3145736 | tf_op jit(solution)/shard_map/ppermute | solution.py:47
  26.8 0.1 collective-permute-done.refs_3_
  27.0 16.9 %collective-permute-done.1.refs_4_ = bf16[4096,128]{1,0:T(8,128)(2,1)} collective-permute-done((bf16[4096,128]{1,0:T(8,128)(2,1)}, bf16[4096,128]{1,0:T(8,128)(2,1)}, u32[]{:S(2)}, u32[]{:S(2)}) %collective-permute-start.1) | collective-permute-done | bytes 1048608 | tf_op jit(solution)/shard_map/ppermute | solution.py:47
  43.8 0.0 all-to-all-done.1.rows_ref
  43.8 4.4 %collective-permute-start.2 = (bf16[4,2,16,4096]{3,2,1,0:T(8,128)(2,1)}, bf16[4,2,16,4096]{3,2,1,0:T(8,128)(2,1)S(1)}, u32[]{:S(2)}, u32[]{:S(2)}) collective-permute-start(bf16[4,2,16,4096]{3,2,1,0:T(8,128)(2,1)} %all-to-all-done.1.rows_ref), channel_id=1, source_target_pairs={{0,48},{64,67},{1,49},{80,83},{2,50},{96,99},{3,51},{112,115},{16,... | collective-permute-start | bytes 3145736 | tf_op jit(solution)/shard_map/ppermute | solution.py:51
  48.2 6.9 %collective-permute-done.3.refs_5_ = bf16[128,4096]{1,0:T(8,128)(2,1)} collective-permute-done((bf16[128,4096]{1,0:T(8,128)(2,1)S(1)}, bf16[128,4096]{1,0:T(8,128)(2,1)}, u32[]{:S(2)}, u32[]{:S(2)}) %collective-permute-start.3) | collective-permute-done | bytes 1048608 | tf_op jit(solution)/shard_map/ppermute | solution.py:47
  55.0 0.0 copy-done
  55.1 0.0 copy-done.1
  55.1 5.4 %shard_map.79.refs_6_ = bf16[4,2,16,4096]{3,2,1,0:T(8,128)(2,1)S(1)} custom-call(bf16[4,2,16,4096]{3,2,1,0:T(8,128)(2,1)} %all-to-all-done.1.rows_ref, bf16[4096,128]{1,0:T(8,128)(2,1)S(1)} %bitcast.6, bf16[4096,128]{1,0:T(8,128)(2,1)S(1)} %bitcast.9, bf16[128,4096]{1,0:T(8,128)(2,1)S(1)} %bitcast.12, bf16[4096,128]{1,0:T(8,128)(2,1)} %collective-permute-done.refs_3_, ...), custom_call_target="tpu_custom_call" | custom-call | flops 805306368 | bytes 8388608 | tf_op jit(solution)/shard_map/pallas_call | solution.py:107
  60.5 0.6 collective-permute-done.2.rows_ref
  61.1 5.2 %shard_map.80 = bf16[4,2,2,16,4096]{4,3,2,1,0:T(8,128)(2,1)S(1)} custom-call(bf16[4,2,16,4096]{3,2,1,0:T(8,128)(2,1)S(1)} %collective-permute-done.2.rows_ref, bf16[4096,128]{1,0:T(8,128)(2,1)S(1)} %bitcast.7, bf16[4096,128]{1,0:T(8,128)(2,1)S(1)} %bitcast.10, bf16[128,4096]{1,0:T(8,128)(2,1)S(1)} %bitcast.13, ...), custom_call_target="tpu_custom_call" | custom-call | flops 805306368 | bytes 8388608 | tf_op jit(solution)/shard_map/pallas_call | solution.py:107
  66.3 19.2 %all_to_all.20.got_ref = bf16[4,2,2,16,4096]{4,3,2,1,0:T(8,128)(2,1)S(1)} all-to-all(bf16[4,2,2,16,4096]{4,3,2,1,0:T(8,128)(2,1)S(1)} %shard_map.80), channel_id=1, replica_groups={{0,1,2,3},{16,17,18,19},{32,33,34,35},{48,49,50,51},{4,5,6,7},{20,21,22..., dimensions={0} | all-to-all | bytes 4194304 | tf_op jit(solution)/shard_map/all_to_all | solution.py:219
  85.5 0.0 copy-start.7
  85.5 0.2 shard_map.81
  85.8 4.6 %collective-permute-start.4 = (bf16[2,16,4096]{2,1,0:T(8,128)(2,1)S(1)}, bf16[2,16,4096]{2,1,0:T(8,128)(2,1)S(1)}, u32[]{:S(2)}, u32[]{:S(2)}) collective-permute-start(bf16[2,16,4096]{2,1,0:T(8,128)(2,1)S(1)} %get-tuple-element.11), channel_id=1, source_target_pairs={{0,48},{64,67},{1,49},{80,83},{2,50},{96,99},{3,51},{112,115},{16,... | collective-permute-start | bytes 786440 | tf_op jit(solution)/shard_map/ppermute | solution.py:51
  90.4 3.7 %collective-permute-done.4.got_ref = bf16[2,16,4096]{2,1,0:T(8,128)(2,1)S(1)} collective-permute-done((bf16[2,16,4096]{2,1,0:T(8,128)(2,1)S(1)}, bf16[2,16,4096]{2,1,0:T(8,128)(2,1)S(1)}, u32[]{:S(2)}, u32[]{:S(2)}) %collective-permute-start.4) | collective-permute-done | bytes 262176 | tf_op jit(solution)/shard_map/ppermute | solution.py:51
  94.1 0.1 shard_map.82
  94.2 10.5 %all_to_all.21.got_ref = bf16[4,2,4,4096]{3,2,1,0:T(4,128)(2,1)S(1)} all-to-all(bf16[4,2,4,4096]{3,2,1,0:T(4,128)(2,1)S(1)} %shard_map.82), channel_id=1, replica_groups=mesh['zh'=4,'c'=2,'y'=4,'zl'=4,'x'=4] {'zl'}, dimensions={0} | all-to-all | bytes 524288 | tf_op jit(solution)/shard_map/all_to_all | solution.py:219
  104.7 0.1 shard_map.83
  104.7 33.5 %all-gather = bf16[16,4,4096]{2,1,0:T(4,128)(2,1)S(1)} all-gather(bf16[2,4,4096]{2,1,0:T(4,128)(2,1)S(1)} %shard_map.83), channel_id=2, replica_groups=mesh['zh'=4,'c'=2,'y'=4,'zl'=4,'x'=4] {'zh','c'}, dimensions={0}, use_global_device_ids=true | all-gather | bytes 589824 | tf_op jit(solution)/shard_map/all_gather | solution.py:245
  138.3 0.0 copy-done.7
  138.3 1.0 shard_map.84
Async XLA Ops:
  0.6 0.9 copy-start.4
  1.5 0.9 copy-start.5
  2.4 0.7 copy-start.6
  3.4 0.7 copy-start.3
  4.1 19.5 %copy-start.2 = (bf16[1,128,4096]{2,1,0:T(8,128)(2,1)S(1)}, bf16[1,128,4096]{2,1,0:T(8,128)(2,1)}, u32[]{:S(2)}) copy-start(bf16[1,128,4096]{2,1,0:T(8,128)(2,1)} %param.11) | copy-start | bytes 3145732
  4.1 50.9 %copy-start = (bf16[1,4096,128]{2,1,0:T(8,128)(2,1)S(1)}, bf16[1,4096,128]{2,1,0:T(8,128)(2,1)}, u32[]{:S(2)}) copy-start(bf16[1,4096,128]{2,1,0:T(8,128)(2,1)} %param.9) | copy-start | bytes 3145732
  4.1 50.9 %copy-start.1 = (bf16[1,4096,128]{2,1,0:T(8,128)(2,1)S(1)}, bf16[1,4096,128]{2,1,0:T(8,128)(2,1)}, u32[]{:S(2)}) copy-start(bf16[1,4096,128]{2,1,0:T(8,128)(2,1)} %param.10) | copy-start | bytes 3145732
  4.1 12.3 %all-to-all-start = ((bf16[4,2,4,4096]{3,2,1,0:T(4,128)(2,1)}), bf16[4,2,4,4096]{3,2,1,0:T(4,128)(2,1)S(1)}, u32[]{:S(2)}, u32[]{:S(2)}) async-start(bf16[4,2,4,4096]{3,2,1,0:T(4,128)(2,1)} %copy-done.3), calls=%async_computation | async-start | bytes 524288 | tf_op jit(solution)/shard_map/all_to_all | solution.py:219
  10.8 16.1 %collective-permute-start = (bf16[4096,128]{1,0:T(8,128)(2,1)}, bf16[4096,128]{1,0:T(8,128)(2,1)}, u32[]{:S(2)}, u32[]{:S(2)}) collective-permute-start(bf16[4096,128]{1,0:T(8,128)(2,1)} %bitcast.5), channel_id=1, source_target_pairs={{0,16},{64,65},{1,17},{80,81},{2,18},{96,97},{3,19},{112,113},{16,... | collective-permute-start | bytes 3145736 | tf_op jit(solution)/shard_map/ppermute | solution.py:47
  13.9 29.9 %collective-permute-start.1 = (bf16[4096,128]{1,0:T(8,128)(2,1)}, bf16[4096,128]{1,0:T(8,128)(2,1)}, u32[]{:S(2)}, u32[]{:S(2)}) collective-permute-start(bf16[4096,128]{1,0:T(8,128)(2,1)} %bitcast.8), channel_id=1, source_target_pairs={{0,16},{64,65},{1,17},{80,81},{2,18},{96,97},{3,19},{112,113},{16,... | collective-permute-start | bytes 3145736 | tf_op jit(solution)/shard_map/ppermute | solution.py:47
  17.5 26.3 %all-to-all-start.1 = ((bf16[4,2,16,4096]{3,2,1,0:T(8,128)(2,1)}), bf16[4,2,16,4096]{3,2,1,0:T(8,128)(2,1)}, u32[]{:S(2)}, u32[]{:S(2)}) async-start(bf16[4,2,16,4096]{3,2,1,0:T(8,128)(2,1)} %shard_map.78), calls=%async_computation.1 | async-start | bytes 2097152 | tf_op jit(solution)/shard_map/all_to_all | solution.py:219
  23.6 31.4 %collective-permute-start.3 = (bf16[128,4096]{1,0:T(8,128)(2,1)S(1)}, bf16[128,4096]{1,0:T(8,128)(2,1)}, u32[]{:S(2)}, u32[]{:S(2)}) collective-permute-start(bf16[128,4096]{1,0:T(8,128)(2,1)S(1)} %bitcast.11), channel_id=1, source_target_pairs={{0,16},{64,65},{1,17},{80,81},{2,18},{96,97},{3,19},{112,113},{16,... | collective-permute-start | bytes 3145736 | tf_op jit(solution)/shard_map/ppermute | solution.py:47
  43.8 17.2 %collective-permute-start.2 = (bf16[4,2,16,4096]{3,2,1,0:T(8,128)(2,1)}, bf16[4,2,16,4096]{3,2,1,0:T(8,128)(2,1)S(1)}, u32[]{:S(2)}, u32[]{:S(2)}) collective-permute-start(bf16[4,2,16,4096]{3,2,1,0:T(8,128)(2,1)} %all-to-all-done.1.rows_ref), channel_id=1, source_target_pairs={{0,48},{64,67},{1,49},{80,83},{2,50},{96,99},{3,51},{112,115},{16,... | collective-permute-start | bytes 3145736 | tf_op jit(solution)/shard_map/ppermute | solution.py:51
  85.5 52.8 %copy-start.7 = (s32[16]{0:T(128)S(1)}, s32[16]{0:T(128)}, u32[]{:S(2)}) copy-start(s32[16]{0:T(128)} %param.8) | copy-start | bytes 196
  85.8 8.4 %collective-permute-start.4 = (bf16[2,16,4096]{2,1,0:T(8,128)(2,1)S(1)}, bf16[2,16,4096]{2,1,0:T(8,128)(2,1)S(1)}, u32[]{:S(2)}, u32[]{:S(2)}) collective-permute-start(bf16[2,16,4096]{2,1,0:T(8,128)(2,1)S(1)} %get-tuple-element.11), channel_id=1, source_target_pairs={{0,48},{64,67},{1,49},{80,83},{2,50},{96,99},{3,51},{112,115},{16,... | collective-permute-start | bytes 786440 | tf_op jit(solution)/shard_map/ppermute | solution.py:51

commit v12 on v10

--- a/solution.py
+++ b/solution.py
@@ -51,10 +51,16 @@
     return lax.ppermute(array, AXES, ring_pairs(lambda p: 3 - p))
 
 
-def block_kernel(rows_ref, *refs):
-    weights, beside, out_ref = refs[:6], refs[6:-1], refs[-1]
-    for ref in beside:
-        out_ref[:, 0] = ref[...]
+def block_kernel(fetch, rows_ref, *refs):
+    copies = []
+    if fetch:
+        given, out_ref, weights, sems = refs[:6], refs[6], refs[7:13], refs[13]
+        for i, (one, two) in enumerate(zip(given, weights)):
+            copies.append(pltpu.make_async_copy(one, two, sems.at[i]))
+            copies[i].start()
+    else:
+        weights, beside_ref, out_ref = refs[:6], refs[6], refs[7]
+        out_ref[:, 0] = beside_ref[...]
         out_ref = out_ref.at[:, 1]
     gates, ups, downs = weights[0::3], weights[1::3], weights[2::3]
     width, hidden = gates[0].shape
@@ -62,7 +68,9 @@
     deep = rows_ref.shape[0] * 16
     pieces = range(0, width, chunk)
     gates_of, ups_of, dhids_of = [], [], []
-    for wg_ref, wu_ref, wd_ref in zip(gates, ups, downs):
+    for i, (wg_ref, wu_ref, wd_ref) in enumerate(zip(gates, ups, downs)):
+        for copy in copies[3 * i : 3 * i + 3]:
+            copy.wait()
         gu = dh = None
         for k in pieces:
             tok = rows_ref[:, 0, :, k : k + chunk].reshape(deep, chunk)
@@ -101,21 +109,33 @@
         out_ref[:, 1, :, cut] = din.astype(jnp.bfloat16).reshape(-1, 16, chunk)
 
 
-def experts(block, weights, *beside):
+def experts(block, weights, beside=None):
     width, hidden = weights[0].shape
     count = block.shape[0] * 16
+    cost = pl.CostEstimate(
+        flops=24 * count * width * hidden,
+        bytes_accessed=(6 << 20) + 8 * count * width,
+        transcendentals=2 * count * hidden,
+    )
+    params = pltpu.CompilerParams(vmem_limit_bytes=24 << 20)
+    if beside is None:
+        return pl.pallas_call(
+            functools.partial(block_kernel, True),
+            in_specs=[INSIDE] + [pl.BlockSpec(memory_space=pl.ANY)] * 6,
+            out_specs=[INSIDE] * 7,
+            out_shape=[like(*block.shape)] + [like(*weight.shape) for weight in weights],
+            scratch_shapes=[pltpu.SemaphoreType.DMA((6,))],
+            compiler_params=params,
+            cost_estimate=cost,
+        )(block, *weights)
     return pl.pallas_call(
-        block_kernel,
-        in_specs=[INSIDE] * (7 + len(beside)),
+        functools.partial(block_kernel, False),
+        in_specs=[INSIDE] * 8,
         out_specs=INSIDE,
-        out_shape=like(4, *[2] * len(beside), *block.shape[1:]),
-        compiler_params=pltpu.CompilerParams(vmem_limit_bytes=24 << 20),
-        cost_estimate=pl.CostEstimate(
-            flops=24 * count * width * hidden,
-            bytes_accessed=(6 << 20) + 8 * count * width,
-            transcendentals=2 * count * hidden,
-        ),
-    )(block, *weights, *beside)
+        out_shape=like(4, 2, *block.shape[1:]),
+        compiler_params=params,
+        cost_estimate=cost,
+    )(block, *weights, beside)
 
 
 def widen_kernel(got_ref, _, out_ref):
@@ -234,7 +254,8 @@
     part = small(widen_kernel, like(4, 2, 16, width), part, after=mates[:1])
     block, mates[1] = lax.optimization_barrier((exchange(part, AXES, first), mates[1]))
     other = from_other(block)
-    part = experts(other, held + mates, experts(block, held + mates))
+    own, *weights = experts(block, held + mates)
+    part = experts(other, weights, own)
     total = jax.ShapeDtypeStruct((2, 16, width), jnp.float32)
     own, other = small(light_kernel, [total, like(2, 16, width)], exchange(part, AXES, first))
     part = small(pair_kernel, like(4, 2, SEND, width), own, from_other(other))

time: 136 us -> 133 us (0.978)
  Pallas kernels: 13.6 us -> 11.2 us
    pallas_call x2, Pallas kernels: 10.1 us -> 7.8 us  [the longest x1 4.44 us: experts(): pl.pallas_call(functools.partial(block_kernel, True), in_specs=[INSIDE] +...]
    unnamed x16 -> x14, local copies, waits for them, and re-layouts: 3.7 us -> 4.91 us
where the time goes in v12:
time: 133 us
  blocking collectives  61.3 us (46%)
  starting transfers between devices  27.4 us (21%)
  waiting for transfers between devices  27.3 us (21%)
  Pallas kernels  11.2 us (8%)
  local copies, waits for them, and re-layouts  4.91 us (4%)
    all_gather x1, blocking collectives, shards(): every = lax.all_gather(mine, ('zh', 'c'), axis=0)  33.4 us
    all_to_all x2, blocking collectives, exchange(): lax.all_to_all(blocks, axis, 0, 0, axis_index_groups=groups, tiled=True)  27.9 us
    all_to_all x2, waiting for transfers between devices, exchange(): lax.all_to_all(blocks, axis, 0, 0, axis_index_groups=groups, tiled=True)  14.7 us
    all_to_all x2, starting transfers between devices, exchange(): lax.all_to_all(blocks, axis, 0, 0, axis_index_groups=groups, tiled=True)  11.7 us
    ppermute x3, starting transfers between devices, from_mate(): return lax.ppermute(array, AXES, ring_pairs(lambda p: p ^ 1))  8.15 us
    ppermute x2, waiting for transfers between devices, from_other(): return lax.ppermute(array, AXES, ring_pairs(lambda p: 3 - p))  7.99 us
    ppermute x2, starting transfers between devices, from_other(): return lax.ppermute(array, AXES, ring_pairs(lambda p: 3 - p))  7.47 us
    unnamed x14, local copies, waits for them, and re-layouts  4.91 us
  transfers between devices with their start and end apart: 7, of which 6 were waited for; matrix products, arithmetic and copies ran while one was open for 0% of the time, Pallas kernels for 5%

profile of v12, /device:TPU:1, one launch (start us, length us, event | category | flops | bytes accessed | tf_op | source)
XLA Modules:
  0.0 132.8 jit_solution(14299395817160489497)
XLA Ops:
  0.6 4.0 %collective-permute-start = (bf16[4096,128]{1,0:T(8,128)(2,1)}, bf16[4096,128]{1,0:T(8,128)(2,1)S(1)}, u32[]{:S(2)}, u32[]{:S(2)}) collective-permute-start(bf16[4096,128]{1,0:T(8,128)(2,1)} %bitcast.6), channel_id=1, source_target_pairs={{0,16},{64,65},{1,17},{80,81},{2,18},{96,97},{3,19},{112,113},{16,... | collective-permute-start | bytes 3145736 | tf_op jit(solution)/shard_map/ppermute | solution.py:47
  4.6 0.0 copy-start.3
  4.6 0.9 copy-done.3
  5.5 0.0 copy-start.4
  5.5 0.9 copy-done.4
  6.4 0.0 copy-start.5
  6.4 0.7 copy-done.5
  7.1 1.0 shard_map.77
  8.1 5.6 %all-to-all-start = ((bf16[4,2,4,4096]{3,2,1,0:T(4,128)(2,1)}), bf16[4,2,4,4096]{3,2,1,0:T(4,128)(2,1)S(1)}, u32[]{:S(2)}, u32[]{:S(2)}) async-start(bf16[4,2,4,4096]{3,2,1,0:T(4,128)(2,1)} %shard_map.77), calls=%async_computation | async-start | bytes 524288 | tf_op jit(solution)/shard_map/all_to_all | solution.py:239
  13.7 0.0 copy-start
  13.7 2.3 %collective-permute-start.1 = (bf16[4096,128]{1,0:T(8,128)(2,1)}, bf16[4096,128]{1,0:T(8,128)(2,1)}, u32[]{:S(2)}, u32[]{:S(2)}) collective-permute-start(bf16[4096,128]{1,0:T(8,128)(2,1)} %bitcast.8), channel_id=1, source_target_pairs={{0,16},{64,65},{1,17},{80,81},{2,18},{96,97},{3,19},{112,113},{16,... | collective-permute-start | bytes 3145736 | tf_op jit(solution)/shard_map/ppermute | solution.py:47
  16.0 3.3 %all-to-all-done.got_ref = bf16[4,2,4,4096]{3,2,1,0:T(4,128)(2,1)S(1)} async-done(((bf16[4,2,4,4096]{3,2,1,0:T(4,128)(2,1)}), bf16[4,2,4,4096]{3,2,1,0:T(4,128)(2,1)S(1)}, u32[]{:S(2)}, u32[]{:S(2)}) %all-to-all-start) | async-done | bytes 262176 | tf_op jit(solution)/shard_map/all_to_all | solution.py:239
  19.3 0.0 collective-permute-done._.refs_3_
  19.3 1.0 shard_map.78
  20.3 6.1 %all-to-all-start.1 = ((bf16[4,2,16,4096]{3,2,1,0:T(8,128)(2,1)}), bf16[4,2,16,4096]{3,2,1,0:T(8,128)(2,1)S(1)}, u32[]{:S(2)}, u32[]{:S(2)}) async-start(bf16[4,2,16,4096]{3,2,1,0:T(8,128)(2,1)} %shard_map.78), calls=%async_computation.1 | async-start | bytes 2097152 | tf_op jit(solution)/shard_map/all_to_all | solution.py:239
  26.5 1.9 %collective-permute-start.3 = (bf16[128,4096]{1,0:T(8,128)(2,1)}, bf16[128,4096]{1,0:T(8,128)(2,1)}, u32[]{:S(2)}, u32[]{:S(2)}) collective-permute-start(bf16[128,4096]{1,0:T(8,128)(2,1)} %bitcast.10), channel_id=1, source_target_pairs={{0,16},{64,65},{1,17},{80,81},{2,18},{96,97},{3,19},{112,113},{16,... | collective-permute-start | bytes 3145736 | tf_op jit(solution)/shard_map/ppermute | solution.py:47
  28.4 1.6 %collective-permute-done.1.refs_4_ = bf16[4096,128]{1,0:T(8,128)(2,1)} collective-permute-done((bf16[4096,128]{1,0:T(8,128)(2,1)}, bf16[4096,128]{1,0:T(8,128)(2,1)}, u32[]{:S(2)}, u32[]{:S(2)}) %collective-permute-start.1) | collective-permute-done | bytes 1048608 | tf_op jit(solution)/shard_map/ppermute | solution.py:47
  30.0 11.4 %all-to-all-done.1.rows_ref = bf16[4,2,16,4096]{3,2,1,0:T(8,128)(2,1)S(1)} async-done(((bf16[4,2,16,4096]{3,2,1,0:T(8,128)(2,1)}), bf16[4,2,16,4096]{3,2,1,0:T(8,128)(2,1)S(1)}, u32[]{:S(2)}, u32[]{:S(2)}) %all-to-all-start.1) | async-done | bytes 1048608 | tf_op jit(solution)/shard_map/all_to_all | solution.py:239
  41.4 3.9 %collective-permute-start.2 = (bf16[4,2,16,4096]{3,2,1,0:T(8,128)(2,1)S(1)}, bf16[4,2,16,4096]{3,2,1,0:T(8,128)(2,1)S(1)}, u32[]{:S(2)}, u32[]{:S(2)}) collective-permute-start(bf16[4,2,16,4096]{3,2,1,0:T(8,128)(2,1)S(1)} %all-to-all-done.1.rows_ref), channel_id=1, source_target_pairs={{0,48},{64,67},{1,49},{80,83},{2,50},{96,99},{3,51},{112,115},{16,... | collective-permute-start | bytes 3145736 | tf_op jit(solution)/shard_map/ppermute | solution.py:51
  45.3 3.0 %collective-permute-done.3.refs_5_ = bf16[128,4096]{1,0:T(8,128)(2,1)} collective-permute-done((bf16[128,4096]{1,0:T(8,128)(2,1)}, bf16[128,4096]{1,0:T(8,128)(2,1)}, u32[]{:S(2)}, u32[]{:S(2)}) %collective-permute-start.3) | collective-permute-done | bytes 1048608 | tf_op jit(solution)/shard_map/ppermute | solution.py:47
  48.2 0.0 copy-done
  48.2 0.0 copy-start.1
  48.2 1.2 copy-done.1
  49.5 0.0 copy-start.2
  49.5 1.2 copy-done.2
  50.7 4.4 %shard_map.79 = (bf16[4,2,16,4096]{3,2,1,0:T(8,128)(2,1)S(1)}, bf16[4096,128]{1,0:T(8,128)(2,1)S(1)}, bf16[4096,128]{1,0:T(8,128)(2,1)S(1)}, bf16[128,4096]{1,0:...) custom-call(bf16[4,2,16,4096]{3,2,1,0:T(8,128)(2,1)S(1)} %all-to-all-, ...), custom_call_target="tpu_custom_call" | custom-call | flops 805306368 | bytes 8388608 | tf_op jit(solution)/shard_map/pallas_call | solution.py:122
  55.1 3.2 %collective-permute-done.2.rows_ref = bf16[4,2,16,4096]{3,2,1,0:T(8,128)(2,1)S(1)} collective-permute-done((bf16[4,2,16,4096]{3,2,1,0:T(8,128)(2,1)S(1)}, bf16[4,2,16,4096]{3,2,1,0:T(8,128)(2,1)S(1)}, u32[]{:S(2)}, u32[]{:S(2)}) %collective-permute-start.2) | collective-permute-done | bytes 1048608 | tf_op jit(solution)/shard_map/ppermute | solution.py:51
  58.4 3.4 %shard_map.80 = bf16[4,2,2,16,4096]{4,3,2,1,0:T(8,128)(2,1)S(1)} custom-call(bf16[4,2,16,4096]{3,2,1,0:T(8,128)(2,1)S(1)} %collective-permute-done.2.rows_ref, bf16[4096,128]{1,0:T(8,128)(2,1)S(1)} %get-tuple-element.15.refs_0_, bf16[4096,128]{1,0:T(8,128)(2,1)S(1)} %get-tuple-element.16.refs_1_, bf16[128,4096]{1,0:T(8,128)(2,1)S(1)} %get-tuple-element.17.refs_2_, ...), custom_call_target="tpu_custom_call" | custom-call | flops 805306368 | bytes 8388608 | tf_op jit(solution)/shard_map/pallas_call | solution.py:131
  61.8 18.5 %all_to_all.20.got_ref = bf16[4,2,2,16,4096]{4,3,2,1,0:T(8,128)(2,1)S(1)} all-to-all(bf16[4,2,2,16,4096]{4,3,2,1,0:T(8,128)(2,1)S(1)} %shard_map.80), channel_id=1, replica_groups={{0,1,2,3},{16,17,18,19},{32,33,34,35},{48,49,50,51},{4,5,6,7},{20,21,22..., dimensions={0} | all-to-all | bytes 4194304 | tf_op jit(solution)/shard_map/all_to_all | solution.py:239
  80.2 0.0 copy-start.6
  80.2 0.2 shard_map.81
  80.5 3.6 %collective-permute-start.4 = (bf16[2,16,4096]{2,1,0:T(8,128)(2,1)S(1)}, bf16[2,16,4096]{2,1,0:T(8,128)(2,1)S(1)}, u32[]{:S(2)}, u32[]{:S(2)}) collective-permute-start(bf16[2,16,4096]{2,1,0:T(8,128)(2,1)S(1)} %get-tuple-element.23), channel_id=1, source_target_pairs={{0,48},{64,67},{1,49},{80,83},{2,50},{96,99},{3,51},{112,115},{16,... | collective-permute-start | bytes 786440 | tf_op jit(solution)/shard_map/ppermute | solution.py:51
  84.0 4.7 %collective-permute-done.4.got_ref = bf16[2,16,4096]{2,1,0:T(8,128)(2,1)S(1)} collective-permute-done((bf16[2,16,4096]{2,1,0:T(8,128)(2,1)S(1)}, bf16[2,16,4096]{2,1,0:T(8,128)(2,1)S(1)}, u32[]{:S(2)}, u32[]{:S(2)}) %collective-permute-start.4) | collective-permute-done | bytes 262176 | tf_op jit(solution)/shard_map/ppermute | solution.py:51
  88.8 0.1 shard_map.82
  88.9 9.5 %all_to_all.21.got_ref = bf16[4,2,4,4096]{3,2,1,0:T(4,128)(2,1)S(1)} all-to-all(bf16[4,2,4,4096]{3,2,1,0:T(4,128)(2,1)S(1)} %shard_map.82), channel_id=1, replica_groups=mesh['zh'=4,'c'=2,'y'=4,'zl'=4,'x'=4] {'zl'}, dimensions={0} | all-to-all | bytes 524288 | tf_op jit(solution)/shard_map/all_to_all | solution.py:239
  98.3 0.1 shard_map.83
  98.4 33.4 %all-gather = bf16[16,4,4096]{2,1,0:T(4,128)(2,1)S(1)} all-gather(bf16[2,4,4096]{2,1,0:T(4,128)(2,1)S(1)} %shard_map.83), channel_id=2, replica_groups=mesh['zh'=4,'c'=2,'y'=4,'zl'=4,'x'=4] {'zh','c'}, dimensions={0}, use_global_device_ids=true | all-gather | bytes 589824 | tf_op jit(solution)/shard_map/all_gather | solution.py:264
  131.8 0.0 copy-done.6
  131.8 1.0 shard_map.84
Async XLA Ops:
  0.6 18.7 %collective-permute-start = (bf16[4096,128]{1,0:T(8,128)(2,1)}, bf16[4096,128]{1,0:T(8,128)(2,1)S(1)}, u32[]{:S(2)}, u32[]{:S(2)}) collective-permute-start(bf16[4096,128]{1,0:T(8,128)(2,1)} %bitcast.6), channel_id=1, source_target_pairs={{0,16},{64,65},{1,17},{80,81},{2,18},{96,97},{3,19},{112,113},{16,... | collective-permute-start | bytes 3145736 | tf_op jit(solution)/shard_map/ppermute | solution.py:47
  4.6 0.9 copy-start.3
  5.5 0.9 copy-start.4
  6.4 0.7 copy-start.5
  8.1 11.2 %all-to-all-start = ((bf16[4,2,4,4096]{3,2,1,0:T(4,128)(2,1)}), bf16[4,2,4,4096]{3,2,1,0:T(4,128)(2,1)S(1)}, u32[]{:S(2)}, u32[]{:S(2)}) async-start(bf16[4,2,4,4096]{3,2,1,0:T(4,128)(2,1)} %shard_map.77), calls=%async_computation | async-start | bytes 524288 | tf_op jit(solution)/shard_map/all_to_all | solution.py:239
  13.7 34.6 %copy-start = (bf16[1,4096,128]{2,1,0:T(8,128)(2,1)S(1)}, bf16[1,4096,128]{2,1,0:T(8,128)(2,1)}, u32[]{:S(2)}) copy-start(bf16[1,4096,128]{2,1,0:T(8,128)(2,1)} %param.9) | copy-start | bytes 3145732
  13.7 16.3 %collective-permute-start.1 = (bf16[4096,128]{1,0:T(8,128)(2,1)}, bf16[4096,128]{1,0:T(8,128)(2,1)}, u32[]{:S(2)}, u32[]{:S(2)}) collective-permute-start(bf16[4096,128]{1,0:T(8,128)(2,1)} %bitcast.8), channel_id=1, source_target_pairs={{0,16},{64,65},{1,17},{80,81},{2,18},{96,97},{3,19},{112,113},{16,... | collective-permute-start | bytes 3145736 | tf_op jit(solution)/shard_map/ppermute | solution.py:47
  20.3 21.0 %all-to-all-start.1 = ((bf16[4,2,16,4096]{3,2,1,0:T(8,128)(2,1)}), bf16[4,2,16,4096]{3,2,1,0:T(8,128)(2,1)S(1)}, u32[]{:S(2)}, u32[]{:S(2)}) async-start(bf16[4,2,16,4096]{3,2,1,0:T(8,128)(2,1)} %shard_map.78), calls=%async_computation.1 | async-start | bytes 2097152 | tf_op jit(solution)/shard_map/all_to_all | solution.py:239
  26.5 21.8 %collective-permute-start.3 = (bf16[128,4096]{1,0:T(8,128)(2,1)}, bf16[128,4096]{1,0:T(8,128)(2,1)}, u32[]{:S(2)}, u32[]{:S(2)}) collective-permute-start(bf16[128,4096]{1,0:T(8,128)(2,1)} %bitcast.10), channel_id=1, source_target_pairs={{0,16},{64,65},{1,17},{80,81},{2,18},{96,97},{3,19},{112,113},{16,... | collective-permute-start | bytes 3145736 | tf_op jit(solution)/shard_map/ppermute | solution.py:47
  41.4 17.0 %collective-permute-start.2 = (bf16[4,2,16,4096]{3,2,1,0:T(8,128)(2,1)S(1)}, bf16[4,2,16,4096]{3,2,1,0:T(8,128)(2,1)S(1)}, u32[]{:S(2)}, u32[]{:S(2)}) collective-permute-start(bf16[4,2,16,4096]{3,2,1,0:T(8,128)(2,1)S(1)} %all-to-all-done.1.rows_ref), channel_id=1, source_target_pairs={{0,48},{64,67},{1,49},{80,83},{2,50},{96,99},{3,51},{112,115},{16,... | collective-permute-start | bytes 3145736 | tf_op jit(solution)/shard_map/ppermute | solution.py:51
  48.2 1.2 copy-start.1
  49.5 1.2 copy-start.2
  80.2 51.6 %copy-start.6 = (s32[16]{0:T(128)S(1)}, s32[16]{0:T(128)}, u32[]{:S(2)}) copy-start(s32[16]{0:T(128)} %param.8) | copy-start | bytes 196
  80.5 8.3 %collective-permute-start.4 = (bf16[2,16,4096]{2,1,0:T(8,128)(2,1)S(1)}, bf16[2,16,4096]{2,1,0:T(8,128)(2,1)S(1)}, u32[]{:S(2)}, u32[]{:S(2)}) collective-permute-start(bf16[2,16,4096]{2,1,0:T(8,128)(2,1)S(1)} %get-tuple-element.23), channel_id=1, source_target_pairs={{0,48},{64,67},{1,49},{80,83},{2,50},{96,99},{3,51},{112,115},{16,... | collective-permute-start | bytes 786440 | tf_op jit(solution)/shard_map/ppermute | solution.py:51

commit v13 on v12

--- a/solution.py
+++ b/solution.py
@@ -233,7 +233,9 @@
     ids = expert_id.reshape(1, count)
     first = mixed_groups("x")
     held = [gate_weight[0], up_weight[0], down_weight[0]]
-    mates = [from_mate(weight) for weight in held]
+    mates = [from_mate(weight) for weight in held[:2]]
+    mates[1], down = lax.optimization_barrier((mates[1], held[2]))
+    mates.append(from_mate(down))
 
     def exchange(blocks, axis, groups=None):
         return lax.all_to_all(blocks, axis, 0, 0, axis_index_groups=groups, tiled=True)

time: 133 us -> 134 us (level)
  blocking collectives: 61.3 us -> 63.2 us
    ppermute x3, waiting for transfers between devices: 4.54 us -> 9.5 us  [from_mate(): return lax.ppermute(array, AXES, ring_pairs(lambda p: p ^ 1))]
    all_to_all x2, waiting for transfers between devices: 14.7 us -> 10.1 us  [exchange(): lax.all_to_all(blocks, axis, 0, 0, axis_index_groups=groups, tiled=True)]
  transfers between devices with their start and end apart: 7 -> 7, of which waited for: 6 -> 5; matrix products, arithmetic and copies ran while one was open for 0% -> 0% of each run, Pallas kernels for 5% -> 5%
where the time goes in v13:
time: 134 us; the launch traced here: 133 us
  blocking collectives  63.2 us (47%)
  starting transfers between devices  26.6 us (20%)
  waiting for transfers between devices  26.5 us (20%)
  Pallas kernels  11.2 us (8%)
  local copies, waits for them, and re-layouts  4.91 us (4%)
    all_gather x1, blocking collectives, shards(): every = lax.all_gather(mine, ('zh', 'c'), axis=0)  34.1 us
    all_to_all x2, blocking collectives, exchange(): lax.all_to_all(blocks, axis, 0, 0, axis_index_groups=groups, tiled=True)  29 us
    all_to_all x2, starting transfers between devices, exchange(): lax.all_to_all(blocks, axis, 0, 0, axis_index_groups=groups, tiled=True)  11.7 us
    all_to_all x2, waiting for transfers between devices, exchange(): lax.all_to_all(blocks, axis, 0, 0, axis_index_groups=groups, tiled=True)  10.1 us
    ppermute x3, waiting for transfers between devices, from_mate(): return lax.ppermute(array, AXES, ring_pairs(lambda p: p ^ 1))  9.5 us
    ppermute x3, starting transfers between devices, from_mate(): return lax.ppermute(array, AXES, ring_pairs(lambda p: p ^ 1))  8.4 us
    ppermute x2, waiting for transfers between devices, from_other(): return lax.ppermute(array, AXES, ring_pairs(lambda p: 3 - p))  6.89 us
    ppermute x2, starting transfers between devices, from_other(): return lax.ppermute(array, AXES, ring_pairs(lambda p: 3 - p))  6.47 us
  transfers between devices with their start and end apart: 7, of which 5 were waited for; matrix products, arithmetic and copies ran while one was open for 0% of the time, Pallas kernels for 5%

profile of v13, /device:TPU:1, one launch (start us, length us, event | category | flops | bytes accessed | tf_op | source)
XLA Modules:
  0.0 133.1 jit_solution(1989624396400709977)
XLA Ops:
  0.6 4.0 %collective-permute-start = (bf16[4096,128]{1,0:T(8,128)(2,1)}, bf16[4096,128]{1,0:T(8,128)(2,1)S(1)}, u32[]{:S(2)}, u32[]{:S(2)}) collective-permute-start(bf16[4096,128]{1,0:T(8,128)(2,1)} %bitcast.6), channel_id=1, source_target_pairs={{0,16},{64,65},{1,17},{80,81},{2,18},{96,97},{3,19},{112,113},{16,... | collective-permute-start | bytes 3145736 | tf_op jit(solution)/shard_map/ppermute | solution.py:47
  4.6 0.0 copy-start.3
  4.6 0.9 copy-done.3
  5.5 0.0 copy-start.4
  5.5 0.9 copy-done.4
  6.4 0.0 copy-start.5
  6.4 0.7 copy-done.5
  7.1 1.0 shard_map.77
  8.1 5.6 %all-to-all-start = ((bf16[4,2,4,4096]{3,2,1,0:T(4,128)(2,1)}), bf16[4,2,4,4096]{3,2,1,0:T(4,128)(2,1)S(1)}, u32[]{:S(2)}, u32[]{:S(2)}) async-start(bf16[4,2,4,4096]{3,2,1,0:T(4,128)(2,1)} %shard_map.77), calls=%async_computation | async-start | bytes 524288 | tf_op jit(solution)/shard_map/all_to_all | solution.py:241
  13.7 0.0 copy-start
  13.7 2.3 %collective-permute-start.1 = (bf16[4096,128]{1,0:T(8,128)(2,1)}, bf16[4096,128]{1,0:T(8,128)(2,1)}, u32[]{:S(2)}, u32[]{:S(2)}) collective-permute-start(bf16[4096,128]{1,0:T(8,128)(2,1)} %bitcast.8), channel_id=1, source_target_pairs={{0,16},{64,65},{1,17},{80,81},{2,18},{96,97},{3,19},{112,113},{16,... | collective-permute-start | bytes 3145736 | tf_op jit(solution)/shard_map/ppermute | solution.py:47
  16.0 3.3 %all-to-all-done.got_ref = bf16[4,2,4,4096]{3,2,1,0:T(4,128)(2,1)S(1)} async-done(((bf16[4,2,4,4096]{3,2,1,0:T(4,128)(2,1)}), bf16[4,2,4,4096]{3,2,1,0:T(4,128)(2,1)S(1)}, u32[]{:S(2)}, u32[]{:S(2)}) %all-to-all-start) | async-done | bytes 262176 | tf_op jit(solution)/shard_map/all_to_all | solution.py:241
  19.3 0.0 collective-permute-done._.refs_3_
  19.3 1.0 shard_map.78
  20.3 6.1 %all-to-all-start.1 = ((bf16[4,2,16,4096]{3,2,1,0:T(8,128)(2,1)}), bf16[4,2,16,4096]{3,2,1,0:T(8,128)(2,1)S(1)}, u32[]{:S(2)}, u32[]{:S(2)}) async-start(bf16[4,2,16,4096]{3,2,1,0:T(8,128)(2,1)} %shard_map.78), calls=%async_computation.1 | async-start | bytes 2097152 | tf_op jit(solution)/shard_map/all_to_all | solution.py:241
  26.5 3.5 %collective-permute-done.1.refs_4_ = bf16[4096,128]{1,0:T(8,128)(2,1)} collective-permute-done((bf16[4096,128]{1,0:T(8,128)(2,1)}, bf16[4096,128]{1,0:T(8,128)(2,1)}, u32[]{:S(2)}, u32[]{:S(2)}) %collective-permute-start.1) | collective-permute-done | bytes 1048608 | tf_op jit(solution)/shard_map/ppermute | solution.py:47
  30.0 2.2 %collective-permute-start.3 = (bf16[128,4096]{1,0:T(8,128)(2,1)}, bf16[128,4096]{1,0:T(8,128)(2,1)}, u32[]{:S(2)}, u32[]{:S(2)}) collective-permute-start(bf16[128,4096]{1,0:T(8,128)(2,1)} %bitcast.10), channel_id=1, source_target_pairs={{0,16},{64,65},{1,17},{80,81},{2,18},{96,97},{3,19},{112,113},{16,... | collective-permute-start | bytes 3145736 | tf_op jit(solution)/shard_map/ppermute | solution.py:47
  32.1 6.7 %all-to-all-done.1.rows_ref = bf16[4,2,16,4096]{3,2,1,0:T(8,128)(2,1)S(1)} async-done(((bf16[4,2,16,4096]{3,2,1,0:T(8,128)(2,1)}), bf16[4,2,16,4096]{3,2,1,0:T(8,128)(2,1)S(1)}, u32[]{:S(2)}, u32[]{:S(2)}) %all-to-all-start.1) | async-done | bytes 1048608 | tf_op jit(solution)/shard_map/all_to_all | solution.py:241
  38.9 4.4 %collective-permute-start.2 = (bf16[4,2,16,4096]{3,2,1,0:T(8,128)(2,1)S(1)}, bf16[4,2,16,4096]{3,2,1,0:T(8,128)(2,1)S(1)}, u32[]{:S(2)}, u32[]{:S(2)}) collective-permute-start(bf16[4,2,16,4096]{3,2,1,0:T(8,128)(2,1)S(1)} %all-to-all-done.1.rows_ref), channel_id=1, source_target_pairs={{0,48},{64,67},{1,49},{80,83},{2,50},{96,99},{3,51},{112,115},{16,... | collective-permute-start | bytes 3145736 | tf_op jit(solution)/shard_map/ppermute | solution.py:51
  43.2 6.0 %collective-permute-done.3.refs_5_ = bf16[128,4096]{1,0:T(8,128)(2,1)} collective-permute-done((bf16[128,4096]{1,0:T(8,128)(2,1)}, bf16[128,4096]{1,0:T(8,128)(2,1)}, u32[]{:S(2)}, u32[]{:S(2)}) %collective-permute-start.3) | collective-permute-done | bytes 1048608 | tf_op jit(solution)/shard_map/ppermute | solution.py:47
  49.3 0.0 copy-done
  49.3 0.0 copy-start.1
  49.3 1.2 copy-done.1
  50.5 0.0 copy-start.2
  50.5 1.2 copy-done.2
  51.7 4.4 %shard_map.79 = (bf16[4,2,16,4096]{3,2,1,0:T(8,128)(2,1)S(1)}, bf16[4096,128]{1,0:T(8,128)(2,1)S(1)}, bf16[4096,128]{1,0:T(8,128)(2,1)S(1)}, bf16[128,4096]{1,0:...) custom-call(bf16[4,2,16,4096]{3,2,1,0:T(8,128)(2,1)S(1)} %all-to-all-, ...), custom_call_target="tpu_custom_call" | custom-call | flops 805306368 | bytes 8388608 | tf_op jit(solution)/shard_map/pallas_call | solution.py:122
  56.2 0.0 collective-permute-done.2.rows_ref
  56.2 3.4 %shard_map.80 = bf16[4,2,2,16,4096]{4,3,2,1,0:T(8,128)(2,1)S(1)} custom-call(bf16[4,2,16,4096]{3,2,1,0:T(8,128)(2,1)S(1)} %collective-permute-done.2.rows_ref, bf16[4096,128]{1,0:T(8,128)(2,1)S(1)} %get-tuple-element.19.refs_0_, bf16[4096,128]{1,0:T(8,128)(2,1)S(1)} %get-tuple-element.20.refs_1_, bf16[128,4096]{1,0:T(8,128)(2,1)S(1)} %get-tuple-element.21.refs_2_, ...), custom_call_target="tpu_custom_call" | custom-call | flops 805306368 | bytes 8388608 | tf_op jit(solution)/shard_map/pallas_call | solution.py:131
  59.5 20.7 %all_to_all.20.got_ref = bf16[4,2,2,16,4096]{4,3,2,1,0:T(8,128)(2,1)S(1)} all-to-all(bf16[4,2,2,16,4096]{4,3,2,1,0:T(8,128)(2,1)S(1)} %shard_map.80), channel_id=1, replica_groups={{0,1,2,3},{16,17,18,19},{32,33,34,35},{48,49,50,51},{4,5,6,7},{20,21,22..., dimensions={0} | all-to-all | bytes 4194304 | tf_op jit(solution)/shard_map/all_to_all | solution.py:241
  80.2 0.0 copy-start.6
  80.2 0.2 shard_map.81
  80.5 2.1 %collective-permute-start.4 = (bf16[2,16,4096]{2,1,0:T(8,128)(2,1)S(1)}, bf16[2,16,4096]{2,1,0:T(8,128)(2,1)S(1)}, u32[]{:S(2)}, u32[]{:S(2)}) collective-permute-start(bf16[2,16,4096]{2,1,0:T(8,128)(2,1)S(1)} %get-tuple-element.27), channel_id=1, source_target_pairs={{0,48},{64,67},{1,49},{80,83},{2,50},{96,99},{3,51},{112,115},{16,... | collective-permute-start | bytes 786440 | tf_op jit(solution)/shard_map/ppermute | solution.py:51
  82.6 6.9 %collective-permute-done.4.got_ref = bf16[2,16,4096]{2,1,0:T(8,128)(2,1)S(1)} collective-permute-done((bf16[2,16,4096]{2,1,0:T(8,128)(2,1)S(1)}, bf16[2,16,4096]{2,1,0:T(8,128)(2,1)S(1)}, u32[]{:S(2)}, u32[]{:S(2)}) %collective-permute-start.4) | collective-permute-done | bytes 262176 | tf_op jit(solution)/shard_map/ppermute | solution.py:51
  89.5 0.1 shard_map.82
  89.5 8.4 %all_to_all.21.got_ref = bf16[4,2,4,4096]{3,2,1,0:T(4,128)(2,1)S(1)} all-to-all(bf16[4,2,4,4096]{3,2,1,0:T(4,128)(2,1)S(1)} %shard_map.82), channel_id=1, replica_groups=mesh['zh'=4,'c'=2,'y'=4,'zl'=4,'x'=4] {'zl'}, dimensions={0} | all-to-all | bytes 524288 | tf_op jit(solution)/shard_map/all_to_all | solution.py:241
  97.9 0.1 shard_map.83
  97.9 34.1 %all-gather = bf16[16,4,4096]{2,1,0:T(4,128)(2,1)S(1)} all-gather(bf16[2,4,4096]{2,1,0:T(4,128)(2,1)S(1)} %shard_map.83), channel_id=2, replica_groups=mesh['zh'=4,'c'=2,'y'=4,'zl'=4,'x'=4] {'zh','c'}, dimensions={0}, use_global_device_ids=true | all-gather | bytes 589824 | tf_op jit(solution)/shard_map/all_gather | solution.py:266
  132.1 0.0 copy-done.6
  132.1 1.0 shard_map.84
Async XLA Ops:
  0.6 18.7 %collective-permute-start = (bf16[4096,128]{1,0:T(8,128)(2,1)}, bf16[4096,128]{1,0:T(8,128)(2,1)S(1)}, u32[]{:S(2)}, u32[]{:S(2)}) collective-permute-start(bf16[4096,128]{1,0:T(8,128)(2,1)} %bitcast.6), channel_id=1, source_target_pairs={{0,16},{64,65},{1,17},{80,81},{2,18},{96,97},{3,19},{112,113},{16,... | collective-permute-start | bytes 3145736 | tf_op jit(solution)/shard_map/ppermute | solution.py:47
  4.6 0.9 copy-start.3
  5.5 0.9 copy-start.4
  6.4 0.7 copy-start.5
  8.1 11.2 %all-to-all-start = ((bf16[4,2,4,4096]{3,2,1,0:T(4,128)(2,1)}), bf16[4,2,4,4096]{3,2,1,0:T(4,128)(2,1)S(1)}, u32[]{:S(2)}, u32[]{:S(2)}) async-start(bf16[4,2,4,4096]{3,2,1,0:T(4,128)(2,1)} %shard_map.77), calls=%async_computation | async-start | bytes 524288 | tf_op jit(solution)/shard_map/all_to_all | solution.py:241
  13.7 35.6 %copy-start = (bf16[1,4096,128]{2,1,0:T(8,128)(2,1)S(1)}, bf16[1,4096,128]{2,1,0:T(8,128)(2,1)}, u32[]{:S(2)}) copy-start(bf16[1,4096,128]{2,1,0:T(8,128)(2,1)} %param.9) | copy-start | bytes 3145732
  13.7 16.3 %collective-permute-start.1 = (bf16[4096,128]{1,0:T(8,128)(2,1)}, bf16[4096,128]{1,0:T(8,128)(2,1)}, u32[]{:S(2)}, u32[]{:S(2)}) collective-permute-start(bf16[4096,128]{1,0:T(8,128)(2,1)} %bitcast.8), channel_id=1, source_target_pairs={{0,16},{64,65},{1,17},{80,81},{2,18},{96,97},{3,19},{112,113},{16,... | collective-permute-start | bytes 3145736 | tf_op jit(solution)/shard_map/ppermute | solution.py:47
  20.3 18.5 %all-to-all-start.1 = ((bf16[4,2,16,4096]{3,2,1,0:T(8,128)(2,1)}), bf16[4,2,16,4096]{3,2,1,0:T(8,128)(2,1)S(1)}, u32[]{:S(2)}, u32[]{:S(2)}) async-start(bf16[4,2,16,4096]{3,2,1,0:T(8,128)(2,1)} %shard_map.78), calls=%async_computation.1 | async-start | bytes 2097152 | tf_op jit(solution)/shard_map/all_to_all | solution.py:241
  30.0 19.3 %collective-permute-start.3 = (bf16[128,4096]{1,0:T(8,128)(2,1)}, bf16[128,4096]{1,0:T(8,128)(2,1)}, u32[]{:S(2)}, u32[]{:S(2)}) collective-permute-start(bf16[128,4096]{1,0:T(8,128)(2,1)} %bitcast.10), channel_id=1, source_target_pairs={{0,16},{64,65},{1,17},{80,81},{2,18},{96,97},{3,19},{112,113},{16,... | collective-permute-start | bytes 3145736 | tf_op jit(solution)/shard_map/ppermute | solution.py:47
  38.9 17.3 %collective-permute-start.2 = (bf16[4,2,16,4096]{3,2,1,0:T(8,128)(2,1)S(1)}, bf16[4,2,16,4096]{3,2,1,0:T(8,128)(2,1)S(1)}, u32[]{:S(2)}, u32[]{:S(2)}) collective-permute-start(bf16[4,2,16,4096]{3,2,1,0:T(8,128)(2,1)S(1)} %all-to-all-done.1.rows_ref), channel_id=1, source_target_pairs={{0,48},{64,67},{1,49},{80,83},{2,50},{96,99},{3,51},{112,115},{16,... | collective-permute-start | bytes 3145736 | tf_op jit(solution)/shard_map/ppermute | solution.py:51
  49.3 1.2 copy-start.1
  50.5 1.2 copy-start.2
  80.2 51.9 %copy-start.6 = (s32[16]{0:T(128)S(1)}, s32[16]{0:T(128)}, u32[]{:S(2)}) copy-start(s32[16]{0:T(128)} %param.8) | copy-start | bytes 196
  80.5 9.0 %collective-permute-start.4 = (bf16[2,16,4096]{2,1,0:T(8,128)(2,1)S(1)}, bf16[2,16,4096]{2,1,0:T(8,128)(2,1)S(1)}, u32[]{:S(2)}, u32[]{:S(2)}) collective-permute-start(bf16[2,16,4096]{2,1,0:T(8,128)(2,1)S(1)} %get-tuple-element.27), channel_id=1, source_target_pairs={{0,48},{64,67},{1,49},{80,83},{2,50},{96,99},{3,51},{112,115},{16,... | collective-permute-start | bytes 786440 | tf_op jit(solution)/shard_map/ppermute | solution.py:51
